TPU v7x, 128 devices: a whole 4x4x4 slice. The times are simulated.
128 devices in a mesh: rows: 16 (over y, x), cols: 8 (over z, core).
Axes of the slice: x: 4, y: 4, z: 4, core: 2. Of those that a mesh axis runs over, the one named last changes fastest.
Arguments:
- slab: bfloat16 [4096, 262144], P('rows', 'cols')
- sign_bits: int32 [262144], P('cols'), may hold values from 0 to 1
- sampled: int32 [512], replicated, may hold values from 0 to 262143
Outputs:
- projected: float32 [512, 262144], P('rows', 'cols')
All inputs are finite; a program needn't handle non-finite values.
Results may differ from a plain program's by a relative error of at most 0.0029.
Values may be sent and summed in bfloat16 or wider, within the bound.
No kernel may reach another device: no remote copies, remote signals or barrier semaphores. Data moves between devices by JAX's collectives and lax.ppermute only.
A program may use at most 256 MiB of HBM per device.

v0:
```python
import math

import jax
import jax.numpy as jnp
from jax import lax
from jax.sharding import PartitionSpec as P

N = 262144


epsilon = 1e-06


def parity_bits(values, width):
    result = jnp.zeros_like(values)
    for shift_by in range(width):
        result = jnp.bitwise_xor(result, jnp.bitwise_and(jnp.right_shift(values, shift_by), 1))
    return result


def sign_table(indices, sampled):
    masked = jnp.bitwise_and(indices[:, None], sampled[None, :])
    parity = parity_bits(masked, N.bit_length())
    return (1 - 2 * parity).astype(jnp.bfloat16)


def per_device(slab, sign_bits, sampled):
    local_cols = slab.shape[1]
    total_rows = slab.shape[0] * lax.axis_size("rows")
    first_col = lax.axis_index("cols") * local_cols
    low_count = math.gcd(local_cols, 128)
    high_count = local_cols // low_count
    high_index = first_col + jnp.arange(high_count, dtype=jnp.int32) * low_count
    low_index = jnp.arange(low_count, dtype=jnp.int32)
    high_signs = sign_table(high_index, sampled)
    low_signs = sign_table(low_index, sampled)
    column_signs = ((1 - 2 * sign_bits).astype(jnp.float32) * (1.0 / math.sqrt(N))).astype(
        jnp.bfloat16
    )
    outer_signs = (high_signs[:, None, :] * low_signs[None, :, :]).reshape(
        local_cols, sampled.shape[0]
    )
    mixing = outer_signs * column_signs[:, None]
    partial_sketch = jnp.dot(slab, mixing, preferred_element_type=jnp.float32)
    sketch = lax.psum(partial_sketch, "cols")
    squares = lax.psum(jnp.sum(sketch * sketch, axis=0), "rows")
    basis = (sketch * lax.rsqrt(squares / total_rows + epsilon)).astype(jnp.bfloat16)
    scale_out = 1.0 / math.sqrt(total_rows)
    result = lax.psum_scatter(
        lax.dot_general(basis, slab, (((0,), (0,)), ((), ())), preferred_element_type=jnp.float32),
        "rows",
        scatter_dimension=0,
        tiled=True,
    )
    return result * scale_out


def solution(mesh):
    return jax.shard_map(
        per_device,
        mesh=mesh,
        in_specs=(P("rows", "cols"), P("cols"), P()),
        out_specs=P("rows", "cols"),
        check_vma=False,
    )
```

profile of v0, /device:TPU:0, one launch (start us, length us, event | category | flops | bytes accessed | tf_op | source)
XLA Modules:
  0.0 566.2 jit_solution(9333374048139813323)
XLA Ops:
  6.5 0.0 all-reduce.2.cloned.1.call-start
  6.5 0.9 multiply_convert_fusion.2
  7.5 1.2 subtract_convert_fusion
  8.7 1.8 fusion.39
  10.4 11.1 %broadcast_multiply_fusion = bf16[256,128,512]{2,1,0:T(8,128)(2,1)} fusion(bf16[128,512]{1,0:T(8,128)(2,1)S(1)} %subtract_convert_fusion, bf16[256,512]{1,0:T(8,128)(2,1)S(1)} %fusion.39), kind=kLoop, calls=%fused_computation.1 | loop fusion | flops 16777216 | bytes 33947648 | tf_op jit(solution)/shard_map/mul | solution.py:40
  21.5 22.9 %bitcast_multiply_fusion = bf16[32768,512]{1,0:T(8,128)(2,1)} fusion(bf16[256,128,512]{2,1,0:T(8,128)(2,1)} %broadcast_multiply_fusion, bf16[32768]{0:T(1024)(128)(2,1)S(1)} %multiply_convert_fusion.2), kind=kLoop, calls=%fused_computation | loop fusion | flops 16777216 | bytes 67174400 | tf_op jit(solution)/shard_map/mul | solution.py:43
  44.4 19.5 %convolution_bitcast_fusion = f32[256,512]{0,1:T(8,128)} fusion(bf16[32768,512]{1,0:T(8,128)(2,1)} %bitcast_multiply_fusion, bf16[256,32768]{1,0:T(8,128)(2,1)} %param.3), kind=kOutput, calls=%fused_computation.22 | convolution fusion | flops 8589934592 | bytes 50855936 | tf_op jit(solution)/shard_map/dot_general | solution.py:44
  63.8 0.0 all-reduce.2.cloned.1.call-update
  63.9 0.0 reduce-scatter.2.cloned.1.call-start
  63.9 63.5 %all-reduce.2.cloned.1.call-done = f32[256,512]{0,1:T(8,128)} async-done(((f32[256,512]{0,1:T(8,128)}), f32[256,512]{0,1:T(8,128)}) %all-reduce.2.cloned.1.call-update) | async-done | bytes 524304 | tf_op jit(solution)/shard_map/psum | solution.py:45
  127.4 1.2 multiply_reduce_fusion
  128.6 40.3 %psum.15 = f32[512]{0:T(512)S(1)} all-reduce(f32[512]{0:T(512)S(1)} %multiply_reduce_fusion), channel_id=1, replica_groups=mesh['rows'=16,'cols'=8] {'rows'}, use_global_device_ids=true, to_apply=%region_2.0 | all-reduce | flops 512 | bytes 4096 | tf_op jit(solution)/shard_map/psum | solution.py:46
  168.9 28.7 %fusion.40 = f32[512,32768]{1,0:T(8,128)} fusion(bf16[256,32768]{1,0:T(8,128)(2,1)} %param.3, f32[256,512]{0,1:T(8,128)} %all-reduce.2.cloned.1.call-done, f32[512]{0:T(512)S(1)} %add_rsqrt_fusion), kind=kOutput, calls=%fused_computation.65 | convolution fusion | flops 8590196736 | bytes 84412416 | tf_op jit(solution)/shard_map/dot_general | solution.py:50
  197.6 0.0 reduce-scatter.2.cloned.1.call-update
  197.6 357.3 %reduce-scatter.2.cloned.1.call-done = f32[32,32768]{1,0:T(8,128)} async-done(((f32[512,32768]{1,0:T(8,128)}), f32[32,32768]{1,0:T(8,128)}) %reduce-scatter.2.cloned.1.call-update) | async-done | bytes 4194320 | tf_op jit(solution)/shard_map/reduce_scatter | solution.py:49
  554.9 4.5 broadcast_multiply_fusion.1
  (2 shorter events, 0.0 us)
Async XLA Ops:
  6.5 120.9 %all-reduce.2.cloned.1.call-start = ((), (), s32[]{:S(2)}) async-start(), calls=%async_computation.1 | async-start | bytes 1048576 | tf_op jit(solution)/shard_map/psum | solution.py:45
  63.9 491.1 %reduce-scatter.2.cloned.1.call-start = ((), (), s32[]{:S(2)}) async-start(), calls=%async_computation.2 | async-start | bytes 71303168 | tf_op jit(solution)/shard_map/reduce_scatter | solution.py:49
Sparse Core Ops, SparseCore 0:
  64.0 63.3 all-reduce.1
  197.7 357.1 reduce-scatter.1
where the time goes:
time: 567 us; the launch traced here: 566 us
  waiting for transfers between devices  421 us (74%)
  matrix products  48.1 us (8%)
  other arithmetic  43.5 us (8%)
  blocking collectives  40.3 us (7%)
  between operations  13.4 us (2%)
    reduce_scatter x1, waiting for transfers between devices, per_device(): lax.psum_scatter(lax.dot_general(basis, slab, (((0,), (0,)), ((), ())), p...  357 us
    psum x1, waiting for transfers between devices, per_device(): sketch = lax.psum(partial_sketch, 'cols')  63.5 us
    psum x1, blocking collectives, per_device(): squares = lax.psum(jnp.sum(sketch * sketch, axis=0), 'rows')  40.3 us
    dot_general x1, matrix products, per_device(): lax.dot_general(basis, slab, (((0,), (0,)), ((), ())), preferred_element_...  28.7 us
    mul x1, other arithmetic, per_device(): mixing = outer_signs * column_signs[:, None]  22.9 us
    dot_general x1, matrix products, per_device(): partial_sketch = jnp.dot(slab, mixing, preferred_element_type=jnp.float32)  19.5 us
  transfers between devices with their start and end apart: 2, of which 2 were waited for; matrix products, arithmetic and copies ran while one was open for 0% of the time, Pallas kernels for 0%

commit v1 on v0

v1 whole, which is shorter than its diff:
```python
import math

import jax
import jax.numpy as jnp
from jax import lax
from jax.experimental import pallas as pl
from jax.experimental.pallas import tpu as pltpu
from jax.sharding import PartitionSpec as P

N = 262144
EPSILON = 1e-06
SIDE = 4
LOW = 1024
SKETCH_BLOCK = 4096
TILE = 512
WAVES = 2
DISTANCES = (1, 3, 2)
VMEM = 48 * 1024 * 1024


def x_perm(move):
    return [(y * SIDE + x, y * SIDE + move(x)) for y in range(SIDE) for x in range(SIDE)]


def y_perm(move):
    return [(y * SIDE + x, move(y) * SIDE + x) for y in range(SIDE) for x in range(SIDE)]


def parity_sign(values):
    for shift_by in (16, 8, 4, 2, 1):
        values = jnp.bitwise_xor(values, jnp.right_shift(values, shift_by))
    return (1 - 2 * jnp.bitwise_and(values, 1)).astype(jnp.float32)


def sketch_kernel(first_ref, slab_ref, bits_ref, sampled_ref, out_ref, low_ref, acc_ref):
    step = pl.program_id(0)
    sampled = sampled_ref[...]

    @pl.when(step == 0)
    def _():
        acc_ref[...] = jnp.zeros_like(acc_ref)
        column = lax.broadcasted_iota(jnp.int32, (sampled.shape[0], 128), 1)
        base = parity_sign(jnp.bitwise_and(column, sampled)) * (1.0 / math.sqrt(N))
        for part in range(LOW // 128):
            sign = parity_sign(jnp.bitwise_and(sampled, part * 128))
            low_ref[:, part * 128 : (part + 1) * 128] = (base * sign).astype(jnp.bfloat16)

    total = acc_ref[...]
    for part in range(SKETCH_BLOCK // LOW):
        where = slice(part * LOW, (part + 1) * LOW)
        flip = (1 - 2 * bits_ref[:, where]).astype(jnp.bfloat16)
        signed = slab_ref[:, where] * flip
        term = lax.dot_general(
            low_ref[...], signed, (((1,), (1,)), ((), ())), preferred_element_type=jnp.float32
        )
        high = first_ref[0] + step * SKETCH_BLOCK + part * LOW
        total = total + term * parity_sign(jnp.bitwise_and(sampled, high))
    acc_ref[...] = total

    @pl.when(step == pl.num_programs(0) - 1)
    def _():
        out_ref[...] = acc_ref[...]


def local_sketch(slab, sign_bits, sampled):
    rows, cols = slab.shape
    count = sampled.shape[0]
    first = (lax.axis_index("cols") * cols).astype(jnp.int32).reshape(1)
    return pl.pallas_call(
        sketch_kernel,
        grid_spec=pltpu.PrefetchScalarGridSpec(
            num_scalar_prefetch=1,
            grid=(cols // SKETCH_BLOCK,),
            in_specs=[
                pl.BlockSpec((rows, SKETCH_BLOCK), lambda i, s: (0, i)),
                pl.BlockSpec((1, SKETCH_BLOCK), lambda i, s: (0, i)),
                pl.BlockSpec((count, 1), lambda i, s: (0, 0)),
            ],
            out_specs=pl.BlockSpec((count, rows), lambda i, s: (0, 0)),
            scratch_shapes=[
                pltpu.VMEM((count, LOW), jnp.bfloat16),
                pltpu.VMEM((count, rows), jnp.float32),
            ],
        ),
        out_shape=jax.ShapeDtypeStruct((count, rows), jnp.float32),
        compiler_params=pltpu.CompilerParams(vmem_limit_bytes=VMEM),
        cost_estimate=pl.CostEstimate(
            flops=2 * count * rows * cols, bytes_accessed=2 * rows * cols, transcendentals=0
        ),
        name="sketch",
    )(first, slab, sign_bits.reshape(1, cols), sampled.reshape(count, 1))


def four_term_dot(basis, pieces):
    depth = pieces[0].shape[0]
    total = None
    for k, piece in enumerate(pieces):
        term = jnp.dot(
            basis[:, k * depth : (k + 1) * depth], piece[...], preferred_element_type=jnp.float32
        )
        total = term if total is None else total + term
    return total


def first_kernel(where_ref, low_ref, high_ref, p0, p1, p2, p3, out_ref):
    chunk = low_ref.shape[0]
    basis = jnp.concatenate([low_ref[...], high_ref[...]], axis=0)
    out_ref[...] = four_term_dot(basis, (p0, p1, p2, p3)).astype(out_ref.dtype)


def second_kernel(where_ref, basis_ref, p0, p1, p2, p3, got_ref, out_ref):
    total = four_term_dot(basis_ref[...], (p0, p1, p2, p3))
    out_ref[...] = (total + got_ref[...].astype(jnp.float32)).astype(out_ref.dtype)


def third_kernel(where_ref, basis_ref, p0, p1, p2, p3, ga1, ga2, gb1, gb2, own, o1, o2, o3, total_ref):
    total = four_term_dot(basis_ref[...], (p0, p1, p2, p3))
    is_a = pl.program_id(0) < pl.num_programs(0) // 2

    @pl.when(is_a)
    def _():
        total_ref[...] = total + ga1[...].astype(jnp.float32) + ga2[...].astype(jnp.float32)

    @pl.when(jnp.logical_not(is_a))
    def _():
        total_ref[...] = total + gb1[...].astype(jnp.float32) + gb2[...].astype(jnp.float32)

    height = own.shape[0]
    place = where_ref[4]
    own[...] = total_ref[pl.ds(pl.multiple_of(place * height, height), height), :]
    for out, distance in zip((o1, o2, o3), DISTANCES):
        row = lax.rem(place + distance, SIDE) * height
        out[...] = total_ref[pl.ds(pl.multiple_of(row, height), height), :].astype(out.dtype)


def product_call(kernel, name, where, out_shapes, out_specs, basis_specs, pieces, extra, extra_specs, tiles, column, basis, scratch=()):
    slab, received = pieces
    rows = slab.shape[0]
    piece_specs = [pl.BlockSpec((rows, TILE), lambda t, s: (0, s[5] + column + t))] + [
        pl.BlockSpec((rows, TILE), lambda t, s: (0, column + t)) for _ in received
    ]
    height = sum(spec.block_shape[0] for spec in basis_specs)
    depth = basis.shape[1]
    return pl.pallas_call(
        kernel,
        grid_spec=pltpu.PrefetchScalarGridSpec(
            num_scalar_prefetch=1,
            grid=(tiles,),
            in_specs=[*basis_specs, *piece_specs, *extra_specs],
            out_specs=out_specs,
            scratch_shapes=list(scratch),
        ),
        out_shape=out_shapes,
        compiler_params=pltpu.CompilerParams(vmem_limit_bytes=VMEM),
        cost_estimate=pl.CostEstimate(
            flops=2 * height * depth * tiles * TILE,
            bytes_accessed=2 * depth * (height + tiles * TILE),
            transcendentals=0,
        ),
        name=name,
    )(where, *([basis] * len(basis_specs)), slab, *received, *extra)


def assemble_kernel(where_ref, *refs):
    *pieces, out_ref = refs
    width = pieces[0].shape[1]
    scale = 1.0 / math.sqrt(4096)
    for group in range(len(pieces) // SIDE):
        place = where_ref[group % 2]
        for k, distance in enumerate((0,) + DISTANCES):
            piece = pieces[group * SIDE + k]
            source = lax.rem(place + SIDE - distance, SIDE)
            column = pl.multiple_of((group * SIDE + source) * width, width)
            out_ref[:, pl.ds(column, width)] = piece[...].astype(jnp.float32) * scale


def per_device(slab, sign_bits, sampled):
    rows, cols = slab.shape
    count = sampled.shape[0]
    col_devices = lax.axis_size("cols")
    total_rows = rows * lax.axis_size("rows")
    row_index = lax.axis_index("rows")
    y, x = row_index // SIDE, row_index % SIDE
    places = (x, y)
    perms = (x_perm, y_perm)
    width = cols // (WAVES * 2 * SIDE)
    half = width // 2
    chunk = count // SIDE

    received = {}
    for wave in range(WAVES):
        for axis in range(2):
            base = (wave * 2 + axis) * SIDE * width
            for distance in DISTANCES[::-1]:
                start = base + (places[axis] + distance) % SIDE * width
                block = lax.dynamic_slice(slab, (0, start), (rows, width))
                received[wave, axis, distance] = lax.ppermute(
                    block, "rows", perms[axis](lambda q: (q + distance) % SIDE)
                )

    partial = local_sketch(slab, sign_bits, sampled)
    share = count // col_devices
    parts = lax.all_to_all(partial, "cols", 0, 0, tiled=True)
    sketch = jnp.sum(parts.reshape(col_devices, share, rows), axis=0)
    local_squares = jnp.sum(sketch * sketch, axis=1)
    row_devices = lax.axis_size("rows")
    squares = jnp.sum(
        lax.all_to_all(jnp.broadcast_to(local_squares[None], (row_devices, share)), "rows", 0, 0, tiled=True), axis=0
    )
    basis = (sketch * lax.rsqrt(squares / total_rows + EPSILON)[:, None]).astype(jnp.bfloat16)

    finals = []
    bases = []
    for axis in range(2):
        terms = [basis] + [
            lax.ppermute(basis, "rows", perms[axis](lambda q: (q + distance) % SIDE)) for distance in DISTANCES
        ]
        joined = jnp.concatenate(terms, axis=1)
        whole = lax.all_to_all(jnp.tile(joined, (col_devices, 1)), "cols", 0, 0, tiled=True)
        if axis == 1:
            whole = whole.reshape(SIDE, SIDE, count // SIDE**2, -1).swapaxes(0, 1).reshape(count, -1)
        bases.append(whole)

    for wave in range(WAVES):
        for axis in range(2):
            other = 1 - axis
            q = places[other]
            perm = perms[other]
            basis_all = bases[axis]
            group = wave * 2 + axis
            pieces = (slab, [received[wave, axis, distance] for distance in DISTANCES])
            own_tile = (group * SIDE * width + places[axis] * width) // TILE
            tiles = half // TILE
            firsts, seconds = [], []
            for variant in range(2):
                if variant == 0:
                    one, two = (lambda v: v ^ 1), (lambda v: 3 - v)
                else:
                    one, two = (lambda v: 3 - v), (lambda v: v ^ 1)
                partner = one(q)
                where = jnp.stack([two(partner), partner, two(q), q, places[axis], own_tile]).astype(jnp.int32)
                column = variant * tiles
                sent = product_call(
                    first_kernel, "first", where,
                    jax.ShapeDtypeStruct((2 * chunk, half), jnp.bfloat16),
                    pl.BlockSpec((2 * chunk, TILE), lambda t, s: (0, t)),
                    [
                        pl.BlockSpec((chunk, basis_all.shape[1]), lambda t, s: (s[0], 0)),
                        pl.BlockSpec((chunk, basis_all.shape[1]), lambda t, s: (s[1], 0)),
                    ],
                    pieces, (), (), tiles, column, basis_all,
                )
                got = lax.ppermute(sent, "rows", perm(one))
                firsts.append(got)
                sent = product_call(
                    second_kernel, "second", where,
                    jax.ShapeDtypeStruct((chunk, half), jnp.bfloat16),
                    pl.BlockSpec((chunk, TILE), lambda t, s: (0, t)),
                    [pl.BlockSpec((chunk, basis_all.shape[1]), lambda t, s: (s[2], 0))],
                    pieces, (got,), (pl.BlockSpec((chunk, TILE), lambda t, s: (0, t)),), tiles, column, basis_all,
                )
                seconds.append(lax.ppermute(sent, "rows", perm(two)))
            height = chunk // SIDE
            a_tile = lambda t, s: (0, jnp.minimum(t, tiles - 1))
            b_tile = lambda t, s: (0, jnp.maximum(t - tiles, 0))
            a_high = lambda t, s: (1, jnp.minimum(t, tiles - 1))
            b_high = lambda t, s: (1, jnp.maximum(t - tiles, 0))
            out_spec = pl.BlockSpec((height, TILE), lambda t, s: (0, t))
            own, *sends = product_call(
                third_kernel, "third", where,
                [jax.ShapeDtypeStruct((height, width), jnp.float32)]
                + [jax.ShapeDtypeStruct((height, width), jnp.bfloat16)] * 3,
                [out_spec] * 4,
                [pl.BlockSpec((chunk, basis_all.shape[1]), lambda t, s: (s[3], 0))],
                pieces, (firsts[0], seconds[0], firsts[1], seconds[1]),
                tuple(pl.BlockSpec((chunk, TILE), m) for m in (a_high, a_tile, b_high, b_tile)),
                2 * tiles, 0, basis_all,
                (pltpu.VMEM((chunk, TILE), jnp.float32),),
            )
            finals.append(own)
            for distance, send in zip(DISTANCES, sends):
                finals.append(lax.ppermute(send, "rows", perms[axis](lambda v: (v + distance) % SIDE)))

    where = jnp.stack([x, y]).astype(jnp.int32)
    height = count // row_devices
    return pl.pallas_call(
        assemble_kernel,
        grid_spec=pltpu.PrefetchScalarGridSpec(
            num_scalar_prefetch=1,
            grid=(1,),
            in_specs=[pl.BlockSpec((height, width), lambda i, s: (0, 0))] * len(finals),
            out_specs=pl.BlockSpec((height, cols), lambda i, s: (0, 0)),
        ),
        out_shape=jax.ShapeDtypeStruct((height, cols), jnp.float32),
        compiler_params=pltpu.CompilerParams(vmem_limit_bytes=VMEM),
        name="assemble",
    )(where, *finals)


def solution(mesh):
    return jax.shard_map(
        per_device,
        mesh=mesh,
        in_specs=(P("rows", "cols"), P("cols"), P()),
        out_specs=P("rows", "cols"),
        check_vma=False,
    )
```

time: 567 us -> 297 us (0.52)
  waiting for transfers between devices: 421 us -> 99.4 us
  starting transfers between devices: 0.04 us -> 94 us
  Pallas kernels: 0 us -> 80.7 us
  matrix products: 48.1 us -> 0 us
  other arithmetic: 43.5 us -> 0.34 us
  blocking collectives: 40.3 us -> 0 us
  local copies, waits for them, and re-layouts: 0 us -> 20.8 us
  between operations: 13.4 us -> 0.41 us
    reduce_scatter x1 -> x0, waiting for transfers between devices: 357 us -> none  [per_device(): lax.psum_scatter(lax.dot_general(basis, slab, (((0,), (0,)), ((), ())), p...]
    pallas_call x0 -> x22, Pallas kernels: none -> 80.7 us  [the longest x20 62.1 us: product_call(): pl.pallas_call(kernel, grid_spec=pltpu.PrefetchScalarGridSpec(num_scalar_...]
    ppermute x0 -> x46, starting transfers between devices: none -> 74 us  [the longest x12 23.8 us: per_device(): lax.ppermute(block, 'rows', perms[axis](lambda q: (q + distance) % SIDE))]
    ppermute x0 -> x46, waiting for transfers between devices: none -> 64 us  [the longest x12 38.6 us: per_device(): lax.ppermute(block, 'rows', perms[axis](lambda q: (q + distance) % SIDE))]
    psum x1 -> x0, waiting for transfers between devices: 63.5 us -> none  [per_device(): sketch = lax.psum(partial_sketch, 'cols')]
    dot_general x2 -> x0, matrix products: 48.1 us -> none  [the longest x1 28.7 us: per_device(): lax.dot_general(basis, slab, (((0,), (0,)), ((), ())), preferred_element_...]
    psum x1 -> x0, blocking collectives: 40.3 us -> none  [per_device(): squares = lax.psum(jnp.sum(sketch * sketch, axis=0), 'rows')]
    mul x3 -> x0, other arithmetic: 38.4 us -> none  [the longest x1 22.9 us: per_device(): mixing = outer_signs * column_signs[:, None]]
  transfers between devices with their start and end apart: 2 -> 50, of which waited for: 2 -> 14; matrix products, arithmetic and copies ran while one was open for 0% -> 5% of each run, Pallas kernels for 0% -> 21%
where the time goes in v1:
time: 297 us; the launch traced here: 296 us
  waiting for transfers between devices  99.4 us (33%)
  starting transfers between devices  94 us (32%)
  Pallas kernels  80.7 us (27%)
  local copies, waits for them, and re-layouts  20.8 us (7%)
    pallas_call x20, Pallas kernels, product_call(): pl.pallas_call(kernel, grid_spec=pltpu.PrefetchScalarGridSpec(num_scalar_...  62.1 us
    ppermute x12, waiting for transfers between devices, per_device(): lax.ppermute(block, 'rows', perms[axis](lambda q: (q + distance) % SIDE))  38.6 us
    all_to_all x1, waiting for transfers between devices, per_device(): lax.all_to_all(jnp.broadcast_to(local_squares[None], (row_devices, share)...  35.2 us
    ppermute x12, starting transfers between devices, per_device(): lax.ppermute(block, 'rows', perms[axis](lambda q: (q + distance) % SIDE))  23.8 us
    ppermute x6, waiting for transfers between devices, per_device(): lax.ppermute(basis, 'rows', perms[axis](lambda q: (q + distance) % SIDE))  20.2 us
    ppermute x12, starting transfers between devices, per_device(): lax.ppermute(send, 'rows', perms[axis](lambda v: (v + distance) % SIDE))  17.9 us
    pallas_call x1, Pallas kernels, local_sketch(): pl.pallas_call(sketch_kernel, grid_spec=pltpu.PrefetchScalarGridSpec(num_...  15.7 us
    ppermute x8, starting transfers between devices, per_device(): seconds.append(lax.ppermute(sent, 'rows', perm(two)))  11.1 us
  transfers between devices with their start and end apart: 50, of which 14 were waited for; matrix products, arithmetic and copies ran while one was open for 5% of the time, Pallas kernels for 21%

profile of v1, /device:TPU:0, one launch (start us, length us, event | category | flops | bytes accessed | tf_op | source)
XLA Modules:
  0.0 295.7 jit_solution(2164903864200056466)
XLA Ops:
  1.7 15.7 %sketch.1 = f32[512,256]{1,0:T(8,128)} custom-call(s32[1]{0:T(128)} %bitcast.6.first_ref, bf16[256,32768]{1,0:T(8,128)(2,1)} %p0.39, s32[1,32768]{1,0:T(1,128)S(1)} %bitcast.52, s32[512,1]{1,0:T(8,128)S(1)} %copy.8.sampled_ref), custom_call_target="tpu_custom_call" | custom-call | flops 8589934592 | bytes 16777216 | tf_op jit(solution)/shard_map/sketch/pallas_call | solution.py:69
  17.4 5.4 %all-to-all-start = ((f32[8,64,256]{2,1,0:T(8,128)}), f32[8,64,256]{2,1,0:T(8,128)S(1)}, u32[]{:S(2)}, u32[]{:S(2)}) async-start(f32[8,64,256]{2,1,0:T(8,128)} %bitcast.9), calls=%async_computation | async-start | bytes 1048576 | tf_op jit(solution)/shard_map/all_to_all | solution.py:203
  22.8 9.4 %constant_dynamic-slice_fusion = (bf16[256,2048]{1,0:T(8,128)(2,1)}, bf16[256,2048]{1,0:T(8,128)(2,1)}, bf16[256,2048]{1,0:T(8,128)(2,1)}, bf16[256,2048]{1,0:T(...) fusion(bf16[256,32768]{1,0:T(8,128)(2,1)} %p0.39, ...), kind=kLoop, calls=%fused_computation.8 | loop fusion | bytes 25165872 | tf_op jit(solution)/shard_map/dynamic_slice | solution.py:196
  36.3 5.8 %all-to-all-start.1 = ((f32[16,1,64]{2,1,0:T(1,128)}), f32[16,1,64]{2,1,0:T(1,128)S(1)}, u32[]{:S(2)}, u32[]{:S(2)}) async-start(f32[16,1,64]{2,1,0:T(1,128)} %broadcast_in_dim.2), calls=%async_computation.1 | async-start | bytes 16384 | tf_op jit(solution)/shard_map/all_to_all | solution.py:208
  42.2 3.4 %collective-permute-start.38 = (bf16[256,2048]{1,0:T(8,128)(2,1)}, bf16[256,2048]{1,0:T(8,128)(2,1)S(1)}, u32[]{:S(2)}, u32[]{:S(2)}) collective-permute-start(bf16[256,2048]{1,0:T(8,128)(2,1)} %get-tuple-element.37), channel_id=1, source_target_pairs={{0,64},{8,72},{16,80},{24,88},{32,96},{40,104},{48,112},{56,120},{... | collective-permute-start | bytes 3145736 | tf_op jit(solution)/shard_map/ppermute | solution.py:197
  45.6 35.2 %all-to-all-done.1 = f32[16,1,64]{2,1,0:T(1,128)S(1)} async-done(((f32[16,1,64]{2,1,0:T(1,128)}), f32[16,1,64]{2,1,0:T(1,128)S(1)}, u32[]{:S(2)}, u32[]{:S(2)}) %all-to-all-start.1) | async-done | bytes 4128 | tf_op jit(solution)/shard_map/all_to_all | solution.py:208
  86.4 4.4 %collective-permute-start.14 = (bf16[64,256]{1,0:T(8,128)(2,1)S(1)}, bf16[64,256]{1,0:T(8,128)(2,1)S(1)}, u32[]{:S(2)}, u32[]{:S(2)}) collective-permute-start(bf16[64,256]{1,0:T(8,128)(2,1)S(1)} %multiply_convert_fusion), channel_id=1, source_target_pairs={{0,96},{8,104},{16,112},{24,120},{32,0},{40,8},{48,16},{56,24},{64... | collective-permute-start | bytes 98312 | tf_op jit(solution)/shard_map/ppermute | solution.py:216
  94.2 4.0 %collective-permute-done.15 = bf16[64,256]{1,0:T(8,128)(2,1)S(1)} collective-permute-done((bf16[64,256]{1,0:T(8,128)(2,1)S(1)}, bf16[64,256]{1,0:T(8,128)(2,1)S(1)}, u32[]{:S(2)}, u32[]{:S(2)}) %collective-permute-start.15) | collective-permute-done | bytes 32800 | tf_op jit(solution)/shard_map/ppermute | solution.py:216
  100.0 12.2 %collective-permute-done.2 = bf16[64,256]{1,0:T(8,128)(2,1)S(1)} collective-permute-done((bf16[64,256]{1,0:T(8,128)(2,1)S(1)}, bf16[64,256]{1,0:T(8,128)(2,1)S(1)}, u32[]{:S(2)}, u32[]{:S(2)}) %collective-permute-start.2) | collective-permute-done | bytes 32800 | tf_op jit(solution)/shard_map/ppermute | solution.py:216
  113.3 4.4 %all-to-all-start.3 = ((bf16[8,64,1024]{2,1,0:T(8,128)(2,1)}), bf16[8,64,1024]{2,1,0:T(8,128)(2,1)}, u32[]{:S(2)}, u32[]{:S(2)}) async-start(bf16[8,64,1024]{2,1,0:T(8,128)(2,1)} %tile.5), calls=%async_computation.3 | async-start | bytes 2097152 | tf_op jit(solution)/shard_map/all_to_all | solution.py:219
  123.3 10.4 %collective-permute-done.27.p2 = bf16[256,2048]{1,0:T(8,128)(2,1)} collective-permute-done((bf16[256,2048]{1,0:T(8,128)(2,1)}, bf16[256,2048]{1,0:T(8,128)(2,1)}, u32[]{:S(2)}, u32[]{:S(2)}) %collective-permute-start.27) | collective-permute-done | bytes 1048608 | tf_op jit(solution)/shard_map/ppermute | solution.py:197
  134.9 4.3 %all-to-all-start.2 = ((bf16[8,64,1024]{2,1,0:T(8,128)(2,1)}), bf16[8,64,1024]{2,1,0:T(8,128)(2,1)S(1)}, u32[]{:S(2)}, u32[]{:S(2)}) async-start(bf16[8,64,1024]{2,1,0:T(8,128)(2,1)} %tile.4), calls=%async_computation.2 | async-start | bytes 2097152 | tf_op jit(solution)/shard_map/all_to_all | solution.py:219
  139.3 6.4 %collective-permute-done.28.p3 = bf16[256,2048]{1,0:T(8,128)(2,1)} collective-permute-done((bf16[256,2048]{1,0:T(8,128)(2,1)}, bf16[256,2048]{1,0:T(8,128)(2,1)}, u32[]{:S(2)}, u32[]{:S(2)}) %collective-permute-start.28) | collective-permute-done | bytes 1048608 | tf_op jit(solution)/shard_map/ppermute | solution.py:197
  145.7 8.6 %collective-permute-start.4 = (bf16[256,2048]{1,0:T(8,128)(2,1)}, bf16[256,2048]{1,0:T(8,128)(2,1)}, u32[]{:S(2)}, u32[]{:S(2)}) collective-permute-start(bf16[256,2048]{1,0:T(8,128)(2,1)} %get-tuple-element.47), channel_id=1, source_target_pairs={{0,24},{8,0},{16,8},{24,16},{32,56},{40,32},{48,40},{56,48},{64,88... | collective-permute-start | bytes 3145736 | tf_op jit(solution)/shard_map/ppermute | solution.py:197
  154.2 13.6 %collective-permute-done.16.p1 = bf16[256,2048]{1,0:T(8,128)(2,1)} collective-permute-done((bf16[256,2048]{1,0:T(8,128)(2,1)}, bf16[256,2048]{1,0:T(8,128)(2,1)}, u32[]{:S(2)}, u32[]{:S(2)}) %collective-permute-start.16) | collective-permute-done | bytes 1048608 | tf_op jit(solution)/shard_map/ppermute | solution.py:197
  185.4 3.4 %first.13 = bf16[256,1024]{1,0:T(8,128)(2,1)} custom-call(s32[6]{0:T(128)S(1)} %stack.123.where_ref, bf16[512,1024]{1,0:T(8,128)(2,1)S(1)} %bitcast.24, bf16[512,1024]{1,0:T(8,128)(2,1)S(1)} %bitcast.25, bf16[256,32768]{1,0:T(8,128)(2,1)} %p0.39, bf16[256,2048]{1,0:T(8,128)(2,1)} %collective-permute-done.26.p1, ...), custom_call_target="tpu_custom_call" | custom-call | flops 536870912 | bytes 2621440 | tf_op jit(solution)/shard_map/first/pallas_call | solution.py:144
  189.1 3.4 %first.12 = bf16[256,1024]{1,0:T(8,128)(2,1)} custom-call(s32[6]{0:T(128)S(1)} %stack.124.where_ref, bf16[512,1024]{1,0:T(8,128)(2,1)S(1)} %bitcast.26, bf16[512,1024]{1,0:T(8,128)(2,1)S(1)} %bitcast.27, bf16[256,32768]{1,0:T(8,128)(2,1)} %p0.39, bf16[256,2048]{1,0:T(8,128)(2,1)} %collective-permute-done.26.p1, ...), custom_call_target="tpu_custom_call" | custom-call | flops 536870912 | bytes 2621440 | tf_op jit(solution)/shard_map/first/pallas_call | solution.py:144
  192.5 8.1 %collective-permute-done.4.p2 = bf16[256,2048]{1,0:T(8,128)(2,1)} collective-permute-done((bf16[256,2048]{1,0:T(8,128)(2,1)}, bf16[256,2048]{1,0:T(8,128)(2,1)}, u32[]{:S(2)}, u32[]{:S(2)}) %collective-permute-start.4) | collective-permute-done | bytes 1048608 | tf_op jit(solution)/shard_map/ppermute | solution.py:197
  204.4 3.7 %collective-permute-start.21 = (bf16[256,1024]{1,0:T(8,128)(2,1)}, bf16[256,1024]{1,0:T(8,128)(2,1)}, u32[]{:S(2)}, u32[]{:S(2)}) collective-permute-start(bf16[256,1024]{1,0:T(8,128)(2,1)} %first.11), channel_id=1, source_target_pairs={{0,24},{8,16},{16,8},{24,0},{32,56},{40,48},{48,40},{56,32},{64,88... | collective-permute-start | bytes 1572872 | tf_op jit(solution)/shard_map/ppermute | solution.py:253
  214.7 3.9 %collective-permute-start.8 = (bf16[256,1024]{1,0:T(8,128)(2,1)S(1)}, bf16[256,1024]{1,0:T(8,128)(2,1)S(1)}, u32[]{:S(2)}, u32[]{:S(2)}) collective-permute-start(bf16[256,1024]{1,0:T(8,128)(2,1)S(1)} %first.9), channel_id=1, source_target_pairs={{0,96},{8,104},{16,112},{24,120},{32,64},{40,72},{48,80},{56,88},{... | collective-permute-start | bytes 1572872 | tf_op jit(solution)/shard_map/ppermute | solution.py:253
  252.2 4.2 %third.7 = (f32[32,2048]{1,0:T(8,128)S(1)}, bf16[32,2048]{1,0:T(8,128)(2,1)S(1)}, bf16[32,2048]{1,0:T(8,128)(2,1)S(1)}, bf16[32,2048]{1,0:T(8,128)(2,1)S(1)}) custom-call(s32[6]{0:T(128)S(1)} %stack.126.where_ref, bf16[512,1024]{1,0:T(8,128)(2,1)S(1)} %bitcast.50, bf16[256,32768]{1,0:T(8,128)(2,1)} %p0.39, bf16[256,2048]{1,0:T(8,128)(2,1)S(1)} %collective-permute-done.36.p1, ...), custom_call_target="tpu_custom_call" | custom-call | flops 536870912 | bytes 4456448 | tf_op jit(solution)/shard_map/third/pallas_call | solution.py:144
  259.6 4.5 %third.6 = (f32[32,2048]{1,0:T(8,128)S(1)}, bf16[32,2048]{1,0:T(8,128)(2,1)S(1)}, bf16[32,2048]{1,0:T(8,128)(2,1)S(1)}, bf16[32,2048]{1,0:T(8,128)(2,1)S(1)}) custom-call(s32[6]{0:T(128)S(1)} %stack.123.where_ref, bf16[512,1024]{1,0:T(8,128)(2,1)S(1)} %bitcast.36, bf16[256,32768]{1,0:T(8,128)(2,1)} %p0.39, bf16[256,2048]{1,0:T(8,128)(2,1)} %collective-permute-done.26.p1, ...), custom_call_target="tpu_custom_call" | custom-call | flops 536870912 | bytes 4456448 | tf_op jit(solution)/shard_map/third/pallas_call | solution.py:144
  264.6 4.5 %third.5 = (f32[32,2048]{1,0:T(8,128)S(1)}, bf16[32,2048]{1,0:T(8,128)(2,1)S(1)}, bf16[32,2048]{1,0:T(8,128)(2,1)S(1)}, bf16[32,2048]{1,0:T(8,128)(2,1)S(1)}) custom-call(s32[6]{0:T(128)S(1)} %stack.119.where_ref, bf16[512,1024]{1,0:T(8,128)(2,1)S(1)} %bitcast.51, bf16[256,32768]{1,0:T(8,128)(2,1)} %p0.39, bf16[256,2048]{1,0:T(8,128)(2,1)} %collective-permute-done.16.p1, ...), custom_call_target="tpu_custom_call" | custom-call | flops 536870912 | bytes 4456448 | tf_op jit(solution)/shard_map/third/pallas_call | solution.py:144
  274.0 4.3 %third.4 = (f32[32,2048]{1,0:T(8,128)S(1)}, bf16[32,2048]{1,0:T(8,128)(2,1)S(1)}, bf16[32,2048]{1,0:T(8,128)(2,1)S(1)}, bf16[32,2048]{1,0:T(8,128)(2,1)S(1)}) custom-call(s32[6]{0:T(128)S(1)} %stack.53.where_ref, bf16[512,1024]{1,0:T(8,128)(2,1)S(1)} %bitcast.37, bf16[256,32768]{1,0:T(8,128)(2,1)} %p0.39, bf16[256,2048]{1,0:T(8,128)(2,1)} %collective-permute-done.3.p1, ...), custom_call_target="tpu_custom_call" | custom-call | flops 536870912 | bytes 4456448 | tf_op jit(solution)/shard_map/third/pallas_call | solution.py:144
  (137 shorter events, 112.0 us)
Async XLA Ops:
  32.3 85.5 %collective-permute-start.36 = (bf16[256,2048]{1,0:T(8,128)(2,1)}, bf16[256,2048]{1,0:T(8,128)(2,1)S(1)}, u32[]{:S(2)}, u32[]{:S(2)}) collective-permute-start(bf16[256,2048]{1,0:T(8,128)(2,1)} %get-tuple-element.39), channel_id=1, source_target_pairs={{0,32},{8,40},{16,48},{24,56},{32,64},{40,72},{48,80},{56,88},{64,... | collective-permute-start | bytes 3145736 | tf_op jit(solution)/shard_map/ppermute | solution.py:197
  33.9 84.8 %collective-permute-start.37 = (bf16[256,2048]{1,0:T(8,128)(2,1)}, bf16[256,2048]{1,0:T(8,128)(2,1)S(1)}, u32[]{:S(2)}, u32[]{:S(2)}) collective-permute-start(bf16[256,2048]{1,0:T(8,128)(2,1)} %get-tuple-element.38), channel_id=1, source_target_pairs={{0,96},{8,104},{16,112},{24,120},{32,0},{40,8},{48,16},{56,24},{64... | collective-permute-start | bytes 3145736 | tf_op jit(solution)/shard_map/ppermute | solution.py:197
  36.3 44.5 %all-to-all-start.1 = ((f32[16,1,64]{2,1,0:T(1,128)}), f32[16,1,64]{2,1,0:T(1,128)S(1)}, u32[]{:S(2)}, u32[]{:S(2)}) async-start(f32[16,1,64]{2,1,0:T(1,128)} %broadcast_in_dim.2), calls=%async_computation.1 | async-start | bytes 16384 | tf_op jit(solution)/shard_map/all_to_all | solution.py:208
  42.2 77.1 %collective-permute-start.38 = (bf16[256,2048]{1,0:T(8,128)(2,1)}, bf16[256,2048]{1,0:T(8,128)(2,1)S(1)}, u32[]{:S(2)}, u32[]{:S(2)}) collective-permute-start(bf16[256,2048]{1,0:T(8,128)(2,1)} %get-tuple-element.37), channel_id=1, source_target_pairs={{0,64},{8,72},{16,80},{24,88},{32,96},{40,104},{48,112},{56,120},{... | collective-permute-start | bytes 3145736 | tf_op jit(solution)/shard_map/ppermute | solution.py:197
  93.9 28.0 %collective-permute-start.26 = (bf16[256,2048]{1,0:T(8,128)(2,1)}, bf16[256,2048]{1,0:T(8,128)(2,1)}, u32[]{:S(2)}, u32[]{:S(2)}) collective-permute-start(bf16[256,2048]{1,0:T(8,128)(2,1)} %get-tuple-element.42), channel_id=1, source_target_pairs={{0,8},{8,16},{16,24},{24,0},{32,40},{40,48},{48,56},{56,32},{64,72... | collective-permute-start | bytes 3145736 | tf_op jit(solution)/shard_map/ppermute | solution.py:197
  112.2 21.5 %collective-permute-start.27 = (bf16[256,2048]{1,0:T(8,128)(2,1)}, bf16[256,2048]{1,0:T(8,128)(2,1)}, u32[]{:S(2)}, u32[]{:S(2)}) collective-permute-start(bf16[256,2048]{1,0:T(8,128)(2,1)} %get-tuple-element.41), channel_id=1, source_target_pairs={{0,24},{8,0},{16,8},{24,16},{32,56},{40,32},{48,40},{56,48},{64,88... | collective-permute-start | bytes 3145736 | tf_op jit(solution)/shard_map/ppermute | solution.py:197
  117.7 27.9 %collective-permute-start.28 = (bf16[256,2048]{1,0:T(8,128)(2,1)}, bf16[256,2048]{1,0:T(8,128)(2,1)}, u32[]{:S(2)}, u32[]{:S(2)}) collective-permute-start(bf16[256,2048]{1,0:T(8,128)(2,1)} %get-tuple-element.40), channel_id=1, source_target_pairs={{0,16},{8,24},{16,0},{24,8},{32,48},{40,56},{48,32},{56,40},{64,80... | collective-permute-start | bytes 3145736 | tf_op jit(solution)/shard_map/ppermute | solution.py:197
  118.7 49.2 %collective-permute-start.16 = (bf16[256,2048]{1,0:T(8,128)(2,1)}, bf16[256,2048]{1,0:T(8,128)(2,1)}, u32[]{:S(2)}, u32[]{:S(2)}) collective-permute-start(bf16[256,2048]{1,0:T(8,128)(2,1)} %get-tuple-element.45), channel_id=1, source_target_pairs={{0,32},{8,40},{16,48},{24,56},{32,64},{40,72},{48,80},{56,88},{64,... | collective-permute-start | bytes 3145736 | tf_op jit(solution)/shard_map/ppermute | solution.py:197
  119.2 58.4 %collective-permute-start.17 = (bf16[256,2048]{1,0:T(8,128)(2,1)}, bf16[256,2048]{1,0:T(8,128)(2,1)}, u32[]{:S(2)}, u32[]{:S(2)}) collective-permute-start(bf16[256,2048]{1,0:T(8,128)(2,1)} %get-tuple-element.44), channel_id=1, source_target_pairs={{0,96},{8,104},{16,112},{24,120},{32,0},{40,8},{48,16},{56,24},{64... | collective-permute-start | bytes 3145736 | tf_op jit(solution)/shard_map/ppermute | solution.py:197
  121.9 63.0 %collective-permute-start.18 = (bf16[256,2048]{1,0:T(8,128)(2,1)}, bf16[256,2048]{1,0:T(8,128)(2,1)}, u32[]{:S(2)}, u32[]{:S(2)}) collective-permute-start(bf16[256,2048]{1,0:T(8,128)(2,1)} %get-tuple-element.43), channel_id=1, source_target_pairs={{0,64},{8,72},{16,80},{24,88},{32,96},{40,104},{48,112},{56,120},{... | collective-permute-start | bytes 3145736 | tf_op jit(solution)/shard_map/ppermute | solution.py:197
  133.7 55.1 %collective-permute-start.3 = (bf16[256,2048]{1,0:T(8,128)(2,1)}, bf16[256,2048]{1,0:T(8,128)(2,1)}, u32[]{:S(2)}, u32[]{:S(2)}) collective-permute-start(bf16[256,2048]{1,0:T(8,128)(2,1)} %get-tuple-element.48), channel_id=1, source_target_pairs={{0,8},{8,16},{16,24},{24,0},{32,40},{40,48},{48,56},{56,32},{64,72... | collective-permute-start | bytes 3145736 | tf_op jit(solution)/shard_map/ppermute | solution.py:197
  134.9 50.5 %all-to-all-start.2 = ((bf16[8,64,1024]{2,1,0:T(8,128)(2,1)}), bf16[8,64,1024]{2,1,0:T(8,128)(2,1)S(1)}, u32[]{:S(2)}, u32[]{:S(2)}) async-start(bf16[8,64,1024]{2,1,0:T(8,128)(2,1)} %tile.4), calls=%async_computation.2 | async-start | bytes 2097152 | tf_op jit(solution)/shard_map/all_to_all | solution.py:219
  145.7 55.0 %collective-permute-start.4 = (bf16[256,2048]{1,0:T(8,128)(2,1)}, bf16[256,2048]{1,0:T(8,128)(2,1)}, u32[]{:S(2)}, u32[]{:S(2)}) collective-permute-start(bf16[256,2048]{1,0:T(8,128)(2,1)} %get-tuple-element.47), channel_id=1, source_target_pairs={{0,24},{8,0},{16,8},{24,16},{32,56},{40,32},{48,40},{56,48},{64,88... | collective-permute-start | bytes 3145736 | tf_op jit(solution)/shard_map/ppermute | solution.py:197
  167.9 36.5 %collective-permute-start.5 = (bf16[256,2048]{1,0:T(8,128)(2,1)}, bf16[256,2048]{1,0:T(8,128)(2,1)}, u32[]{:S(2)}, u32[]{:S(2)}) collective-permute-start(bf16[256,2048]{1,0:T(8,128)(2,1)} %get-tuple-element.46), channel_id=1, source_target_pairs={{0,16},{8,24},{16,0},{24,8},{32,48},{40,56},{48,32},{56,40},{64,80... | collective-permute-start | bytes 3145736 | tf_op jit(solution)/shard_map/ppermute | solution.py:197
  177.6 33.8 %collective-permute-start.41 = (bf16[256,1024]{1,0:T(8,128)(2,1)}, bf16[256,1024]{1,0:T(8,128)(2,1)}, u32[]{:S(2)}, u32[]{:S(2)}) collective-permute-start(bf16[256,1024]{1,0:T(8,128)(2,1)} %first.15), channel_id=1, source_target_pairs={{0,24},{8,16},{16,8},{24,0},{32,56},{40,48},{48,40},{56,32},{64,88... | collective-permute-start | bytes 1572872 | tf_op jit(solution)/shard_map/ppermute | solution.py:253
  184.9 29.8 %collective-permute-start.39 = (bf16[256,1024]{1,0:T(8,128)(2,1)}, bf16[256,1024]{1,0:T(8,128)(2,1)}, u32[]{:S(2)}, u32[]{:S(2)}) collective-permute-start(bf16[256,1024]{1,0:T(8,128)(2,1)} %first.14), channel_id=1, source_target_pairs={{0,8},{8,0},{16,24},{24,16},{32,40},{40,32},{48,56},{56,48},{64,72... | collective-permute-start | bytes 1572872 | tf_op jit(solution)/shard_map/ppermute | solution.py:253
  188.8 32.5 %collective-permute-start.31 = (bf16[256,1024]{1,0:T(8,128)(2,1)}, bf16[256,1024]{1,0:T(8,128)(2,1)}, u32[]{:S(2)}, u32[]{:S(2)}) collective-permute-start(bf16[256,1024]{1,0:T(8,128)(2,1)} %first.13), channel_id=1, source_target_pairs={{0,96},{8,104},{16,112},{24,120},{32,64},{40,72},{48,80},{56,88},{... | collective-permute-start | bytes 1572872 | tf_op jit(solution)/shard_map/ppermute | solution.py:253
  200.6 23.1 %collective-permute-start.29 = (bf16[256,1024]{1,0:T(8,128)(2,1)}, bf16[256,1024]{1,0:T(8,128)(2,1)}, u32[]{:S(2)}, u32[]{:S(2)}) collective-permute-start(bf16[256,1024]{1,0:T(8,128)(2,1)} %first.12), channel_id=1, source_target_pairs={{0,32},{8,40},{16,48},{24,56},{32,0},{40,8},{48,16},{56,24},{64,96... | collective-permute-start | bytes 1572872 | tf_op jit(solution)/shard_map/ppermute | solution.py:253
  204.4 23.6 %collective-permute-start.21 = (bf16[256,1024]{1,0:T(8,128)(2,1)}, bf16[256,1024]{1,0:T(8,128)(2,1)}, u32[]{:S(2)}, u32[]{:S(2)}) collective-permute-start(bf16[256,1024]{1,0:T(8,128)(2,1)} %first.11), channel_id=1, source_target_pairs={{0,24},{8,16},{16,8},{24,0},{32,56},{40,48},{48,40},{56,32},{64,88... | collective-permute-start | bytes 1572872 | tf_op jit(solution)/shard_map/ppermute | solution.py:253
  211.5 21.2 %collective-permute-start.19 = (bf16[256,1024]{1,0:T(8,128)(2,1)}, bf16[256,1024]{1,0:T(8,128)(2,1)}, u32[]{:S(2)}, u32[]{:S(2)}) collective-permute-start(bf16[256,1024]{1,0:T(8,128)(2,1)} %first.10), channel_id=1, source_target_pairs={{0,8},{8,0},{16,24},{24,16},{32,40},{40,32},{48,56},{56,48},{64,72... | collective-permute-start | bytes 1572872 | tf_op jit(solution)/shard_map/ppermute | solution.py:253
  235.5 20.8 %collective-permute-start.30 = (bf16[128,1024]{1,0:T(8,128)(2,1)S(1)}, bf16[128,1024]{1,0:T(8,128)(2,1)S(1)}, u32[]{:S(2)}, u32[]{:S(2)}) collective-permute-start(bf16[128,1024]{1,0:T(8,128)(2,1)S(1)} %second.12), channel_id=1, source_target_pairs={{0,96},{8,104},{16,112},{24,120},{32,64},{40,72},{48,80},{56,88},{... | collective-permute-start | bytes 786440 | tf_op jit(solution)/shard_map/ppermute | solution.py:262
  242.7 21.4 %collective-permute-start.20 = (bf16[128,1024]{1,0:T(8,128)(2,1)S(1)}, bf16[128,1024]{1,0:T(8,128)(2,1)S(1)}, u32[]{:S(2)}, u32[]{:S(2)}) collective-permute-start(bf16[128,1024]{1,0:T(8,128)(2,1)S(1)} %second.10), channel_id=1, source_target_pairs={{0,24},{8,16},{16,8},{24,0},{32,56},{40,48},{48,40},{56,32},{64,88... | collective-permute-start | bytes 786440 | tf_op jit(solution)/shard_map/ppermute | solution.py:262
  246.3 22.7 %collective-permute-start.9 = (bf16[128,1024]{1,0:T(8,128)(2,1)S(1)}, bf16[128,1024]{1,0:T(8,128)(2,1)S(1)}, u32[]{:S(2)}, u32[]{:S(2)}) collective-permute-start(bf16[128,1024]{1,0:T(8,128)(2,1)S(1)} %second.9), channel_id=1, source_target_pairs={{0,32},{8,40},{16,48},{24,56},{32,0},{40,8},{48,16},{56,24},{64,96... | collective-permute-start | bytes 786440 | tf_op jit(solution)/shard_map/ppermute | solution.py:262
  248.9 21.6 %collective-permute-start.7 = (bf16[128,1024]{1,0:T(8,128)(2,1)S(1)}, bf16[128,1024]{1,0:T(8,128)(2,1)S(1)}, u32[]{:S(2)}, u32[]{:S(2)}) collective-permute-start(bf16[128,1024]{1,0:T(8,128)(2,1)S(1)} %second.8), channel_id=1, source_target_pairs={{0,96},{8,104},{16,112},{24,120},{32,64},{40,72},{48,80},{56,88},{... | collective-permute-start | bytes 786440 | tf_op jit(solution)/shard_map/ppermute | solution.py:262
  (35 other events, 408.8 us)

commit v2 on v0

v2 whole, which is shorter than its diff:
```python
import functools
import math

import jax
import jax.numpy as jnp
from jax import lax
from jax.experimental import pallas as pl
from jax.experimental.pallas import tpu as pltpu
from jax.sharding import PartitionSpec as P

N = 262144
EPSILON = 1e-06
SIDE = 4
LOW = 2048
SKETCH_BLOCK = 8192
TILE = 1024
EXCHANGE_WAVES = 1
WAVES = 1
DISTANCES = (1, 3, 2)
VMEM = 48 * 1024 * 1024


def x_perm(move):
    return [(y * SIDE + x, y * SIDE + move(x)) for y in range(SIDE) for x in range(SIDE)]


def y_perm(move):
    return [(y * SIDE + x, move(y) * SIDE + x) for y in range(SIDE) for x in range(SIDE)]


def parity_sign(values):
    for shift_by in (16, 8, 4, 2, 1):
        values = jnp.bitwise_xor(values, jnp.right_shift(values, shift_by))
    return (1 - 2 * jnp.bitwise_and(values, 1)).astype(jnp.float32)


def sketch_kernel(first_ref, slab_ref, bits_ref, sampled_ref, out_ref, low_ref, acc_ref):
    step = pl.program_id(0)
    sampled = sampled_ref[...]

    @pl.when(step == 0)
    def _():
        acc_ref[...] = jnp.zeros_like(acc_ref)
        column = lax.broadcasted_iota(jnp.int32, (sampled.shape[0], 128), 1)
        base = parity_sign(jnp.bitwise_and(column, sampled)) * (1.0 / math.sqrt(N))
        for part in range(LOW // 128):
            sign = parity_sign(jnp.bitwise_and(sampled, part * 128))
            low_ref[:, part * 128 : (part + 1) * 128] = (base * sign).astype(jnp.bfloat16)

    total = acc_ref[...]
    for part in range(SKETCH_BLOCK // LOW):
        where = slice(part * LOW, (part + 1) * LOW)
        flip = (1 - 2 * bits_ref[:, where]).astype(jnp.bfloat16)
        signed = slab_ref[:, where] * flip
        term = lax.dot_general(
            low_ref[...], signed, (((1,), (1,)), ((), ())), preferred_element_type=jnp.float32
        )
        high = first_ref[0] + step * SKETCH_BLOCK + part * LOW
        total = total + term * parity_sign(jnp.bitwise_and(sampled, high))
    acc_ref[...] = total

    @pl.when(step == pl.num_programs(0) - 1)
    def _():
        out_ref[...] = acc_ref[...]


def local_sketch(slab, sign_bits, sampled):
    rows, cols = slab.shape
    count = sampled.shape[0]
    first = (lax.axis_index("cols") * cols).astype(jnp.int32).reshape(1)
    return pl.pallas_call(
        sketch_kernel,
        grid_spec=pltpu.PrefetchScalarGridSpec(
            num_scalar_prefetch=1,
            grid=(cols // SKETCH_BLOCK,),
            in_specs=[
                pl.BlockSpec((rows, SKETCH_BLOCK), lambda i, s: (0, i)),
                pl.BlockSpec((1, SKETCH_BLOCK), lambda i, s: (0, i)),
                pl.BlockSpec((count, 1), lambda i, s: (0, 0)),
            ],
            out_specs=pl.BlockSpec((count, rows), lambda i, s: (0, 0)),
            scratch_shapes=[
                pltpu.VMEM((count, LOW), jnp.bfloat16),
                pltpu.VMEM((count, rows), jnp.float32),
            ],
        ),
        out_shape=jax.ShapeDtypeStruct((count, rows), jnp.float32),
        compiler_params=pltpu.CompilerParams(vmem_limit_bytes=VMEM),
        cost_estimate=pl.CostEstimate(
            flops=1, bytes_accessed=1, transcendentals=0
        ),
        name="sketch",
    )(first, slab, sign_bits.reshape(1, cols), sampled.reshape(count, 1))


def assemble_kernel(where_ref, *refs):
    *pieces, out_ref = refs
    scale = 1.0 / math.sqrt(4096)
    base = 0
    for group in range(len(pieces) // SIDE):
        width = pieces[group * SIDE].shape[1]
        place = where_ref[group]
        for k, distance in enumerate((0,) + DISTANCES):
            piece = pieces[group * SIDE + k]
            source = lax.rem(place + SIDE - distance, SIDE)
            column = pl.multiple_of(base + source * width, 128)
            out_ref[:, pl.ds(column, width)] = piece[...].astype(jnp.float32) * scale
        base += SIDE * width


def held_row(row, me, count):
    share = count // 8
    apart = jnp.bitwise_xor(row // share, me)
    step = apart // 2
    slot = jnp.bitwise_xor(step, step // 2) + SIDE * (apart % 2)
    return slot * share + row % share


def product_kernel(axis, where_ref, basis_ref, p0, p1, p2, p3, own, o1, o2, o3, lhs_ref, rhs_ref):
    chunk, depth = own.shape[0], p0.shape[0]
    height = chunk // SIDE
    place = where_ref[1 - axis]

    @pl.when(pl.program_id(0) == 0)
    def _():
        for k, distance in enumerate((0,) + DISTANCES):
            target = lax.rem(place + distance, SIDE)
            for m in range(SIDE):
                row = target * chunk + m * height if axis == 0 else m * chunk + target * height
                row = held_row(row, where_ref[2], basis_ref.shape[0]) if axis else row
                rows = pl.ds(pl.multiple_of(row, height), height)
                to = slice(k * chunk + m * height, k * chunk + (m + 1) * height)
                lhs_ref[to, :] = basis_ref[rows, :]

    for k, piece in enumerate((p0, p1, p2, p3)):
        rhs_ref[k * depth : (k + 1) * depth, :] = piece[...]
    product = jnp.dot(lhs_ref[...], rhs_ref[...], preferred_element_type=jnp.float32)
    for k, out in enumerate((own, o1, o2, o3)):
        out[...] = product[k * chunk : (k + 1) * chunk, :].astype(out.dtype)


def product(axis, where, basis, slab, tile_offset, received, width):
    rows = slab.shape[0]
    count = basis.shape[0]
    chunk = count // SIDE
    block_tiles = slab.shape[1] // (2 * SIDE) // TILE
    depth = SIDE * rows
    return pl.pallas_call(
        functools.partial(product_kernel, axis),
        grid_spec=pltpu.PrefetchScalarGridSpec(
            num_scalar_prefetch=1,
            grid=(width // TILE,),
            in_specs=[
                pl.BlockSpec(basis.shape, lambda t, s: (0, 0)),
                pl.BlockSpec((rows, TILE), lambda t, s: (0, tile_offset + s[axis] * block_tiles + t)),
            ]
            + [pl.BlockSpec((rows, TILE), lambda t, s, first=first: (0, first + t)) for _, first in received],
            out_specs=[pl.BlockSpec((chunk, TILE), lambda t, s: (0, t))] * 4,
            scratch_shapes=[
                pltpu.VMEM((count, depth), jnp.bfloat16),
                pltpu.VMEM((depth, TILE), jnp.bfloat16),
            ],
        ),
        out_shape=[jax.ShapeDtypeStruct((chunk, width), jnp.float32)]
        + [jax.ShapeDtypeStruct((chunk, width), jnp.bfloat16)] * 3,
        compiler_params=pltpu.CompilerParams(vmem_limit_bytes=VMEM),
        cost_estimate=pl.CostEstimate(flops=1, bytes_accessed=1, transcendentals=0),
        name="product",
    )(where, basis, slab, *(piece for piece, _ in received))


def collect_kernel(axis, where_ref, own_ref, g1, g2, g3, *refs):
    *outs, total_ref = refs[-5:]
    total = own_ref[...]
    for got in (g1, g2, g3):
        total = total + got[...].astype(jnp.float32)
    total_ref[...] = total
    height = outs[0].shape[0]
    place = where_ref[axis]
    for out, distance in zip(outs, (0,) + DISTANCES):
        row = lax.rem(place + distance, SIDE) * height
        out[...] = total_ref[pl.ds(pl.multiple_of(row, height), height), :].astype(out.dtype)


def collect(axis, where, own, got, tile_offset, whole_width, earlier):
    chunk, width = own.shape
    height = chunk // SIDE
    return pl.pallas_call(
        functools.partial(collect_kernel, axis),
        grid_spec=pltpu.PrefetchScalarGridSpec(
            num_scalar_prefetch=1,
            grid=(width // TILE,),
            in_specs=[pl.BlockSpec((chunk, TILE), lambda t, s: (0, t))] * 4
            + [pl.BlockSpec(memory_space=pl.ANY)] * len(earlier),
            out_specs=[pl.BlockSpec((height, TILE), lambda t, s: (0, tile_offset + t))] * 4,
            scratch_shapes=[pltpu.VMEM((chunk, TILE), jnp.float32)],
        ),
        out_shape=[jax.ShapeDtypeStruct((height, whole_width), jnp.float32)]
        + [jax.ShapeDtypeStruct((height, whole_width), jnp.bfloat16)] * 3,
        input_output_aliases={5 + k: k for k in range(len(earlier))},
        compiler_params=pltpu.CompilerParams(vmem_limit_bytes=VMEM),
        cost_estimate=pl.CostEstimate(flops=1, bytes_accessed=1, transcendentals=0),
        name="collect",
    )(where, own, *got, *earlier)


PERMS = (x_perm, y_perm)


def shift(value, axis, distance):
    return lax.ppermute(value, "rows", PERMS[axis](lambda q: (q + distance) % SIDE))


def per_device(slab, sign_bits, sampled):
    rows, cols = slab.shape
    count = sampled.shape[0]
    col_devices = lax.axis_size("cols")
    row_devices = lax.axis_size("rows")
    total_rows = rows * row_devices
    share = count // col_devices
    row_index = lax.axis_index("rows")
    places = (row_index % SIDE, row_index // SIDE)
    where = jnp.stack((*places, lax.axis_index("cols"))).astype(jnp.int32)
    width = cols // (2 * SIDE)
    starts = (0, cols // 2)

    def block(source, axis, distance, first=0, size=width):
        start = starts[axis] + (places[axis] + distance) % SIDE * width + first
        return lax.dynamic_slice(source, (0, start), (rows, size))

    x_far, y_far = block(slab, 0, 2), block(slab, 1, 2)
    slab_now, x_far, y_far = lax.optimization_barrier((slab, x_far, y_far))
    x_far, y_far = shift(x_far, 0, 2), shift(y_far, 1, 2)

    partial = local_sketch(slab_now, sign_bits, sampled)
    parts = lax.all_to_all(partial, "cols", 0, 0, tiled=True)
    sketch = jnp.sum(parts.reshape(col_devices, share, rows), axis=0)

    size = width // EXCHANGE_WAVES

    def near_blocks(axis):
        return [[block(slab_now, axis, d, w * size, size) for d in (1, 3)] for w in range(EXCHANGE_WAVES)]

    def send_near(blocks, axis):
        return [[shift(part, axis, d) for part, d in zip(pair, (1, 3))] for pair in blocks]

    x_sketch = [sketch] + [shift(sketch, 0, distance) for distance in DISTANCES]
    x_near, x_sketch, x_far = lax.optimization_barrier((near_blocks(0), x_sketch, x_far))
    x_near = send_near(x_near, 0)
    x_squares = sum(jnp.sum(part * part, axis=1, keepdims=True) for part in x_sketch)
    sent = jnp.concatenate([sketch, jnp.broadcast_to(x_squares, (share, 128))], axis=1)
    y_sketch = [sent] + [shift(sent, 1, distance) for distance in DISTANCES]
    y_near, y_sketch, y_far = lax.optimization_barrier((near_blocks(1), y_sketch, y_far))
    y_near = send_near(y_near, 1)
    squares = sum(part[:, rows : rows + 1] for part in y_sketch)
    scale = lax.rsqrt(squares / total_rows + EPSILON)

    bases = []
    for sketches in (x_sketch, y_sketch):
        joined = jnp.concatenate([(part[:, :rows] * scale).astype(jnp.bfloat16) for part in sketches], axis=1)
        bases.append(joined)
    bases[0] = lax.all_to_all(jnp.tile(bases[0], (col_devices, 1)), "cols", 0, 0, tiled=True)
    for mask in (2, 6, 1):
        other = lax.ppermute(bases[1], "cols", [(k, k ^ mask) for k in range(col_devices)])
        bases[1] = jnp.concatenate([bases[1], other], axis=0)

    far, near = (x_far, y_far), (x_near, y_near)
    height = count // row_devices
    wave_width = width // WAVES
    wave_tiles = wave_width // TILE
    collected = [(), ()]
    for wave in range(WAVES):
        terms = []
        for axis in range(2):
            first = wave * wave_tiles
            if EXCHANGE_WAVES > 1:
                one, three = ((part, 0) for part in near[axis][wave])
            else:
                one, three = ((part, first) for part in near[axis][0])
            offset = starts[axis] // TILE + first
            own, *sends = product(axis, where, bases[axis], slab, offset, (one, three, (far[axis], first)), wave_width)
            order = (2, 0, 1)
            got = {k: shift(sends[k], 1 - axis, DISTANCES[k]) for k in order}
            terms.append((own, [got[k] for k in range(3)]))
        for axis in range(2):
            own, got = terms[axis]
            collected[axis] = collect(axis, where, own, got, wave * wave_tiles, width, collected[axis])
    pieces = []
    for axis in range(2):
        own, *sends = collected[axis]
        pieces += [own] + [shift(send, axis, distance) for send, distance in zip(sends, DISTANCES)]
    return pl.pallas_call(
        assemble_kernel,
        grid_spec=pltpu.PrefetchScalarGridSpec(
            num_scalar_prefetch=1,
            grid=(1,),
            in_specs=[pl.BlockSpec(piece.shape, lambda i, s: (0, 0)) for piece in pieces],
            out_specs=pl.BlockSpec((height, cols), lambda i, s: (0, 0)),
        ),
        out_shape=jax.ShapeDtypeStruct((height, cols), jnp.float32),
        compiler_params=pltpu.CompilerParams(vmem_limit_bytes=VMEM),
        name="assemble",
    )(where, *pieces)


def solution(mesh):
    return jax.shard_map(
        per_device,
        mesh=mesh,
        in_specs=(P("rows", "cols"), P("cols"), P()),
        out_specs=P("rows", "cols"),
        check_vma=False,
    )
```

time: 567 us -> 202 us (0.36)
  waiting for transfers between devices: 421 us -> 84.5 us
  starting transfers between devices: 0.04 us -> 59.1 us
  matrix products: 48.1 us -> 0 us
  other arithmetic: 43.5 us -> 1.45 us
  Pallas kernels: 0 us -> 42 us
  blocking collectives: 40.3 us -> 0 us
  local copies, waits for them, and re-layouts: 0 us -> 13.9 us
  between operations: 13.4 us -> 0.23 us
    reduce_scatter x1 -> x0, waiting for transfers between devices: 357 us -> none  [per_device(): lax.psum_scatter(lax.dot_general(basis, slab, (((0,), (0,)), ((), ())), p...]
    ppermute x0 -> x27, waiting for transfers between devices: none -> 74.2 us  [the longest x24 58.8 us: shift(): lax.ppermute(value, 'rows', PERMS[axis](lambda q: (q + distance) % SIDE))]
    psum x1 -> x0, waiting for transfers between devices: 63.5 us -> none  [per_device(): sketch = lax.psum(partial_sketch, 'cols')]
    ppermute x0 -> x27, starting transfers between devices: none -> 48.3 us  [the longest x24 44.1 us: shift(): lax.ppermute(value, 'rows', PERMS[axis](lambda q: (q + distance) % SIDE))]
    dot_general x2 -> x0, matrix products: 48.1 us -> none  [the longest x1 28.7 us: per_device(): lax.dot_general(basis, slab, (((0,), (0,)), ((), ())), preferred_element_...]
    pallas_call x0 -> x6, Pallas kernels: none -> 42 us  [the longest x2 16.9 us: product(): pl.pallas_call(functools.partial(product_kernel, axis), grid_spec=pltpu.P...]
    psum x1 -> x0, blocking collectives: 40.3 us -> none  [per_device(): squares = lax.psum(jnp.sum(sketch * sketch, axis=0), 'rows')]
    mul x3 -> x0, other arithmetic: 38.4 us -> none  [the longest x1 22.9 us: per_device(): mixing = outer_signs * column_signs[:, None]]
  transfers between devices with their start and end apart: 2 -> 29, of which waited for: 2 -> 17; matrix products, arithmetic and copies ran while one was open for 0% -> 5% of each run, Pallas kernels for 0% -> 19%
where the time goes in v2:
time: 202 us; the launch traced here: 201 us
  waiting for transfers between devices  84.5 us (42%)
  starting transfers between devices  59.1 us (29%)
  Pallas kernels  42 us (21%)
  local copies, waits for them, and re-layouts  13.9 us (7%)
    ppermute x24, waiting for transfers between devices, shift(): lax.ppermute(value, 'rows', PERMS[axis](lambda q: (q + distance) % SIDE))  58.8 us
    ppermute x24, starting transfers between devices, shift(): lax.ppermute(value, 'rows', PERMS[axis](lambda q: (q + distance) % SIDE))  44.1 us
    pallas_call x2, Pallas kernels, product(): pl.pallas_call(functools.partial(product_kernel, axis), grid_spec=pltpu.P...  16.9 us
    pallas_call x1, Pallas kernels, local_sketch(): pl.pallas_call(sketch_kernel, grid_spec=pltpu.PrefetchScalarGridSpec(num_...  15.5 us
    ppermute x3, waiting for transfers between devices, per_device(): lax.ppermute(bases[1], 'cols', [(k, k ^ mask) for k in range(col_devices)])  15.4 us
    dynamic_slice x2, local copies, waits for them, and re-layouts, block(): return lax.dynamic_slice(source, (0, start), (rows, size))  11.2 us
    all_to_all x1, waiting for transfers between devices, per_device(): parts = lax.all_to_all(partial, 'cols', 0, 0, tiled=True)  10.3 us
    pallas_call x2, Pallas kernels, collect(): pl.pallas_call(functools.partial(collect_kernel, axis), grid_spec=pltpu.P...  6.83 us
  transfers between devices with their start and end apart: 29, of which 17 were waited for; matrix products, arithmetic and copies ran while one was open for 5% of the time, Pallas kernels for 19%

profile of v2, /device:TPU:0, one launch (start us, length us, event | category | flops | bytes accessed | tf_op | source)
XLA Modules:
  0.0 201.2 jit_solution(1393877184901291436)
XLA Ops:
  0.0 4.0 %constant_dynamic-slice_fusion.4 = (bf16[256,4096]{1,0:T(8,128)(2,1)S(1)}, bf16[256,4096]{1,0:T(8,128)(2,1)}) fusion(bf16[256,32768]{1,0:T(8,128)(2,1)} %p0.3, s32[]{:T(128)S(6)} %select_n.58, s32[]{:T(128)S(6)} %select_n.56), kind=kLoop, calls=%fused_computation.23 | loop fusion | bytes 8388616 | tf_op jit(solution)/shard_map/dynamic_slice | solution.py:229
  4.0 3.1 %collective-permute-start.3 = (bf16[256,4096]{1,0:T(8,128)(2,1)}, bf16[256,4096]{1,0:T(8,128)(2,1)}, u32[]{:S(2)}, u32[]{:S(2)}) collective-permute-start(bf16[256,4096]{1,0:T(8,128)(2,1)} %get-tuple-element.39), channel_id=1, source_target_pairs={{0,16},{8,24},{16,0},{24,8},{32,48},{40,56},{48,32},{56,40},{64,80... | collective-permute-start | bytes 6291464 | tf_op jit(solution)/shard_map/ppermute | solution.py:211
  7.2 3.2 %collective-permute-start.7 = (bf16[256,4096]{1,0:T(8,128)(2,1)S(1)}, bf16[256,4096]{1,0:T(8,128)(2,1)}, u32[]{:S(2)}, u32[]{:S(2)}) collective-permute-start(bf16[256,4096]{1,0:T(8,128)(2,1)S(1)} %get-tuple-element.44), channel_id=1, source_target_pairs={{0,64},{8,72},{16,80},{24,88},{32,96},{40,104},{48,112},{56,120},{... | collective-permute-start | bytes 6291464 | tf_op jit(solution)/shard_map/ppermute | solution.py:211
  10.5 15.5 %sketch.1 = f32[512,256]{1,0:T(8,128)} custom-call(s32[1]{0:T(128)} %bitcast.3.first_ref, bf16[256,32768]{1,0:T(8,128)(2,1)} %p0.3, s32[1,32768]{1,0:T(1,128)S(1)} %bitcast.9, s32[512,1]{1,0:T(8,128)S(1)} %copy.4.sampled_ref), custom_call_target="tpu_custom_call" | custom-call | flops 1 | bytes 1 | tf_op jit(solution)/shard_map/sketch/pallas_call | solution.py:71
  26.0 5.3 %all-to-all-start = ((f32[8,64,256]{2,1,0:T(8,128)}), f32[8,64,256]{2,1,0:T(8,128)S(1)}, u32[]{:S(2)}, u32[]{:S(2)}) async-start(f32[8,64,256]{2,1,0:T(8,128)} %bitcast.6), calls=%async_computation | async-start | bytes 1048576 | tf_op jit(solution)/shard_map/all_to_all | solution.py:236
  31.3 10.3 %all-to-all-done = f32[8,64,256]{2,1,0:T(8,128)S(1)} async-done(((f32[8,64,256]{2,1,0:T(8,128)}), f32[8,64,256]{2,1,0:T(8,128)S(1)}, u32[]{:S(2)}, u32[]{:S(2)}) %all-to-all-start) | async-done | bytes 524320 | tf_op jit(solution)/shard_map/all_to_all | solution.py:236
  45.0 7.2 %constant_dynamic-slice_fusion = (bf16[256,4096]{1,0:T(8,128)(2,1)}, bf16[256,4096]{1,0:T(8,128)(2,1)}, bf16[256,4096]{1,0:T(8,128)(2,1)}, bf16[256,4096]{1,0:T(8,128)(2,1)}) fusion(bf16[256,32768]{1,0:T(8,128)(2,1)} %p0.3, s32[]{:T(128)S(6)} %select_n.66, s32[]{:T(128)S(6)} %select_n.64, s32[]{:T(128)S(6)} %select_n.62, s32[]{:T(128)S(6)} %select_n.60), kind=kLoop, calls=%fused_computation.19 | loop fusion | bytes 16777232 | tf_op jit(solution)/shard_map/dynamic_slice | solution.py:229
  52.2 2.9 %collective-permute-done = f32[64,256]{1,0:T(8,128)S(1)} collective-permute-done((f32[64,256]{1,0:T(8,128)S(1)}, f32[64,256]{1,0:T(8,128)S(1)}, u32[]{:S(2)}, u32[]{:S(2)}) %collective-permute-start) | collective-permute-done | bytes 65568 | tf_op jit(solution)/shard_map/ppermute | solution.py:211
  73.6 5.5 %all-to-all-start.1 = ((bf16[8,64,1024]{2,1,0:T(8,128)(2,1)}), bf16[8,64,1024]{2,1,0:T(8,128)(2,1)S(1)}, u32[]{:S(2)}, u32[]{:S(2)}) async-start(bf16[8,64,1024]{2,1,0:T(8,128)(2,1)} %tile.2), calls=%async_computation.1 | async-start | bytes 2097152 | tf_op jit(solution)/shard_map/all_to_all | solution.py:262
  81.1 15.2 %collective-permute-done.16 = bf16[64,1024]{1,0:T(8,128)(2,1)S(1)} collective-permute-done((bf16[64,1024]{1,0:T(8,128)(2,1)S(1)}, bf16[64,1024]{1,0:T(8,128)(2,1)S(1)}, u32[]{:S(2)}, u32[]{:S(2)}) %collective-permute-start.16) | collective-permute-done | bytes 131104 | tf_op jit(solution)/shard_map/ppermute | solution.py:264
  99.2 5.2 %collective-permute-done.8.p1 = bf16[256,4096]{1,0:T(8,128)(2,1)} collective-permute-done((bf16[256,4096]{1,0:T(8,128)(2,1)}, bf16[256,4096]{1,0:T(8,128)(2,1)}, u32[]{:S(2)}, u32[]{:S(2)}) %collective-permute-start.8) | collective-permute-done | bytes 2097184 | tf_op jit(solution)/shard_map/ppermute | solution.py:211
  104.4 8.3 %product.2 = (f32[128,4096]{1,0:T(8,128)}, bf16[128,4096]{1,0:T(8,128)(2,1)S(1)}, bf16[128,4096]{1,0:T(8,128)(2,1)S(1)}, bf16[128,4096]{1,0:T(8,128)(2,1)S(1)}) custom-call(s32[3]{0:T(128)S(1)} %pad_add_fusion.where_ref, bf16[512,1024]{1,0:T(8,128)(2,1)S(1)} %bitcast.8, bf16[256,32768]{1,0:T(8,128)(2,1)} %p0.3, bf16[256,4096]{1,0:T(8,128)(2,1)} %collective-permute-done.8.p1, ...), custom_call_target="tpu_custom_call" | custom-call | flops 1 | bytes 1 | tf_op jit(solution)/shard_map/product/pallas_call | solution.py:148
  116.5 3.0 %collective-permute-start.12 = (bf16[128,4096]{1,0:T(8,128)(2,1)S(1)}, bf16[128,4096]{1,0:T(8,128)(2,1)S(1)}, u32[]{:S(2)}, u32[]{:S(2)}) collective-permute-start(bf16[128,4096]{1,0:T(8,128)(2,1)S(1)} %get-tuple-element.55), channel_id=1, source_target_pairs={{0,64},{8,72},{16,80},{24,88},{32,96},{40,104},{48,112},{56,120},{... | collective-permute-start | bytes 3145736 | tf_op jit(solution)/shard_map/ppermute | solution.py:211
  120.9 8.5 %product.3 = (f32[128,4096]{1,0:T(8,128)}, bf16[128,4096]{1,0:T(8,128)(2,1)S(1)}, bf16[128,4096]{1,0:T(8,128)(2,1)S(1)}, bf16[128,4096]{1,0:T(8,128)(2,1)S(1)}) custom-call(s32[3]{0:T(128)S(1)} %pad_add_fusion.where_ref, bf16[512,1024]{1,0:T(8,128)(2,1)S(1)} %pad_maximum_fusion.basis_ref, bf16[256,32768]{1,0:T(8,128)(2,1)} %p0.3, ...), custom_call_target="tpu_custom_call" | custom-call | flops 1 | bytes 1 | tf_op jit(solution)/shard_map/product/pallas_call | solution.py:148
  132.7 8.2 %collective-permute-done.10.g1 = bf16[128,4096]{1,0:T(8,128)(2,1)S(1)} collective-permute-done((bf16[128,4096]{1,0:T(8,128)(2,1)S(1)}, bf16[128,4096]{1,0:T(8,128)(2,1)S(1)}, u32[]{:S(2)}, u32[]{:S(2)}) %collective-permute-start.10) | collective-permute-done | bytes 1048608 | tf_op jit(solution)/shard_map/ppermute | solution.py:211
  142.5 19.0 %collective-permute-done.12.g3 = bf16[128,4096]{1,0:T(8,128)(2,1)S(1)} collective-permute-done((bf16[128,4096]{1,0:T(8,128)(2,1)S(1)}, bf16[128,4096]{1,0:T(8,128)(2,1)S(1)}, u32[]{:S(2)}, u32[]{:S(2)}) %collective-permute-start.12) | collective-permute-done | bytes 1048608 | tf_op jit(solution)/shard_map/ppermute | solution.py:211
  161.5 3.4 %collect.2 = (f32[32,4096]{1,0:T(8,128)S(1)}, bf16[32,4096]{1,0:T(8,128)(2,1)S(1)}, bf16[32,4096]{1,0:T(8,128)(2,1)S(1)}, bf16[32,4096]{1,0:T(8,128)(2,1)S(1)}) custom-call(s32[3]{0:T(128)S(1)} %pad_add_fusion.where_ref, f32[128,4096]{1,0:T(8,128)} %get-tuple-element.52.own_ref, bf16[128,4096]{1,0:T(8,128)(2,1)S(1)} %collective-permute-done.10.g1, ...), custom_call_target="tpu_custom_call" | custom-call | flops 1 | bytes 1 | tf_op jit(solution)/shard_map/collect/pallas_call | solution.py:188
  169.1 7.1 %collective-permute-done.22.g2 = bf16[128,4096]{1,0:T(8,128)(2,1)S(1)} collective-permute-done((bf16[128,4096]{1,0:T(8,128)(2,1)S(1)}, bf16[128,4096]{1,0:T(8,128)(2,1)S(1)}, u32[]{:S(2)}, u32[]{:S(2)}) %collective-permute-start.22) | collective-permute-done | bytes 1048608 | tf_op jit(solution)/shard_map/ppermute | solution.py:211
  176.1 4.2 %collective-permute-done.23.g3 = bf16[128,4096]{1,0:T(8,128)(2,1)S(1)} collective-permute-done((bf16[128,4096]{1,0:T(8,128)(2,1)S(1)}, bf16[128,4096]{1,0:T(8,128)(2,1)S(1)}, u32[]{:S(2)}, u32[]{:S(2)}) %collective-permute-start.23) | collective-permute-done | bytes 1048608 | tf_op jit(solution)/shard_map/ppermute | solution.py:211
  180.4 3.4 %collect.3 = (f32[32,4096]{1,0:T(8,128)S(1)}, bf16[32,4096]{1,0:T(8,128)(2,1)S(1)}, bf16[32,4096]{1,0:T(8,128)(2,1)S(1)}, bf16[32,4096]{1,0:T(8,128)(2,1)S(1)}) custom-call(s32[3]{0:T(128)S(1)} %pad_add_fusion.where_ref, f32[128,4096]{1,0:T(8,128)} %get-tuple-element.63.own_ref, bf16[128,4096]{1,0:T(8,128)(2,1)S(1)} %collective-permute-done.21.g1, ...), custom_call_target="tpu_custom_call" | custom-call | flops 1 | bytes 1 | tf_op jit(solution)/shard_map/collect/pallas_call | solution.py:188
  183.9 3.2 %collective-permute-start.25 = (bf16[32,4096]{1,0:T(8,128)(2,1)S(1)}, bf16[32,4096]{1,0:T(8,128)(2,1)S(1)}, u32[]{:S(2)}, u32[]{:S(2)}) collective-permute-start(bf16[32,4096]{1,0:T(8,128)(2,1)S(1)} %get-tuple-element.69), channel_id=1, source_target_pairs={{0,96},{8,104},{16,112},{24,120},{32,0},{40,8},{48,16},{56,24},{64... | collective-permute-start | bytes 786440 | tf_op jit(solution)/shard_map/ppermute | solution.py:211
  187.1 3.8 %collective-permute-start.26 = (bf16[32,4096]{1,0:T(8,128)(2,1)S(1)}, bf16[32,4096]{1,0:T(8,128)(2,1)S(1)}, u32[]{:S(2)}, u32[]{:S(2)}) collective-permute-start(bf16[32,4096]{1,0:T(8,128)(2,1)S(1)} %get-tuple-element.70), channel_id=1, source_target_pairs={{0,64},{8,72},{16,80},{24,88},{32,96},{40,104},{48,112},{56,120},{... | collective-permute-start | bytes 786440 | tf_op jit(solution)/shard_map/ppermute | solution.py:211
  194.2 4.2 %collective-permute-done.26.refs_7_ = bf16[32,4096]{1,0:T(8,128)(2,1)S(1)} collective-permute-done((bf16[32,4096]{1,0:T(8,128)(2,1)S(1)}, bf16[32,4096]{1,0:T(8,128)(2,1)S(1)}, u32[]{:S(2)}, u32[]{:S(2)}) %collective-permute-start.26) | collective-permute-done | bytes 262176 | tf_op jit(solution)/shard_map/ppermute | solution.py:211
  198.4 2.8 %assemble.1 = f32[32,32768]{1,0:T(8,128)} custom-call(s32[3]{0:T(128)S(1)} %pad_add_fusion.where_ref, f32[32,4096]{1,0:T(8,128)S(1)} %get-tuple-element.56.refs_0_, bf16[32,4096]{1,0:T(8,128)(2,1)S(1)} %collective-permute-done.13.refs_1_, bf16[32,4096]{1,0:T(8,128)(2,1)S(1)} %collective-permute-done.14.refs_2_, ...), custom_call_target="tpu_custom_call" | custom-call | tf_op jit(solution)/shard_map/assemble/pallas_call | solution.py:292
  (80 shorter events, 44.3 us)
Async XLA Ops:
  4.0 51.8 %collective-permute-start.3 = (bf16[256,4096]{1,0:T(8,128)(2,1)}, bf16[256,4096]{1,0:T(8,128)(2,1)}, u32[]{:S(2)}, u32[]{:S(2)}) collective-permute-start(bf16[256,4096]{1,0:T(8,128)(2,1)} %get-tuple-element.39), channel_id=1, source_target_pairs={{0,16},{8,24},{16,0},{24,8},{32,48},{40,56},{48,32},{56,40},{64,80... | collective-permute-start | bytes 6291464 | tf_op jit(solution)/shard_map/ppermute | solution.py:211
  7.2 55.7 %collective-permute-start.7 = (bf16[256,4096]{1,0:T(8,128)(2,1)S(1)}, bf16[256,4096]{1,0:T(8,128)(2,1)}, u32[]{:S(2)}, u32[]{:S(2)}) collective-permute-start(bf16[256,4096]{1,0:T(8,128)(2,1)S(1)} %get-tuple-element.44), channel_id=1, source_target_pairs={{0,64},{8,72},{16,80},{24,88},{32,96},{40,104},{48,112},{56,120},{... | collective-permute-start | bytes 6291464 | tf_op jit(solution)/shard_map/ppermute | solution.py:211
  26.0 15.7 %all-to-all-start = ((f32[8,64,256]{2,1,0:T(8,128)}), f32[8,64,256]{2,1,0:T(8,128)S(1)}, u32[]{:S(2)}, u32[]{:S(2)}) async-start(f32[8,64,256]{2,1,0:T(8,128)} %bitcast.6), calls=%async_computation | async-start | bytes 1048576 | tf_op jit(solution)/shard_map/all_to_all | solution.py:236
  41.7 13.4 %collective-permute-start = (f32[64,256]{1,0:T(8,128)S(1)}, f32[64,256]{1,0:T(8,128)S(1)}, u32[]{:S(2)}, u32[]{:S(2)}) collective-permute-start(f32[64,256]{1,0:T(8,128)S(1)} %reduce_sum.45), channel_id=1, source_target_pairs={{0,8},{8,16},{16,24},{24,0},{32,40},{40,48},{48,56},{56,32},{64,72... | collective-permute-start | bytes 196616 | tf_op jit(solution)/shard_map/ppermute | solution.py:211
  42.3 13.1 %collective-permute-start.1 = (f32[64,256]{1,0:T(8,128)S(1)}, f32[64,256]{1,0:T(8,128)S(1)}, u32[]{:S(2)}, u32[]{:S(2)}) collective-permute-start(f32[64,256]{1,0:T(8,128)S(1)} %reduce_sum.45), channel_id=1, source_target_pairs={{0,24},{8,0},{16,8},{24,16},{32,56},{40,32},{48,40},{56,48},{64,88... | collective-permute-start | bytes 196616 | tf_op jit(solution)/shard_map/ppermute | solution.py:211
  45.0 10.9 %collective-permute-start.2 = (f32[64,256]{1,0:T(8,128)S(1)}, f32[64,256]{1,0:T(8,128)S(1)}, u32[]{:S(2)}, u32[]{:S(2)}) collective-permute-start(f32[64,256]{1,0:T(8,128)S(1)} %reduce_sum.45), channel_id=1, source_target_pairs={{0,16},{8,24},{16,0},{24,8},{32,48},{40,56},{48,32},{56,40},{64,80... | collective-permute-start | bytes 196616 | tf_op jit(solution)/shard_map/ppermute | solution.py:211
  55.8 48.5 %collective-permute-start.8 = (bf16[256,4096]{1,0:T(8,128)(2,1)}, bf16[256,4096]{1,0:T(8,128)(2,1)}, u32[]{:S(2)}, u32[]{:S(2)}) collective-permute-start(bf16[256,4096]{1,0:T(8,128)(2,1)} %get-tuple-element.49), channel_id=1, source_target_pairs={{0,8},{8,16},{16,24},{24,0},{32,40},{40,48},{48,56},{56,32},{64,72... | collective-permute-start | bytes 6291464 | tf_op jit(solution)/shard_map/ppermute | solution.py:211
  57.6 46.8 %collective-permute-start.9 = (bf16[256,4096]{1,0:T(8,128)(2,1)}, bf16[256,4096]{1,0:T(8,128)(2,1)}, u32[]{:S(2)}, u32[]{:S(2)}) collective-permute-start(bf16[256,4096]{1,0:T(8,128)(2,1)} %get-tuple-element.50), channel_id=1, source_target_pairs={{0,24},{8,0},{16,8},{24,16},{32,56},{40,32},{48,40},{56,48},{64,88... | collective-permute-start | bytes 6291464 | tf_op jit(solution)/shard_map/ppermute | solution.py:211
  68.9 50.6 %collective-permute-start.19 = (bf16[256,4096]{1,0:T(8,128)(2,1)}, bf16[256,4096]{1,0:T(8,128)(2,1)S(1)}, u32[]{:S(2)}, u32[]{:S(2)}) collective-permute-start(bf16[256,4096]{1,0:T(8,128)(2,1)} %get-tuple-element.60), channel_id=1, source_target_pairs={{0,32},{8,40},{16,48},{24,56},{32,64},{40,72},{48,80},{56,88},{64,... | collective-permute-start | bytes 6291464 | tf_op jit(solution)/shard_map/ppermute | solution.py:211
  69.4 50.2 %collective-permute-start.20 = (bf16[256,4096]{1,0:T(8,128)(2,1)}, bf16[256,4096]{1,0:T(8,128)(2,1)}, u32[]{:S(2)}, u32[]{:S(2)}) collective-permute-start(bf16[256,4096]{1,0:T(8,128)(2,1)} %get-tuple-element.61), channel_id=1, source_target_pairs={{0,96},{8,104},{16,112},{24,120},{32,0},{40,8},{48,16},{56,24},{64... | collective-permute-start | bytes 6291464 | tf_op jit(solution)/shard_map/ppermute | solution.py:211
  73.6 25.6 %all-to-all-start.1 = ((bf16[8,64,1024]{2,1,0:T(8,128)(2,1)}), bf16[8,64,1024]{2,1,0:T(8,128)(2,1)S(1)}, u32[]{:S(2)}, u32[]{:S(2)}) async-start(bf16[8,64,1024]{2,1,0:T(8,128)(2,1)} %tile.2), calls=%async_computation.1 | async-start | bytes 2097152 | tf_op jit(solution)/shard_map/all_to_all | solution.py:262
  79.0 17.3 %collective-permute-start.16 = (bf16[64,1024]{1,0:T(8,128)(2,1)S(1)}, bf16[64,1024]{1,0:T(8,128)(2,1)S(1)}, u32[]{:S(2)}, u32[]{:S(2)}) collective-permute-start(bf16[64,1024]{1,0:T(8,128)(2,1)S(1)} %pad_maximum_fusion.4), channel_id=1, source_target_pairs={{0,2},{1,3},{2,0},{3,1},{4,6},{5,7},{6,4},{7,5},{8,10},{9,11},{10,... | collective-permute-start | bytes 393224 | tf_op jit(solution)/shard_map/ppermute | solution.py:264
  97.0 17.4 %collective-permute-start.17 = (bf16[128,1024]{1,0:T(8,128)(2,1)}, bf16[128,1024]{1,0:T(8,128)(2,1)S(1)}, u32[]{:S(2)}, u32[]{:S(2)}) collective-permute-start(bf16[128,1024]{1,0:T(8,128)(2,1)} %pad_maximum_fusion.2), channel_id=1, source_target_pairs={{0,6},{1,7},{2,4},{3,5},{4,2},{5,3},{6,0},{7,1},{8,14},{9,15},{10,... | collective-permute-start | bytes 786440 | tf_op jit(solution)/shard_map/ppermute | solution.py:264
  112.8 28.1 %collective-permute-start.10 = (bf16[128,4096]{1,0:T(8,128)(2,1)S(1)}, bf16[128,4096]{1,0:T(8,128)(2,1)S(1)}, u32[]{:S(2)}, u32[]{:S(2)}) collective-permute-start(bf16[128,4096]{1,0:T(8,128)(2,1)S(1)} %get-tuple-element.53), channel_id=1, source_target_pairs={{0,32},{8,40},{16,48},{24,56},{32,64},{40,72},{48,80},{56,88},{64,... | collective-permute-start | bytes 3145736 | tf_op jit(solution)/shard_map/ppermute | solution.py:211
  114.6 27.9 %collective-permute-start.11 = (bf16[128,4096]{1,0:T(8,128)(2,1)S(1)}, bf16[128,4096]{1,0:T(8,128)(2,1)S(1)}, u32[]{:S(2)}, u32[]{:S(2)}) collective-permute-start(bf16[128,4096]{1,0:T(8,128)(2,1)S(1)} %get-tuple-element.54), channel_id=1, source_target_pairs={{0,96},{8,104},{16,112},{24,120},{32,0},{40,8},{48,16},{56,24},{64... | collective-permute-start | bytes 3145736 | tf_op jit(solution)/shard_map/ppermute | solution.py:211
  116.5 45.0 %collective-permute-start.12 = (bf16[128,4096]{1,0:T(8,128)(2,1)S(1)}, bf16[128,4096]{1,0:T(8,128)(2,1)S(1)}, u32[]{:S(2)}, u32[]{:S(2)}) collective-permute-start(bf16[128,4096]{1,0:T(8,128)(2,1)S(1)} %get-tuple-element.55), channel_id=1, source_target_pairs={{0,64},{8,72},{16,80},{24,88},{32,96},{40,104},{48,112},{56,120},{... | collective-permute-start | bytes 3145736 | tf_op jit(solution)/shard_map/ppermute | solution.py:211
  129.4 38.8 %collective-permute-start.21 = (bf16[128,4096]{1,0:T(8,128)(2,1)S(1)}, bf16[128,4096]{1,0:T(8,128)(2,1)S(1)}, u32[]{:S(2)}, u32[]{:S(2)}) collective-permute-start(bf16[128,4096]{1,0:T(8,128)(2,1)S(1)} %get-tuple-element.64), channel_id=1, source_target_pairs={{0,8},{8,16},{16,24},{24,0},{32,40},{40,48},{48,56},{56,32},{64,72... | collective-permute-start | bytes 3145736 | tf_op jit(solution)/shard_map/ppermute | solution.py:211
  130.8 45.3 %collective-permute-start.22 = (bf16[128,4096]{1,0:T(8,128)(2,1)S(1)}, bf16[128,4096]{1,0:T(8,128)(2,1)S(1)}, u32[]{:S(2)}, u32[]{:S(2)}) collective-permute-start(bf16[128,4096]{1,0:T(8,128)(2,1)S(1)} %get-tuple-element.65), channel_id=1, source_target_pairs={{0,24},{8,0},{16,8},{24,16},{32,56},{40,32},{48,40},{56,48},{64,88... | collective-permute-start | bytes 3145736 | tf_op jit(solution)/shard_map/ppermute | solution.py:211
  140.8 39.5 %collective-permute-start.23 = (bf16[128,4096]{1,0:T(8,128)(2,1)S(1)}, bf16[128,4096]{1,0:T(8,128)(2,1)S(1)}, u32[]{:S(2)}, u32[]{:S(2)}) collective-permute-start(bf16[128,4096]{1,0:T(8,128)(2,1)S(1)} %get-tuple-element.66), channel_id=1, source_target_pairs={{0,16},{8,24},{16,0},{24,8},{32,48},{40,56},{48,32},{56,40},{64,80... | collective-permute-start | bytes 3145736 | tf_op jit(solution)/shard_map/ppermute | solution.py:211
  164.9 22.2 %collective-permute-start.13 = (bf16[32,4096]{1,0:T(8,128)(2,1)S(1)}, bf16[32,4096]{1,0:T(8,128)(2,1)S(1)}, u32[]{:S(2)}, u32[]{:S(2)}) collective-permute-start(bf16[32,4096]{1,0:T(8,128)(2,1)S(1)} %get-tuple-element.57), channel_id=1, source_target_pairs={{0,8},{8,16},{16,24},{24,0},{32,40},{40,48},{48,56},{56,32},{64,72... | collective-permute-start | bytes 786440 | tf_op jit(solution)/shard_map/ppermute | solution.py:211
  166.0 25.0 %collective-permute-start.14 = (bf16[32,4096]{1,0:T(8,128)(2,1)S(1)}, bf16[32,4096]{1,0:T(8,128)(2,1)S(1)}, u32[]{:S(2)}, u32[]{:S(2)}) collective-permute-start(bf16[32,4096]{1,0:T(8,128)(2,1)S(1)} %get-tuple-element.58), channel_id=1, source_target_pairs={{0,24},{8,0},{16,8},{24,16},{32,56},{40,32},{48,40},{56,48},{64,88... | collective-permute-start | bytes 786440 | tf_op jit(solution)/shard_map/ppermute | solution.py:211
  168.2 22.8 %collective-permute-start.15 = (bf16[32,4096]{1,0:T(8,128)(2,1)S(1)}, bf16[32,4096]{1,0:T(8,128)(2,1)S(1)}, u32[]{:S(2)}, u32[]{:S(2)}) collective-permute-start(bf16[32,4096]{1,0:T(8,128)(2,1)S(1)} %get-tuple-element.59), channel_id=1, source_target_pairs={{0,16},{8,24},{16,0},{24,8},{32,48},{40,56},{48,32},{56,40},{64,80... | collective-permute-start | bytes 786440 | tf_op jit(solution)/shard_map/ppermute | solution.py:211
  183.9 10.3 %collective-permute-start.25 = (bf16[32,4096]{1,0:T(8,128)(2,1)S(1)}, bf16[32,4096]{1,0:T(8,128)(2,1)S(1)}, u32[]{:S(2)}, u32[]{:S(2)}) collective-permute-start(bf16[32,4096]{1,0:T(8,128)(2,1)S(1)} %get-tuple-element.69), channel_id=1, source_target_pairs={{0,96},{8,104},{16,112},{24,120},{32,0},{40,8},{48,16},{56,24},{64... | collective-permute-start | bytes 786440 | tf_op jit(solution)/shard_map/ppermute | solution.py:211
  187.1 11.2 %collective-permute-start.26 = (bf16[32,4096]{1,0:T(8,128)(2,1)S(1)}, bf16[32,4096]{1,0:T(8,128)(2,1)S(1)}, u32[]{:S(2)}, u32[]{:S(2)}) collective-permute-start(bf16[32,4096]{1,0:T(8,128)(2,1)S(1)} %get-tuple-element.70), channel_id=1, source_target_pairs={{0,64},{8,72},{16,80},{24,88},{32,96},{40,104},{48,112},{56,120},{... | collective-permute-start | bytes 786440 | tf_op jit(solution)/shard_map/ppermute | solution.py:211
  (16 other events, 186.8 us)

commit v3 on v2

v3 whole, which is shorter than its diff:
```python
import functools
import math

import jax
import jax.numpy as jnp
from jax import lax
from jax.experimental import pallas as pl
from jax.experimental.pallas import tpu as pltpu
from jax.sharding import PartitionSpec as P

N = 262144
EPSILON = 1e-06
SIDE = 4
LOW = 2048
SKETCH_BLOCK = 8192
TILE = 1024
DISTANCES = (1, 3, 2)
VMEM = 48 * 1024 * 1024


def x_perm(move):
    return [(y * SIDE + x, y * SIDE + move(x)) for y in range(SIDE) for x in range(SIDE)]


def y_perm(move):
    return [(y * SIDE + x, move(y) * SIDE + x) for y in range(SIDE) for x in range(SIDE)]


def parity_sign(values):
    for shift_by in (16, 8, 4, 2, 1):
        values = jnp.bitwise_xor(values, jnp.right_shift(values, shift_by))
    return (1 - 2 * jnp.bitwise_and(values, 1)).astype(jnp.float32)


def sketch_kernel(first_ref, slab_ref, bits_ref, sampled_ref, out_ref, low_ref, acc_ref):
    step = pl.program_id(0)
    sampled = sampled_ref[...]

    @pl.when(step == 0)
    def _():
        acc_ref[...] = jnp.zeros_like(acc_ref)
        column = lax.broadcasted_iota(jnp.int32, (sampled.shape[0], 128), 1)
        base = parity_sign(jnp.bitwise_and(column, sampled)) * (1.0 / math.sqrt(N))
        for part in range(LOW // 128):
            sign = parity_sign(jnp.bitwise_and(sampled, part * 128))
            low_ref[:, part * 128 : (part + 1) * 128] = (base * sign).astype(jnp.bfloat16)

    total = acc_ref[...]
    for part in range(SKETCH_BLOCK // LOW):
        where = slice(part * LOW, (part + 1) * LOW)
        flip = (1 - 2 * bits_ref[:, where]).astype(jnp.bfloat16)
        signed = slab_ref[:, where] * flip
        term = lax.dot_general(
            low_ref[...], signed, (((1,), (1,)), ((), ())), preferred_element_type=jnp.float32
        )
        high = first_ref[0] + step * SKETCH_BLOCK + part * LOW
        total = total + term * parity_sign(jnp.bitwise_and(sampled, high))
    acc_ref[...] = total

    @pl.when(step == pl.num_programs(0) - 1)
    def _():
        out_ref[...] = acc_ref[...]


def local_sketch(slab, sign_bits, sampled):
    rows, cols = slab.shape
    count = sampled.shape[0]
    first = (lax.axis_index("cols") * cols).astype(jnp.int32).reshape(1)
    return pl.pallas_call(
        sketch_kernel,
        grid_spec=pltpu.PrefetchScalarGridSpec(
            num_scalar_prefetch=1,
            grid=(cols // SKETCH_BLOCK,),
            in_specs=[
                pl.BlockSpec((rows, SKETCH_BLOCK), lambda i, s: (0, i)),
                pl.BlockSpec((1, SKETCH_BLOCK), lambda i, s: (0, i)),
                pl.BlockSpec((count, 1), lambda i, s: (0, 0)),
            ],
            out_specs=pl.BlockSpec((count, rows), lambda i, s: (0, 0)),
            scratch_shapes=[
                pltpu.VMEM((count, LOW), jnp.bfloat16),
                pltpu.VMEM((count, rows), jnp.float32),
            ],
        ),
        out_shape=jax.ShapeDtypeStruct((count, rows), jnp.float32),
        compiler_params=pltpu.CompilerParams(vmem_limit_bytes=VMEM),
        cost_estimate=pl.CostEstimate(
            flops=1, bytes_accessed=1, transcendentals=0
        ),
        name="sketch",
    )(first, slab, sign_bits.reshape(1, cols), sampled.reshape(count, 1))


def assemble_kernel(axis, where_ref, own, g1, g2, g3, one, three, far, *refs):
    out_ref = refs[-1]
    scale = 1.0 / math.sqrt(4096)
    width = own.shape[1]
    total = own[...]
    for got in (g1, g2, g3):
        total = total + got[...].astype(jnp.float32)
    pieces = (total, one[...], three[...], far[...])
    for piece, distance in zip(pieces, (0,) + DISTANCES):
        source = lax.rem(where_ref[axis] + SIDE - distance, SIDE)
        column = pl.multiple_of(source * width, width)
        out_ref[:, pl.ds(column, width)] = piece.astype(jnp.float32) * scale


def assemble(axis, where, own, got, pieces, earlier):
    height, width = pieces[0].shape
    return pl.pallas_call(
        functools.partial(assemble_kernel, axis),
        grid_spec=pltpu.PrefetchScalarGridSpec(
            num_scalar_prefetch=1,
            grid=(1,),
            in_specs=[pl.BlockSpec((height, width), lambda i, s: (SIDE - 1, 0))] * SIDE
            + [pl.BlockSpec((height, width), lambda i, s: (0, 0))] * 3
            + [pl.BlockSpec(memory_space=pl.ANY)] * len(earlier),
            out_specs=pl.BlockSpec((height, SIDE * width), lambda i, s: (0, axis)),
        ),
        out_shape=jax.ShapeDtypeStruct((height, 2 * SIDE * width), jnp.float32),
        input_output_aliases={8 + k: k for k in range(len(earlier))},
        compiler_params=pltpu.CompilerParams(vmem_limit_bytes=VMEM),
        cost_estimate=pl.CostEstimate(flops=1, bytes_accessed=1, transcendentals=0),
        name="assemble",
    )(where, own, *got, *pieces, *earlier)


def held_row(row, me, count):
    share = count // 8
    apart = jnp.bitwise_xor(row // share, me)
    step = apart // 2
    slot = jnp.bitwise_xor(step, step // 2) + SIDE * (apart % 2)
    return slot * share + row % share


def product_kernel(axis, distances, where_ref, basis_ref, p0, p1, p2, p3, *refs):
    *outs, lhs_ref, rhs_ref = refs
    chunk, depth = outs[0].shape[0], p0.shape[0]
    height = chunk // SIDE
    place = where_ref[1 - axis]

    @pl.when(pl.program_id(0) == 0)
    def _():
        for k, distance in enumerate(distances):
            target = lax.rem(place + distance, SIDE)
            for m, step in enumerate(DISTANCES + (0,)):
                other = lax.rem(where_ref[axis] + step, SIDE)
                row = target * chunk + other * height if axis == 0 else other * chunk + target * height
                row = held_row(row, where_ref[2], basis_ref.shape[0]) if axis else row
                rows = pl.ds(pl.multiple_of(row, height), height)
                to = slice(k * chunk + m * height, k * chunk + (m + 1) * height)
                lhs_ref[to, :] = basis_ref[rows, :]

    for k, piece in enumerate((p0, p1, p2, p3)):
        rhs_ref[k * depth : (k + 1) * depth, :] = piece[...]
    product = jnp.dot(lhs_ref[...], rhs_ref[...], preferred_element_type=jnp.float32)
    for k, out in enumerate(outs):
        out[...] = product[k * chunk : (k + 1) * chunk, :].astype(out.dtype)


def product(axis, distances, where, basis, slab, received):
    rows, width = received[0].shape
    count = basis.shape[0]
    chunk = count // SIDE
    tiles = width // TILE
    depth = SIDE * rows
    height = chunk * len(distances)
    return pl.pallas_call(
        functools.partial(product_kernel, axis, distances),
        grid_spec=pltpu.PrefetchScalarGridSpec(
            num_scalar_prefetch=1,
            grid=(tiles,),
            in_specs=[
                pl.BlockSpec(basis.shape, lambda t, s: (0, 0)),
                pl.BlockSpec((rows, TILE), lambda t, s: (0, (axis * SIDE + s[axis]) * tiles + t)),
            ]
            + [pl.BlockSpec((rows, TILE), lambda t, s: (0, t))] * 3,
            out_specs=[pl.BlockSpec((chunk, TILE), lambda t, s: (0, t))] * len(distances),
            scratch_shapes=[
                pltpu.VMEM((height, depth), jnp.bfloat16),
                pltpu.VMEM((depth, TILE), jnp.bfloat16),
            ],
        ),
        out_shape=[
            jax.ShapeDtypeStruct((chunk, width), jnp.bfloat16 if distance else jnp.float32) for distance in distances
        ],
        compiler_params=pltpu.CompilerParams(vmem_limit_bytes=VMEM),
        cost_estimate=pl.CostEstimate(flops=1, bytes_accessed=1, transcendentals=0),
        name="product",
    )(where, basis, slab, *received)


def collect_kernel(own_ref, g1, g2, g3, *outs):
    total = own_ref[...]
    for got in (g1, g2, g3):
        total = total + got[...].astype(jnp.float32)
    height = outs[0].shape[0]
    for k, out in enumerate(outs):
        out[...] = total[k * height : (k + 1) * height, :].astype(out.dtype)


def collect(own, got, first, blocks):
    chunk, width = own.shape
    height = chunk // SIDE
    rows = height * blocks
    return pl.pallas_call(
        collect_kernel,
        grid=(width // TILE,),
        in_specs=[pl.BlockSpec((rows, TILE), lambda t: (first // blocks, t))] * 4,
        out_specs=[pl.BlockSpec((height, TILE), lambda t: (0, t))] * blocks,
        out_shape=[jax.ShapeDtypeStruct((height, width), jnp.bfloat16)] * blocks,
        compiler_params=pltpu.CompilerParams(vmem_limit_bytes=VMEM),
        cost_estimate=pl.CostEstimate(flops=1, bytes_accessed=1, transcendentals=0),
        name="collect",
    )(own, *got)


PERMS = (x_perm, y_perm)


def shift(value, axis, distance):
    return lax.ppermute(value, "rows", PERMS[axis](lambda q: (q + distance) % SIDE))


def per_device(slab, sign_bits, sampled):
    rows, cols = slab.shape
    count = sampled.shape[0]
    col_devices = lax.axis_size("cols")
    row_devices = lax.axis_size("rows")
    total_rows = rows * row_devices
    share = count // col_devices
    row_index = lax.axis_index("rows")
    places = (row_index % SIDE, row_index // SIDE)
    where = jnp.stack((*places, lax.axis_index("cols"))).astype(jnp.int32)
    width = cols // (2 * SIDE)
    starts = (0, cols // 2)

    def block(source, axis, distance, first=0, size=width):
        start = starts[axis] + (places[axis] + distance) % SIDE * width + first
        return lax.dynamic_slice(source, (0, start), (rows, size))

    slab_x, x_far = lax.optimization_barrier((slab, block(slab, 0, 2)))
    x_far = shift(x_far, 0, 2)
    slab_now, y_far = lax.optimization_barrier((slab_x, block(slab_x, 1, 2)))
    y_far = shift(y_far, 1, 2)

    partial = local_sketch(slab_now, sign_bits, sampled)
    parts = lax.all_to_all(partial, "cols", 0, 0, tiled=True)
    sketch = jnp.sum(parts.reshape(col_devices, share, rows), axis=0)

    def near_blocks(axis):
        return [block(slab_now, axis, distance) for distance in (1, 3)]

    def send_near(blocks, axis):
        return [shift(part, axis, distance) for part, distance in zip(blocks, (1, 3))]

    x_sketch = [sketch] + [shift(sketch, 0, distance) for distance in DISTANCES]
    x_near, x_sketch, x_far = lax.optimization_barrier((near_blocks(0), x_sketch, x_far))
    x_near = send_near(x_near, 0)
    x_squares = sum(jnp.sum(part * part, axis=1, keepdims=True) for part in x_sketch)
    sent = jnp.concatenate([sketch, jnp.broadcast_to(x_squares, (share, 128))], axis=1)
    y_sketch = [sent] + [shift(sent, 1, distance) for distance in DISTANCES]
    y_near, y_sketch, y_far = lax.optimization_barrier((near_blocks(1), y_sketch, y_far))
    y_near = send_near(y_near, 1)
    squares = sum(part[:, rows : rows + 1] for part in y_sketch)
    scale = lax.rsqrt(squares / total_rows + EPSILON)

    bases = []
    for sketches in (x_sketch, y_sketch):
        joined = jnp.concatenate([(part[:, :rows] * scale).astype(jnp.bfloat16) for part in sketches], axis=1)
        bases.append(joined)
    bases[0] = lax.all_to_all(jnp.tile(bases[0], (col_devices, 1)), "cols", 0, 0, tiled=True)
    for mask in (2, 6, 1):
        other = lax.ppermute(bases[1], "cols", [(k, k ^ mask) for k in range(col_devices)])
        bases[1] = jnp.concatenate([bases[1], other], axis=0)

    x_received, y_received = (*x_near, x_far), (*y_near, y_far)
    terms = [
        product(axis, (0,) + DISTANCES, where, bases[axis], slab, received)
        for axis, received in enumerate((x_received, y_received))
    ]
    out = ()
    for axis in range(2):
        own, *sends = terms[axis]
        got = [shift(send, 1 - axis, distance) for send, distance in zip(sends, DISTANCES)]
        (far,) = collect(own, got, 2, 1)
        far = shift(far, axis, 2)
        near = collect(own, got, 0, 2)
        near = [shift(part, axis, distance) for part, distance in zip(near, (1, 3))]
        out = (assemble(axis, where, own, got, (*near, far), out),)
    return out[0]


def solution(mesh):
    return jax.shard_map(
        per_device,
        mesh=mesh,
        in_specs=(P("rows", "cols"), P("cols"), P()),
        out_specs=P("rows", "cols"),
        check_vma=False,
    )
```

time: 202 us -> 195 us (0.965)
  waiting for transfers between devices: 84.5 us -> 78.3 us
  Pallas kernels: 42 us -> 38.6 us
  starting transfers between devices: 59.1 us -> 61.7 us
    ppermute x24, waiting for transfers between devices: 58.8 us -> 52.7 us  [shift(): lax.ppermute(value, 'rows', PERMS[axis](lambda q: (q + distance) % SIDE))]
    pallas_call x5 -> x8, Pallas kernels: 26.5 us -> 23.2 us  [the longest x2 17.2 us: product(): pl.pallas_call(functools.partial(product_kernel, axis, distances), grid_s...]
    ppermute x24, starting transfers between devices: 44.1 us -> 46.7 us  [shift(): lax.ppermute(value, 'rows', PERMS[axis](lambda q: (q + distance) % SIDE))]
    dynamic_slice x2 -> x3, local copies, waits for them, and re-layouts: 11.2 us -> 12.8 us  [block(): return lax.dynamic_slice(source, (0, start), (rows, size))]
  transfers between devices with their start and end apart: 29 -> 29, of which waited for: 17 -> 16; matrix products, arithmetic and copies ran while one was open for 5% -> 6% of each run, Pallas kernels for 19% -> 19%
where the time goes in v3:
time: 195 us
  waiting for transfers between devices  78.3 us (40%)
  starting transfers between devices  61.7 us (32%)
  Pallas kernels  38.6 us (20%)
  local copies, waits for them, and re-layouts  14.2 us (7%)
    ppermute x24, waiting for transfers between devices, shift(): lax.ppermute(value, 'rows', PERMS[axis](lambda q: (q + distance) % SIDE))  52.7 us
    ppermute x24, starting transfers between devices, shift(): lax.ppermute(value, 'rows', PERMS[axis](lambda q: (q + distance) % SIDE))  46.7 us
    pallas_call x2, Pallas kernels, product(): pl.pallas_call(functools.partial(product_kernel, axis, distances), grid_s...  17.2 us
    pallas_call x1, Pallas kernels, local_sketch(): pl.pallas_call(sketch_kernel, grid_spec=pltpu.PrefetchScalarGridSpec(num_...  15.5 us
    ppermute x3, waiting for transfers between devices, per_device(): lax.ppermute(bases[1], 'cols', [(k, k ^ mask) for k in range(col_devices)])  15.3 us
    dynamic_slice x3, local copies, waits for them, and re-layouts, block(): return lax.dynamic_slice(source, (0, start), (rows, size))  12.8 us
    all_to_all x1, waiting for transfers between devices, per_device(): parts = lax.all_to_all(partial, 'cols', 0, 0, tiled=True)  10.3 us
    all_to_all x1, starting transfers between devices, per_device(): lax.all_to_all(jnp.tile(bases[0], (col_devices, 1)), 'cols', 0, 0, tiled=...  5.45 us
  transfers between devices with their start and end apart: 29, of which 16 were waited for; matrix products, arithmetic and copies ran while one was open for 6% of the time, Pallas kernels for 19%

profile of v3, /device:TPU:0, one launch (start us, length us, event | category | flops | bytes accessed | tf_op | source)
XLA Modules:
  0.0 194.6 jit_solution(15567047816732069391)
XLA Ops:
  0.0 3.2 %constant_dynamic-slice_fusion.5 = bf16[256,4096]{1,0:T(8,128)(2,1)} fusion(bf16[256,32768]{1,0:T(8,128)(2,1)} %p0.3, s32[]{:T(128)S(6)} %select_n.56), kind=kLoop, calls=%fused_computation.24 | loop fusion | bytes 4194308 | tf_op jit(solution)/shard_map/dynamic_slice | solution.py:240
  3.2 3.1 %collective-permute-start.3 = (bf16[256,4096]{1,0:T(8,128)(2,1)}, bf16[256,4096]{1,0:T(8,128)(2,1)}, u32[]{:S(2)}, u32[]{:S(2)}) collective-permute-start(bf16[256,4096]{1,0:T(8,128)(2,1)} %constant_dynamic-slice_fusion.5), channel_id=1, source_target_pairs={{0,16},{8,24},{16,0},{24,8},{32,48},{40,56},{48,32},{56,40},{64,80... | collective-permute-start | bytes 6291464 | tf_op jit(solution)/shard_map/ppermute | solution.py:222
  6.3 3.2 %constant_dynamic-slice_fusion.4 = bf16[256,4096]{1,0:T(8,128)(2,1)} fusion(bf16[256,32768]{1,0:T(8,128)(2,1)} %p0.3, s32[]{:T(128)S(6)} %select_n.58), kind=kLoop, calls=%fused_computation.23 | loop fusion | bytes 4194308 | tf_op jit(solution)/shard_map/dynamic_slice | solution.py:240
  9.5 3.2 %collective-permute-start.7 = (bf16[256,4096]{1,0:T(8,128)(2,1)}, bf16[256,4096]{1,0:T(8,128)(2,1)}, u32[]{:S(2)}, u32[]{:S(2)}) collective-permute-start(bf16[256,4096]{1,0:T(8,128)(2,1)} %constant_dynamic-slice_fusion.4), channel_id=1, source_target_pairs={{0,64},{8,72},{16,80},{24,88},{32,96},{40,104},{48,112},{56,120},{... | collective-permute-start | bytes 6291464 | tf_op jit(solution)/shard_map/ppermute | solution.py:222
  12.9 15.5 %sketch.1 = f32[512,256]{1,0:T(8,128)} custom-call(s32[1]{0:T(128)} %bitcast.3.first_ref, bf16[256,32768]{1,0:T(8,128)(2,1)} %p0.3, s32[1,32768]{1,0:T(1,128)S(1)} %bitcast.9, s32[512,1]{1,0:T(8,128)S(1)} %copy.5.sampled_ref), custom_call_target="tpu_custom_call" | custom-call | flops 1 | bytes 1 | tf_op jit(solution)/shard_map/sketch/pallas_call | solution.py:69
  28.4 5.3 %all-to-all-start = ((f32[8,64,256]{2,1,0:T(8,128)}), f32[8,64,256]{2,1,0:T(8,128)S(1)}, u32[]{:S(2)}, u32[]{:S(2)}) async-start(f32[8,64,256]{2,1,0:T(8,128)} %bitcast.6), calls=%async_computation | async-start | bytes 1048576 | tf_op jit(solution)/shard_map/all_to_all | solution.py:248
  33.6 10.3 %all-to-all-done = f32[8,64,256]{2,1,0:T(8,128)S(1)} async-done(((f32[8,64,256]{2,1,0:T(8,128)}), f32[8,64,256]{2,1,0:T(8,128)S(1)}, u32[]{:S(2)}, u32[]{:S(2)}) %all-to-all-start) | async-done | bytes 524320 | tf_op jit(solution)/shard_map/all_to_all | solution.py:248
  44.7 2.6 %collective-permute-start.1 = (f32[64,256]{1,0:T(8,128)S(1)}, f32[64,256]{1,0:T(8,128)S(1)}, u32[]{:S(2)}, u32[]{:S(2)}) collective-permute-start(f32[64,256]{1,0:T(8,128)S(1)} %reduce_sum.45), channel_id=1, source_target_pairs={{0,24},{8,0},{16,8},{24,16},{32,56},{40,32},{48,40},{56,48},{64,88... | collective-permute-start | bytes 196616 | tf_op jit(solution)/shard_map/ppermute | solution.py:222
  47.3 6.4 %constant_dynamic-slice_fusion = (bf16[256,4096]{1,0:T(8,128)(2,1)}, bf16[256,4096]{1,0:T(8,128)(2,1)}, bf16[256,4096]{1,0:T(8,128)(2,1)S(1)}, bf16[256,4096]{1,0:T(8,128)(2,1)}) fusion(bf16[256,32768]{1,0:T(8,128)(2,1)} %p0.3, s32[]{:T(128)S(6)} %select_n.66, s32[]{:T(128)S(6)} %select_n.64, s32[]{:T(128)S(6)} %select_n.62, s32[]{:T(128)S(6)} %select_n.60), kind=kLoop, calls=%fused_computation.19 | loop fusion | bytes 16777232 | tf_op jit(solution)/shard_map/dynamic_slice | solution.py:240
  65.7 2.3 %collective-permute-done.6 = f32[64,384]{1,0:T(8,128)S(1)} collective-permute-done((f32[64,384]{1,0:T(8,128)S(1)}, f32[64,384]{1,0:T(8,128)S(1)}, u32[]{:S(2)}, u32[]{:S(2)}) %collective-permute-start.6) | collective-permute-done | bytes 98336 | tf_op jit(solution)/shard_map/ppermute | solution.py:222
  68.6 2.7 %collective-permute-start.12 = (bf16[256,4096]{1,0:T(8,128)(2,1)S(1)}, bf16[256,4096]{1,0:T(8,128)(2,1)}, u32[]{:S(2)}, u32[]{:S(2)}) collective-permute-start(bf16[256,4096]{1,0:T(8,128)(2,1)S(1)} %get-tuple-element.48), channel_id=1, source_target_pairs={{0,96},{8,104},{16,112},{24,120},{32,0},{40,8},{48,16},{56,24},{64... | collective-permute-start | bytes 6291464 | tf_op jit(solution)/shard_map/ppermute | solution.py:222
  72.7 5.5 %all-to-all-start.1 = ((bf16[8,64,1024]{2,1,0:T(8,128)(2,1)}), bf16[8,64,1024]{2,1,0:T(8,128)(2,1)S(1)}, u32[]{:S(2)}, u32[]{:S(2)}) async-start(bf16[8,64,1024]{2,1,0:T(8,128)(2,1)} %tile.2), calls=%async_computation.1 | async-start | bytes 2097152 | tf_op jit(solution)/shard_map/all_to_all | solution.py:272
  80.3 15.2 %collective-permute-done.8 = bf16[64,1024]{1,0:T(8,128)(2,1)S(1)} collective-permute-done((bf16[64,1024]{1,0:T(8,128)(2,1)S(1)}, bf16[64,1024]{1,0:T(8,128)(2,1)S(1)}, u32[]{:S(2)}, u32[]{:S(2)}) %collective-permute-start.8) | collective-permute-done | bytes 131104 | tf_op jit(solution)/shard_map/ppermute | solution.py:274
  98.3 5.2 %collective-permute-done.19.p1 = bf16[256,4096]{1,0:T(8,128)(2,1)} collective-permute-done((bf16[256,4096]{1,0:T(8,128)(2,1)}, bf16[256,4096]{1,0:T(8,128)(2,1)}, u32[]{:S(2)}, u32[]{:S(2)}) %collective-permute-start.19) | collective-permute-done | bytes 2097184 | tf_op jit(solution)/shard_map/ppermute | solution.py:222
  103.6 8.4 %product.3 = (f32[128,4096]{1,0:T(8,128)}, bf16[128,4096]{1,0:T(8,128)(2,1)S(1)}, bf16[128,4096]{1,0:T(8,128)(2,1)S(1)}, bf16[128,4096]{1,0:T(8,128)(2,1)S(1)}) custom-call(s32[3]{0:T(128)S(1)} %pad_add_fusion.where_ref, bf16[512,1024]{1,0:T(8,128)(2,1)S(1)} %bitcast.8, bf16[256,32768]{1,0:T(8,128)(2,1)} %p0.3, ...), custom_call_target="tpu_custom_call" | custom-call | flops 1 | bytes 1 | tf_op jit(solution)/shard_map/product/pallas_call | solution.py:168
  115.7 3.0 %collective-permute-start.23 = (bf16[128,4096]{1,0:T(8,128)(2,1)S(1)}, bf16[128,4096]{1,0:T(8,128)(2,1)S(1)}, u32[]{:S(2)}, u32[]{:S(2)}) collective-permute-start(bf16[128,4096]{1,0:T(8,128)(2,1)S(1)} %get-tuple-element.62), channel_id=1, source_target_pairs={{0,64},{8,72},{16,80},{24,88},{32,96},{40,104},{48,112},{56,120},{... | collective-permute-start | bytes 3145736 | tf_op jit(solution)/shard_map/ppermute | solution.py:222
  118.8 8.9 %product.2 = (f32[128,4096]{1,0:T(8,128)}, bf16[128,4096]{1,0:T(8,128)(2,1)}, bf16[128,4096]{1,0:T(8,128)(2,1)S(1)}, bf16[128,4096]{1,0:T(8,128)(2,1)S(1)}) custom-call(s32[3]{0:T(128)S(1)} %pad_add_fusion.where_ref, bf16[512,1024]{1,0:T(8,128)(2,1)S(1)} %pad_maximum_fusion.basis_ref, bf16[256,32768]{1,0:T(8,128)(2,1)} %p0.3, ...), custom_call_target="tpu_custom_call" | custom-call | flops 1 | bytes 1 | tf_op jit(solution)/shard_map/product/pallas_call | solution.py:168
  130.9 9.0 %collective-permute-done.21.g1 = bf16[128,4096]{1,0:T(8,128)(2,1)S(1)} collective-permute-done((bf16[128,4096]{1,0:T(8,128)(2,1)S(1)}, bf16[128,4096]{1,0:T(8,128)(2,1)S(1)}, u32[]{:S(2)}, u32[]{:S(2)}) %collective-permute-start.21) | collective-permute-done | bytes 1048608 | tf_op jit(solution)/shard_map/ppermute | solution.py:222
  141.6 19.0 %collective-permute-done.23.g3 = bf16[128,4096]{1,0:T(8,128)(2,1)S(1)} collective-permute-done((bf16[128,4096]{1,0:T(8,128)(2,1)S(1)}, bf16[128,4096]{1,0:T(8,128)(2,1)S(1)}, u32[]{:S(2)}, u32[]{:S(2)}) %collective-permute-start.23) | collective-permute-done | bytes 1048608 | tf_op jit(solution)/shard_map/ppermute | solution.py:222
  161.0 3.2 %collective-permute-start.26 = (bf16[32,4096]{1,0:T(8,128)(2,1)S(1)}, bf16[32,4096]{1,0:T(8,128)(2,1)S(1)}, u32[]{:S(2)}, u32[]{:S(2)}) collective-permute-start(bf16[32,4096]{1,0:T(8,128)(2,1)S(1)} %collect.7), channel_id=1, source_target_pairs={{0,16},{8,24},{16,0},{24,8},{32,48},{40,56},{48,32},{56,40},{64,80... | collective-permute-start | bytes 786440 | tf_op jit(solution)/shard_map/ppermute | solution.py:222
  165.2 2.9 %collective-permute-start.25 = (bf16[32,4096]{1,0:T(8,128)(2,1)S(1)}, bf16[32,4096]{1,0:T(8,128)(2,1)S(1)}, u32[]{:S(2)}, u32[]{:S(2)}) collective-permute-start(bf16[32,4096]{1,0:T(8,128)(2,1)S(1)} %get-tuple-element.64), channel_id=1, source_target_pairs={{0,24},{8,0},{16,8},{24,16},{32,56},{40,32},{48,40},{56,48},{64,88... | collective-permute-start | bytes 786440 | tf_op jit(solution)/shard_map/ppermute | solution.py:222
  168.1 11.8 %collective-permute-done.14.g2 = bf16[128,4096]{1,0:T(8,128)(2,1)S(1)} collective-permute-done((bf16[128,4096]{1,0:T(8,128)(2,1)S(1)}, bf16[128,4096]{1,0:T(8,128)(2,1)S(1)}, u32[]{:S(2)}, u32[]{:S(2)}) %collective-permute-start.14) | collective-permute-done | bytes 1048608 | tf_op jit(solution)/shard_map/ppermute | solution.py:222
  180.2 4.1 %collective-permute-start.18 = (bf16[32,4096]{1,0:T(8,128)(2,1)S(1)}, bf16[32,4096]{1,0:T(8,128)(2,1)S(1)}, u32[]{:S(2)}, u32[]{:S(2)}) collective-permute-start(bf16[32,4096]{1,0:T(8,128)(2,1)S(1)} %collect.5), channel_id=1, source_target_pairs={{0,64},{8,72},{16,80},{24,88},{32,96},{40,104},{48,112},{56,120},{... | collective-permute-start | bytes 786440 | tf_op jit(solution)/shard_map/ppermute | solution.py:222
  184.9 3.2 %collective-permute-start.17 = (bf16[32,4096]{1,0:T(8,128)(2,1)S(1)}, bf16[32,4096]{1,0:T(8,128)(2,1)S(1)}, u32[]{:S(2)}, u32[]{:S(2)}) collective-permute-start(bf16[32,4096]{1,0:T(8,128)(2,1)S(1)} %get-tuple-element.55), channel_id=1, source_target_pairs={{0,96},{8,104},{16,112},{24,120},{32,0},{40,8},{48,16},{56,24},{64... | collective-permute-start | bytes 786440 | tf_op jit(solution)/shard_map/ppermute | solution.py:222
  (86 shorter events, 37.2 us)
Async XLA Ops:
  3.2 51.8 %collective-permute-start.3 = (bf16[256,4096]{1,0:T(8,128)(2,1)}, bf16[256,4096]{1,0:T(8,128)(2,1)}, u32[]{:S(2)}, u32[]{:S(2)}) collective-permute-start(bf16[256,4096]{1,0:T(8,128)(2,1)} %constant_dynamic-slice_fusion.5), channel_id=1, source_target_pairs={{0,16},{8,24},{16,0},{24,8},{32,48},{40,56},{48,32},{56,40},{64,80... | collective-permute-start | bytes 6291464 | tf_op jit(solution)/shard_map/ppermute | solution.py:222
  9.5 52.4 %collective-permute-start.7 = (bf16[256,4096]{1,0:T(8,128)(2,1)}, bf16[256,4096]{1,0:T(8,128)(2,1)}, u32[]{:S(2)}, u32[]{:S(2)}) collective-permute-start(bf16[256,4096]{1,0:T(8,128)(2,1)} %constant_dynamic-slice_fusion.4), channel_id=1, source_target_pairs={{0,64},{8,72},{16,80},{24,88},{32,96},{40,104},{48,112},{56,120},{... | collective-permute-start | bytes 6291464 | tf_op jit(solution)/shard_map/ppermute | solution.py:222
  28.4 15.6 %all-to-all-start = ((f32[8,64,256]{2,1,0:T(8,128)}), f32[8,64,256]{2,1,0:T(8,128)S(1)}, u32[]{:S(2)}, u32[]{:S(2)}) async-start(f32[8,64,256]{2,1,0:T(8,128)} %bitcast.6), calls=%async_computation | async-start | bytes 1048576 | tf_op jit(solution)/shard_map/all_to_all | solution.py:248
  44.0 10.2 %collective-permute-start = (f32[64,256]{1,0:T(8,128)S(1)}, f32[64,256]{1,0:T(8,128)S(1)}, u32[]{:S(2)}, u32[]{:S(2)}) collective-permute-start(f32[64,256]{1,0:T(8,128)S(1)} %reduce_sum.45), channel_id=1, source_target_pairs={{0,8},{8,16},{16,24},{24,0},{32,40},{40,48},{48,56},{56,32},{64,72... | collective-permute-start | bytes 196616 | tf_op jit(solution)/shard_map/ppermute | solution.py:222
  44.7 9.9 %collective-permute-start.1 = (f32[64,256]{1,0:T(8,128)S(1)}, f32[64,256]{1,0:T(8,128)S(1)}, u32[]{:S(2)}, u32[]{:S(2)}) collective-permute-start(f32[64,256]{1,0:T(8,128)S(1)} %reduce_sum.45), channel_id=1, source_target_pairs={{0,24},{8,0},{16,8},{24,16},{32,56},{40,32},{48,40},{56,48},{64,88... | collective-permute-start | bytes 196616 | tf_op jit(solution)/shard_map/ppermute | solution.py:222
  47.3 7.6 %collective-permute-start.2 = (f32[64,256]{1,0:T(8,128)S(1)}, f32[64,256]{1,0:T(8,128)S(1)}, u32[]{:S(2)}, u32[]{:S(2)}) collective-permute-start(f32[64,256]{1,0:T(8,128)S(1)} %reduce_sum.45), channel_id=1, source_target_pairs={{0,16},{8,24},{16,0},{24,8},{32,48},{40,56},{48,32},{56,40},{64,80... | collective-permute-start | bytes 196616 | tf_op jit(solution)/shard_map/ppermute | solution.py:222
  55.0 48.5 %collective-permute-start.19 = (bf16[256,4096]{1,0:T(8,128)(2,1)}, bf16[256,4096]{1,0:T(8,128)(2,1)}, u32[]{:S(2)}, u32[]{:S(2)}) collective-permute-start(bf16[256,4096]{1,0:T(8,128)(2,1)} %get-tuple-element.56), channel_id=1, source_target_pairs={{0,8},{8,16},{16,24},{24,0},{32,40},{40,48},{48,56},{56,32},{64,72... | collective-permute-start | bytes 6291464 | tf_op jit(solution)/shard_map/ppermute | solution.py:222
  56.7 47.0 %collective-permute-start.20 = (bf16[256,4096]{1,0:T(8,128)(2,1)}, bf16[256,4096]{1,0:T(8,128)(2,1)}, u32[]{:S(2)}, u32[]{:S(2)}) collective-permute-start(bf16[256,4096]{1,0:T(8,128)(2,1)} %get-tuple-element.57), channel_id=1, source_target_pairs={{0,24},{8,0},{16,8},{24,16},{32,56},{40,32},{48,40},{56,48},{64,88... | collective-permute-start | bytes 6291464 | tf_op jit(solution)/shard_map/ppermute | solution.py:222
  68.1 50.7 %collective-permute-start.11 = (bf16[256,4096]{1,0:T(8,128)(2,1)}, bf16[256,4096]{1,0:T(8,128)(2,1)}, u32[]{:S(2)}, u32[]{:S(2)}) collective-permute-start(bf16[256,4096]{1,0:T(8,128)(2,1)} %get-tuple-element.47), channel_id=1, source_target_pairs={{0,32},{8,40},{16,48},{24,56},{32,64},{40,72},{48,80},{56,88},{64,... | collective-permute-start | bytes 6291464 | tf_op jit(solution)/shard_map/ppermute | solution.py:222
  68.6 50.2 %collective-permute-start.12 = (bf16[256,4096]{1,0:T(8,128)(2,1)S(1)}, bf16[256,4096]{1,0:T(8,128)(2,1)}, u32[]{:S(2)}, u32[]{:S(2)}) collective-permute-start(bf16[256,4096]{1,0:T(8,128)(2,1)S(1)} %get-tuple-element.48), channel_id=1, source_target_pairs={{0,96},{8,104},{16,112},{24,120},{32,0},{40,8},{48,16},{56,24},{64... | collective-permute-start | bytes 6291464 | tf_op jit(solution)/shard_map/ppermute | solution.py:222
  72.7 25.6 %all-to-all-start.1 = ((bf16[8,64,1024]{2,1,0:T(8,128)(2,1)}), bf16[8,64,1024]{2,1,0:T(8,128)(2,1)S(1)}, u32[]{:S(2)}, u32[]{:S(2)}) async-start(bf16[8,64,1024]{2,1,0:T(8,128)(2,1)} %tile.2), calls=%async_computation.1 | async-start | bytes 2097152 | tf_op jit(solution)/shard_map/all_to_all | solution.py:272
  78.2 17.3 %collective-permute-start.8 = (bf16[64,1024]{1,0:T(8,128)(2,1)S(1)}, bf16[64,1024]{1,0:T(8,128)(2,1)S(1)}, u32[]{:S(2)}, u32[]{:S(2)}) collective-permute-start(bf16[64,1024]{1,0:T(8,128)(2,1)S(1)} %pad_maximum_fusion.3), channel_id=1, source_target_pairs={{0,2},{1,3},{2,0},{3,1},{4,6},{5,7},{6,4},{7,5},{8,10},{9,11},{10,... | collective-permute-start | bytes 393224 | tf_op jit(solution)/shard_map/ppermute | solution.py:274
  96.2 17.4 %collective-permute-start.9 = (bf16[128,1024]{1,0:T(8,128)(2,1)}, bf16[128,1024]{1,0:T(8,128)(2,1)S(1)}, u32[]{:S(2)}, u32[]{:S(2)}) collective-permute-start(bf16[128,1024]{1,0:T(8,128)(2,1)} %pad_maximum_fusion.2), channel_id=1, source_target_pairs={{0,6},{1,7},{2,4},{3,5},{4,2},{5,3},{6,0},{7,1},{8,14},{9,15},{10,... | collective-permute-start | bytes 786440 | tf_op jit(solution)/shard_map/ppermute | solution.py:274
  112.0 27.9 %collective-permute-start.21 = (bf16[128,4096]{1,0:T(8,128)(2,1)S(1)}, bf16[128,4096]{1,0:T(8,128)(2,1)S(1)}, u32[]{:S(2)}, u32[]{:S(2)}) collective-permute-start(bf16[128,4096]{1,0:T(8,128)(2,1)S(1)} %get-tuple-element.60), channel_id=1, source_target_pairs={{0,32},{8,40},{16,48},{24,56},{32,64},{40,72},{48,80},{56,88},{64,... | collective-permute-start | bytes 3145736 | tf_op jit(solution)/shard_map/ppermute | solution.py:222
  113.8 27.8 %collective-permute-start.22 = (bf16[128,4096]{1,0:T(8,128)(2,1)S(1)}, bf16[128,4096]{1,0:T(8,128)(2,1)S(1)}, u32[]{:S(2)}, u32[]{:S(2)}) collective-permute-start(bf16[128,4096]{1,0:T(8,128)(2,1)S(1)} %get-tuple-element.61), channel_id=1, source_target_pairs={{0,96},{8,104},{16,112},{24,120},{32,0},{40,8},{48,16},{56,24},{64... | collective-permute-start | bytes 3145736 | tf_op jit(solution)/shard_map/ppermute | solution.py:222
  115.7 45.0 %collective-permute-start.23 = (bf16[128,4096]{1,0:T(8,128)(2,1)S(1)}, bf16[128,4096]{1,0:T(8,128)(2,1)S(1)}, u32[]{:S(2)}, u32[]{:S(2)}) collective-permute-start(bf16[128,4096]{1,0:T(8,128)(2,1)S(1)} %get-tuple-element.62), channel_id=1, source_target_pairs={{0,64},{8,72},{16,80},{24,88},{32,96},{40,104},{48,112},{56,120},{... | collective-permute-start | bytes 3145736 | tf_op jit(solution)/shard_map/ppermute | solution.py:222
  127.6 37.6 %collective-permute-start.13 = (bf16[128,4096]{1,0:T(8,128)(2,1)}, bf16[128,4096]{1,0:T(8,128)(2,1)S(1)}, u32[]{:S(2)}, u32[]{:S(2)}) collective-permute-start(bf16[128,4096]{1,0:T(8,128)(2,1)} %get-tuple-element.51), channel_id=1, source_target_pairs={{0,8},{8,16},{16,24},{24,0},{32,40},{40,48},{48,56},{56,32},{64,72... | collective-permute-start | bytes 3145736 | tf_op jit(solution)/shard_map/ppermute | solution.py:222
  129.1 50.7 %collective-permute-start.14 = (bf16[128,4096]{1,0:T(8,128)(2,1)S(1)}, bf16[128,4096]{1,0:T(8,128)(2,1)S(1)}, u32[]{:S(2)}, u32[]{:S(2)}) collective-permute-start(bf16[128,4096]{1,0:T(8,128)(2,1)S(1)} %get-tuple-element.52), channel_id=1, source_target_pairs={{0,24},{8,0},{16,8},{24,16},{32,56},{40,32},{48,40},{56,48},{64,88... | collective-permute-start | bytes 3145736 | tf_op jit(solution)/shard_map/ppermute | solution.py:222
  139.9 40.0 %collective-permute-start.15 = (bf16[128,4096]{1,0:T(8,128)(2,1)S(1)}, bf16[128,4096]{1,0:T(8,128)(2,1)S(1)}, u32[]{:S(2)}, u32[]{:S(2)}) collective-permute-start(bf16[128,4096]{1,0:T(8,128)(2,1)S(1)} %get-tuple-element.53), channel_id=1, source_target_pairs={{0,16},{8,24},{16,0},{24,8},{32,48},{40,56},{48,32},{56,40},{64,80... | collective-permute-start | bytes 3145736 | tf_op jit(solution)/shard_map/ppermute | solution.py:222
  161.0 23.9 %collective-permute-start.26 = (bf16[32,4096]{1,0:T(8,128)(2,1)S(1)}, bf16[32,4096]{1,0:T(8,128)(2,1)S(1)}, u32[]{:S(2)}, u32[]{:S(2)}) collective-permute-start(bf16[32,4096]{1,0:T(8,128)(2,1)S(1)} %collect.7), channel_id=1, source_target_pairs={{0,16},{8,24},{16,0},{24,8},{32,48},{40,56},{48,32},{56,40},{64,80... | collective-permute-start | bytes 786440 | tf_op jit(solution)/shard_map/ppermute | solution.py:222
  164.8 24.1 %collective-permute-start.24 = (bf16[32,4096]{1,0:T(8,128)(2,1)S(1)}, bf16[32,4096]{1,0:T(8,128)(2,1)S(1)}, u32[]{:S(2)}, u32[]{:S(2)}) collective-permute-start(bf16[32,4096]{1,0:T(8,128)(2,1)S(1)} %get-tuple-element.63), channel_id=1, source_target_pairs={{0,8},{8,16},{16,24},{24,0},{32,40},{40,48},{48,56},{56,32},{64,72... | collective-permute-start | bytes 786440 | tf_op jit(solution)/shard_map/ppermute | solution.py:222
  165.2 23.6 %collective-permute-start.25 = (bf16[32,4096]{1,0:T(8,128)(2,1)S(1)}, bf16[32,4096]{1,0:T(8,128)(2,1)S(1)}, u32[]{:S(2)}, u32[]{:S(2)}) collective-permute-start(bf16[32,4096]{1,0:T(8,128)(2,1)S(1)} %get-tuple-element.64), channel_id=1, source_target_pairs={{0,24},{8,0},{16,8},{24,16},{32,56},{40,32},{48,40},{56,48},{64,88... | collective-permute-start | bytes 786440 | tf_op jit(solution)/shard_map/ppermute | solution.py:222
  180.2 10.7 %collective-permute-start.18 = (bf16[32,4096]{1,0:T(8,128)(2,1)S(1)}, bf16[32,4096]{1,0:T(8,128)(2,1)S(1)}, u32[]{:S(2)}, u32[]{:S(2)}) collective-permute-start(bf16[32,4096]{1,0:T(8,128)(2,1)S(1)} %collect.5), channel_id=1, source_target_pairs={{0,64},{8,72},{16,80},{24,88},{32,96},{40,104},{48,112},{56,120},{... | collective-permute-start | bytes 786440 | tf_op jit(solution)/shard_map/ppermute | solution.py:222
  184.8 7.7 %collective-permute-start.16 = (bf16[32,4096]{1,0:T(8,128)(2,1)S(1)}, bf16[32,4096]{1,0:T(8,128)(2,1)S(1)}, u32[]{:S(2)}, u32[]{:S(2)}) collective-permute-start(bf16[32,4096]{1,0:T(8,128)(2,1)S(1)} %get-tuple-element.54), channel_id=1, source_target_pairs={{0,32},{8,40},{16,48},{24,56},{32,64},{40,72},{48,80},{56,88},{64,... | collective-permute-start | bytes 786440 | tf_op jit(solution)/shard_map/ppermute | solution.py:222
  (17 other events, 236.2 us)

commit v4 on v3

--- a/solution.py
+++ b/solution.py
@@ -239,8 +239,9 @@
         start = starts[axis] + (places[axis] + distance) % SIDE * width + first
         return lax.dynamic_slice(source, (0, start), (rows, size))
 
-    slab_x, x_far = lax.optimization_barrier((slab, block(slab, 0, 2)))
-    x_far = shift(x_far, 0, 2)
+    slab_first, x_first = lax.optimization_barrier((slab, block(slab, 0, 2, 0, TILE)))
+    slab_x, x_rest = lax.optimization_barrier((slab_first, block(slab_first, 0, 2, TILE, width - TILE)))
+    x_far = [shift(x_first, 0, 2), shift(x_rest, 0, 2)]
     slab_now, y_far = lax.optimization_barrier((slab_x, block(slab_x, 1, 2)))
     y_far = shift(y_far, 1, 2)
 
@@ -269,6 +270,7 @@
     for sketches in (x_sketch, y_sketch):
         joined = jnp.concatenate([(part[:, :rows] * scale).astype(jnp.bfloat16) for part in sketches], axis=1)
         bases.append(joined)
+    x_far, bases[0] = lax.optimization_barrier((jnp.concatenate(x_far, axis=1), bases[0]))
     bases[0] = lax.all_to_all(jnp.tile(bases[0], (col_devices, 1)), "cols", 0, 0, tiled=True)
     for mask in (2, 6, 1):
         other = lax.ppermute(bases[1], "cols", [(k, k ^ mask) for k in range(col_devices)])

time: 195 us -> 217 us (1.11)
  starting transfers between devices: 61.7 us -> 74.7 us
  waiting for transfers between devices: 78.3 us -> 82.3 us
  other arithmetic: 1.45 us -> 4.36 us
    ppermute x24 -> x25, starting transfers between devices: 46.7 us -> 60.7 us  [shift(): lax.ppermute(value, 'rows', PERMS[axis](lambda q: (q + distance) % SIDE))]
    ppermute x24 -> x25, waiting for transfers between devices: 52.7 us -> 60 us  [shift(): lax.ppermute(value, 'rows', PERMS[axis](lambda q: (q + distance) % SIDE))]
    all_to_all x1, waiting for transfers between devices: 10.3 us -> 7.16 us  [per_device(): parts = lax.all_to_all(partial, 'cols', 0, 0, tiled=True)]
    concatenate x0 -> x1, other arithmetic: none -> 2.92 us  [per_device(): jnp.concatenate(x_far, axis=1)]
    dynamic_slice x3 -> x4, local copies, waits for them, and re-layouts: 12.8 us -> 14.2 us  [block(): return lax.dynamic_slice(source, (0, start), (rows, size))]
  transfers between devices with their start and end apart: 29 -> 30, of which waited for: 16 -> 12; matrix products, arithmetic and copies ran while one was open for 6% -> 7% of each run, Pallas kernels for 19% -> 17%
where the time goes in v4:
time: 217 us; the launch traced here: 216 us
  waiting for transfers between devices  82.3 us (38%)
  starting transfers between devices  74.7 us (34%)
  Pallas kernels  38.6 us (18%)
  local copies, waits for them, and re-layouts  15.6 us (7%)
  other arithmetic  4.36 us (2%)
    ppermute x25, starting transfers between devices, shift(): lax.ppermute(value, 'rows', PERMS[axis](lambda q: (q + distance) % SIDE))  60.7 us
    ppermute x25, waiting for transfers between devices, shift(): lax.ppermute(value, 'rows', PERMS[axis](lambda q: (q + distance) % SIDE))  60 us
    pallas_call x2, Pallas kernels, product(): pl.pallas_call(functools.partial(product_kernel, axis, distances), grid_s...  17.2 us
    pallas_call x1, Pallas kernels, local_sketch(): pl.pallas_call(sketch_kernel, grid_spec=pltpu.PrefetchScalarGridSpec(num_...  15.5 us
    ppermute x3, waiting for transfers between devices, per_device(): lax.ppermute(bases[1], 'cols', [(k, k ^ mask) for k in range(col_devices)])  15.2 us
    dynamic_slice x4, local copies, waits for them, and re-layouts, block(): return lax.dynamic_slice(source, (0, start), (rows, size))  14.2 us
    all_to_all x1, waiting for transfers between devices, per_device(): parts = lax.all_to_all(partial, 'cols', 0, 0, tiled=True)  7.16 us
    all_to_all x1, starting transfers between devices, per_device(): parts = lax.all_to_all(partial, 'cols', 0, 0, tiled=True)  5.32 us
  transfers between devices with their start and end apart: 30, of which 12 were waited for; matrix products, arithmetic and copies ran while one was open for 7% of the time, Pallas kernels for 17%

profile of v4, /device:TPU:0, one launch (start us, length us, event | category | flops | bytes accessed | tf_op | source)
XLA Modules:
  0.0 215.8 jit_solution(16418547072115542922)
XLA Ops:
  4.6 3.1 %collective-permute-start.4 = (bf16[256,3072]{1,0:T(8,128)(2,1)}, bf16[256,3072]{1,0:T(8,128)(2,1)}, u32[]{:S(2)}, u32[]{:S(2)}) collective-permute-start(bf16[256,3072]{1,0:T(8,128)(2,1)} %constant_dynamic-slice_fusion.5), channel_id=1, source_target_pairs={{0,16},{8,24},{16,0},{24,8},{32,48},{40,56},{48,32},{56,40},{64,80... | collective-permute-start | bytes 4718600 | tf_op jit(solution)/shard_map/ppermute | solution.py:222
  7.7 3.2 %constant_dynamic-slice_fusion.4 = bf16[256,4096]{1,0:T(8,128)(2,1)} fusion(bf16[256,32768]{1,0:T(8,128)(2,1)} %p0.3, s32[]{:T(128)S(6)} %select_n.64), kind=kLoop, calls=%fused_computation.24 | loop fusion | bytes 4194308 | tf_op jit(solution)/shard_map/dynamic_slice | solution.py:240
  11.1 15.5 %sketch.1 = f32[512,256]{1,0:T(8,128)} custom-call(s32[1]{0:T(128)} %bitcast.3.first_ref, bf16[256,32768]{1,0:T(8,128)(2,1)} %p0.3, s32[1,32768]{1,0:T(1,128)S(1)} %bitcast.9, s32[512,1]{1,0:T(8,128)S(1)} %copy.5.sampled_ref), custom_call_target="tpu_custom_call" | custom-call | flops 1 | bytes 1 | tf_op jit(solution)/shard_map/sketch/pallas_call | solution.py:69
  26.5 5.3 %all-to-all-start = ((f32[8,64,256]{2,1,0:T(8,128)}), f32[8,64,256]{2,1,0:T(8,128)S(1)}, u32[]{:S(2)}, u32[]{:S(2)}) async-start(f32[8,64,256]{2,1,0:T(8,128)} %bitcast.6), calls=%async_computation | async-start | bytes 1048576 | tf_op jit(solution)/shard_map/all_to_all | solution.py:249
  31.8 3.2 %collective-permute-start.8 = (bf16[256,4096]{1,0:T(8,128)(2,1)}, bf16[256,4096]{1,0:T(8,128)(2,1)}, u32[]{:S(2)}, u32[]{:S(2)}) collective-permute-start(bf16[256,4096]{1,0:T(8,128)(2,1)} %constant_dynamic-slice_fusion.4), channel_id=1, source_target_pairs={{0,64},{8,72},{16,80},{24,88},{32,96},{40,104},{48,112},{56,120},{... | collective-permute-start | bytes 6291464 | tf_op jit(solution)/shard_map/ppermute | solution.py:222
  35.0 7.2 %all-to-all-done = f32[8,64,256]{2,1,0:T(8,128)S(1)} async-done(((f32[8,64,256]{2,1,0:T(8,128)}), f32[8,64,256]{2,1,0:T(8,128)S(1)}, u32[]{:S(2)}, u32[]{:S(2)}) %all-to-all-start) | async-done | bytes 524320 | tf_op jit(solution)/shard_map/all_to_all | solution.py:249
  45.7 13.9 %collective-permute-done = f32[64,256]{1,0:T(8,128)S(1)} collective-permute-done((f32[64,256]{1,0:T(8,128)S(1)}, f32[64,256]{1,0:T(8,128)S(1)}, u32[]{:S(2)}, u32[]{:S(2)}) %collective-permute-start) | collective-permute-done | bytes 65568 | tf_op jit(solution)/shard_map/ppermute | solution.py:222
  59.5 6.4 %constant_dynamic-slice_fusion = (bf16[256,4096]{1,0:T(8,128)(2,1)}, bf16[256,4096]{1,0:T(8,128)(2,1)}, bf16[256,4096]{1,0:T(8,128)(2,1)S(1)}, bf16[256,4096]{1,0:T(8,128)(2,1)}) fusion(bf16[256,32768]{1,0:T(8,128)(2,1)} %p0.3, s32[]{:T(128)S(6)} %select_n.72, s32[]{:T(128)S(6)} %select_n.70, s32[]{:T(128)S(6)} %select_n.68, s32[]{:T(128)S(6)} %select_n.66), kind=kLoop, calls=%fused_computation.20 | loop fusion | bytes 16777232 | tf_op jit(solution)/shard_map/dynamic_slice | solution.py:240
  66.4 2.8 %collective-permute-start.21 = (bf16[256,4096]{1,0:T(8,128)(2,1)}, bf16[256,4096]{1,0:T(8,128)(2,1)}, u32[]{:S(2)}, u32[]{:S(2)}) collective-permute-start(bf16[256,4096]{1,0:T(8,128)(2,1)} %get-tuple-element.67), channel_id=1, source_target_pairs={{0,24},{8,0},{16,8},{24,16},{32,56},{40,32},{48,40},{56,48},{64,88... | collective-permute-start | bytes 6291464 | tf_op jit(solution)/shard_map/ppermute | solution.py:222
  72.9 10.8 %collective-permute-done.5 = f32[64,384]{1,0:T(8,128)S(1)} collective-permute-done((f32[64,384]{1,0:T(8,128)S(1)}, f32[64,384]{1,0:T(8,128)S(1)}, u32[]{:S(2)}, u32[]{:S(2)}) %collective-permute-start.5) | collective-permute-done | bytes 98336 | tf_op jit(solution)/shard_map/ppermute | solution.py:222
  83.7 3.2 %collective-permute-start.7 = (f32[64,384]{1,0:T(8,128)S(1)}, f32[64,384]{1,0:T(8,128)S(1)}, u32[]{:S(2)}, u32[]{:S(2)}) collective-permute-start(f32[64,384]{1,0:T(8,128)S(1)} %pad_maximum_fusion.6), channel_id=1, source_target_pairs={{0,64},{8,72},{16,80},{24,88},{32,96},{40,104},{48,112},{56,120},{... | collective-permute-start | bytes 294920 | tf_op jit(solution)/shard_map/ppermute | solution.py:222
  86.9 2.9 %pad_maximum_fusion.p3 = bf16[256,4096]{1,0:T(8,128)(2,1)} fusion(bf16[256,3072]{1,0:T(8,128)(2,1)} %collective-permute-done.4, bf16[256,1024]{1,0:T(8,128)(2,1)S(1)} %collective-permute-done.3), kind=kLoop, calls=%fused_computation | loop fusion | flops 4194304 | bytes 4194304 | tf_op jit(solution)/shard_map/concatenate | solution.py:273
  94.7 4.4 %all-to-all-start.1 = ((bf16[8,64,1024]{2,1,0:T(8,128)(2,1)}), bf16[8,64,1024]{2,1,0:T(8,128)(2,1)S(1)}, u32[]{:S(2)}, u32[]{:S(2)}) async-start(bf16[8,64,1024]{2,1,0:T(8,128)(2,1)} %tile.2), calls=%async_computation.1 | async-start | bytes 2097152 | tf_op jit(solution)/shard_map/all_to_all | solution.py:274
  101.3 15.2 %collective-permute-done.9 = bf16[64,1024]{1,0:T(8,128)(2,1)S(1)} collective-permute-done((bf16[64,1024]{1,0:T(8,128)(2,1)S(1)}, bf16[64,1024]{1,0:T(8,128)(2,1)S(1)}, u32[]{:S(2)}, u32[]{:S(2)}) %collective-permute-start.9) | collective-permute-done | bytes 131104 | tf_op jit(solution)/shard_map/ppermute | solution.py:276
  119.4 8.4 %product.3 = (f32[128,4096]{1,0:T(8,128)}, bf16[128,4096]{1,0:T(8,128)(2,1)S(1)}, bf16[128,4096]{1,0:T(8,128)(2,1)S(1)}, bf16[128,4096]{1,0:T(8,128)(2,1)S(1)}) custom-call(s32[3]{0:T(128)S(1)} %pad_add_fusion.where_ref, bf16[512,1024]{1,0:T(8,128)(2,1)S(1)} %bitcast.8, bf16[256,32768]{1,0:T(8,128)(2,1)} %p0.3, ...), custom_call_target="tpu_custom_call" | custom-call | flops 1 | bytes 1 | tf_op jit(solution)/shard_map/product/pallas_call | solution.py:168
  128.2 3.0 %collective-permute-start.23 = (bf16[128,4096]{1,0:T(8,128)(2,1)S(1)}, bf16[128,4096]{1,0:T(8,128)(2,1)S(1)}, u32[]{:S(2)}, u32[]{:S(2)}) collective-permute-start(bf16[128,4096]{1,0:T(8,128)(2,1)S(1)} %get-tuple-element.71), channel_id=1, source_target_pairs={{0,96},{8,104},{16,112},{24,120},{32,0},{40,8},{48,16},{56,24},{64... | collective-permute-start | bytes 3145736 | tf_op jit(solution)/shard_map/ppermute | solution.py:222
  132.1 8.0 %collective-permute-done.12.p1 = bf16[256,4096]{1,0:T(8,128)(2,1)} collective-permute-done((bf16[256,4096]{1,0:T(8,128)(2,1)}, bf16[256,4096]{1,0:T(8,128)(2,1)}, u32[]{:S(2)}, u32[]{:S(2)}) %collective-permute-start.12) | collective-permute-done | bytes 2097184 | tf_op jit(solution)/shard_map/ppermute | solution.py:222
  140.2 8.8 %product.2 = (f32[128,4096]{1,0:T(8,128)}, bf16[128,4096]{1,0:T(8,128)(2,1)}, bf16[128,4096]{1,0:T(8,128)(2,1)S(1)}, bf16[128,4096]{1,0:T(8,128)(2,1)S(1)}) custom-call(s32[3]{0:T(128)S(1)} %pad_add_fusion.where_ref, bf16[512,1024]{1,0:T(8,128)(2,1)S(1)} %pad_maximum_fusion.1.basis_ref, bf16[256,32768]{1,0:T(8,128)(2,1)} %p0.3, ...), custom_call_target="tpu_custom_call" | custom-call | flops 1 | bytes 1 | tf_op jit(solution)/shard_map/product/pallas_call | solution.py:168
  152.3 10.2 %collective-permute-done.22.g1 = bf16[128,4096]{1,0:T(8,128)(2,1)S(1)} collective-permute-done((bf16[128,4096]{1,0:T(8,128)(2,1)S(1)}, bf16[128,4096]{1,0:T(8,128)(2,1)S(1)}, u32[]{:S(2)}, u32[]{:S(2)}) %collective-permute-start.22) | collective-permute-done | bytes 1048608 | tf_op jit(solution)/shard_map/ppermute | solution.py:222
  162.5 21.6 %collective-permute-start.16 = (bf16[128,4096]{1,0:T(8,128)(2,1)S(1)}, bf16[128,4096]{1,0:T(8,128)(2,1)S(1)}, u32[]{:S(2)}, u32[]{:S(2)}) collective-permute-start(bf16[128,4096]{1,0:T(8,128)(2,1)S(1)} %get-tuple-element.60), channel_id=1, source_target_pairs={{0,16},{8,24},{16,0},{24,8},{32,48},{40,56},{48,32},{56,40},{64,80... | collective-permute-start | bytes 3145736 | tf_op jit(solution)/shard_map/ppermute | solution.py:222
  185.2 3.7 %collective-permute-start.25 = (bf16[32,4096]{1,0:T(8,128)(2,1)S(1)}, bf16[32,4096]{1,0:T(8,128)(2,1)S(1)}, u32[]{:S(2)}, u32[]{:S(2)}) collective-permute-start(bf16[32,4096]{1,0:T(8,128)(2,1)S(1)} %get-tuple-element.73), channel_id=1, source_target_pairs={{0,8},{8,16},{16,24},{24,0},{32,40},{40,48},{48,56},{56,32},{64,72... | collective-permute-start | bytes 786440 | tf_op jit(solution)/shard_map/ppermute | solution.py:222
  188.9 13.8 %collective-permute-done.16.g3 = bf16[128,4096]{1,0:T(8,128)(2,1)S(1)} collective-permute-done((bf16[128,4096]{1,0:T(8,128)(2,1)S(1)}, bf16[128,4096]{1,0:T(8,128)(2,1)S(1)}, u32[]{:S(2)}, u32[]{:S(2)}) %collective-permute-start.16) | collective-permute-done | bytes 1048608 | tf_op jit(solution)/shard_map/ppermute | solution.py:222
  205.6 3.2 %collective-permute-start.18 = (bf16[32,4096]{1,0:T(8,128)(2,1)S(1)}, bf16[32,4096]{1,0:T(8,128)(2,1)S(1)}, u32[]{:S(2)}, u32[]{:S(2)}) collective-permute-start(bf16[32,4096]{1,0:T(8,128)(2,1)S(1)} %get-tuple-element.62), channel_id=1, source_target_pairs={{0,96},{8,104},{16,112},{24,120},{32,0},{40,8},{48,16},{56,24},{64... | collective-permute-start | bytes 786440 | tf_op jit(solution)/shard_map/ppermute | solution.py:222
  211.0 2.7 %collective-permute-done.17.one = bf16[32,4096]{1,0:T(8,128)(2,1)S(1)} collective-permute-done((bf16[32,4096]{1,0:T(8,128)(2,1)S(1)}, bf16[32,4096]{1,0:T(8,128)(2,1)S(1)}, u32[]{:S(2)}, u32[]{:S(2)}) %collective-permute-start.17) | collective-permute-done | bytes 262176 | tf_op jit(solution)/shard_map/ppermute | solution.py:222
  (90 shorter events, 35.0 us)
Async XLA Ops:
  4.6 61.4 %collective-permute-start.4 = (bf16[256,3072]{1,0:T(8,128)(2,1)}, bf16[256,3072]{1,0:T(8,128)(2,1)}, u32[]{:S(2)}, u32[]{:S(2)}) collective-permute-start(bf16[256,3072]{1,0:T(8,128)(2,1)} %constant_dynamic-slice_fusion.5), channel_id=1, source_target_pairs={{0,16},{8,24},{16,0},{24,8},{32,48},{40,56},{48,32},{56,40},{64,80... | collective-permute-start | bytes 4718600 | tf_op jit(solution)/shard_map/ppermute | solution.py:222
  26.5 15.7 %all-to-all-start = ((f32[8,64,256]{2,1,0:T(8,128)}), f32[8,64,256]{2,1,0:T(8,128)S(1)}, u32[]{:S(2)}, u32[]{:S(2)}) async-start(f32[8,64,256]{2,1,0:T(8,128)} %bitcast.6), calls=%async_computation | async-start | bytes 1048576 | tf_op jit(solution)/shard_map/all_to_all | solution.py:249
  31.8 58.2 %collective-permute-start.8 = (bf16[256,4096]{1,0:T(8,128)(2,1)}, bf16[256,4096]{1,0:T(8,128)(2,1)}, u32[]{:S(2)}, u32[]{:S(2)}) collective-permute-start(bf16[256,4096]{1,0:T(8,128)(2,1)} %constant_dynamic-slice_fusion.4), channel_id=1, source_target_pairs={{0,64},{8,72},{16,80},{24,88},{32,96},{40,104},{48,112},{56,120},{... | collective-permute-start | bytes 6291464 | tf_op jit(solution)/shard_map/ppermute | solution.py:222
  42.2 17.3 %collective-permute-start = (f32[64,256]{1,0:T(8,128)S(1)}, f32[64,256]{1,0:T(8,128)S(1)}, u32[]{:S(2)}, u32[]{:S(2)}) collective-permute-start(f32[64,256]{1,0:T(8,128)S(1)} %reduce_sum.45), channel_id=1, source_target_pairs={{0,8},{8,16},{16,24},{24,0},{32,40},{40,48},{48,56},{56,32},{64,72... | collective-permute-start | bytes 196616 | tf_op jit(solution)/shard_map/ppermute | solution.py:222
  42.9 23.1 %collective-permute-start.3 = (bf16[256,1024]{1,0:T(8,128)(2,1)}, bf16[256,1024]{1,0:T(8,128)(2,1)S(1)}, u32[]{:S(2)}, u32[]{:S(2)}) collective-permute-start(bf16[256,1024]{1,0:T(8,128)(2,1)} %constant_dynamic-slice_fusion.6), channel_id=1, source_target_pairs={{0,16},{8,24},{16,0},{24,8},{32,48},{40,56},{48,32},{56,40},{64,80... | collective-permute-start | bytes 1572872 | tf_op jit(solution)/shard_map/ppermute | solution.py:222
  44.9 21.0 %collective-permute-start.1 = (f32[64,256]{1,0:T(8,128)S(1)}, f32[64,256]{1,0:T(8,128)S(1)}, u32[]{:S(2)}, u32[]{:S(2)}) collective-permute-start(f32[64,256]{1,0:T(8,128)S(1)} %reduce_sum.45), channel_id=1, source_target_pairs={{0,24},{8,0},{16,8},{24,16},{32,56},{40,32},{48,40},{56,48},{64,88... | collective-permute-start | bytes 196616 | tf_op jit(solution)/shard_map/ppermute | solution.py:222
  66.0 53.3 %collective-permute-start.20 = (bf16[256,4096]{1,0:T(8,128)(2,1)}, bf16[256,4096]{1,0:T(8,128)(2,1)}, u32[]{:S(2)}, u32[]{:S(2)}) collective-permute-start(bf16[256,4096]{1,0:T(8,128)(2,1)} %get-tuple-element.66), channel_id=1, source_target_pairs={{0,8},{8,16},{16,24},{24,0},{32,40},{40,48},{48,56},{56,32},{64,72... | collective-permute-start | bytes 6291464 | tf_op jit(solution)/shard_map/ppermute | solution.py:222
  66.4 52.9 %collective-permute-start.21 = (bf16[256,4096]{1,0:T(8,128)(2,1)}, bf16[256,4096]{1,0:T(8,128)(2,1)}, u32[]{:S(2)}, u32[]{:S(2)}) collective-permute-start(bf16[256,4096]{1,0:T(8,128)(2,1)} %get-tuple-element.67), channel_id=1, source_target_pairs={{0,24},{8,0},{16,8},{24,16},{32,56},{40,32},{48,40},{56,48},{64,88... | collective-permute-start | bytes 6291464 | tf_op jit(solution)/shard_map/ppermute | solution.py:222
  69.6 14.1 %collective-permute-start.5 = (f32[64,384]{1,0:T(8,128)S(1)}, f32[64,384]{1,0:T(8,128)S(1)}, u32[]{:S(2)}, u32[]{:S(2)}) collective-permute-start(f32[64,384]{1,0:T(8,128)S(1)} %pad_maximum_fusion.6), channel_id=1, source_target_pairs={{0,32},{8,40},{16,48},{24,56},{32,64},{40,72},{48,80},{56,88},{64,... | collective-permute-start | bytes 294920 | tf_op jit(solution)/shard_map/ppermute | solution.py:222
  71.2 18.6 %collective-permute-start.6 = (f32[64,384]{1,0:T(8,128)S(1)}, f32[64,384]{1,0:T(8,128)S(1)}, u32[]{:S(2)}, u32[]{:S(2)}) collective-permute-start(f32[64,384]{1,0:T(8,128)S(1)} %pad_maximum_fusion.6), channel_id=1, source_target_pairs={{0,96},{8,104},{16,112},{24,120},{32,0},{40,8},{48,16},{56,24},{64... | collective-permute-start | bytes 294920 | tf_op jit(solution)/shard_map/ppermute | solution.py:222
  90.0 50.1 %collective-permute-start.12 = (bf16[256,4096]{1,0:T(8,128)(2,1)}, bf16[256,4096]{1,0:T(8,128)(2,1)}, u32[]{:S(2)}, u32[]{:S(2)}) collective-permute-start(bf16[256,4096]{1,0:T(8,128)(2,1)} %get-tuple-element.54), channel_id=1, source_target_pairs={{0,32},{8,40},{16,48},{24,56},{32,64},{40,72},{48,80},{56,88},{64,... | collective-permute-start | bytes 6291464 | tf_op jit(solution)/shard_map/ppermute | solution.py:222
  91.6 48.7 %collective-permute-start.13 = (bf16[256,4096]{1,0:T(8,128)(2,1)S(1)}, bf16[256,4096]{1,0:T(8,128)(2,1)}, u32[]{:S(2)}, u32[]{:S(2)}) collective-permute-start(bf16[256,4096]{1,0:T(8,128)(2,1)S(1)} %get-tuple-element.55), channel_id=1, source_target_pairs={{0,96},{8,104},{16,112},{24,120},{32,0},{40,8},{48,16},{56,24},{64... | collective-permute-start | bytes 6291464 | tf_op jit(solution)/shard_map/ppermute | solution.py:222
  94.7 24.6 %all-to-all-start.1 = ((bf16[8,64,1024]{2,1,0:T(8,128)(2,1)}), bf16[8,64,1024]{2,1,0:T(8,128)(2,1)S(1)}, u32[]{:S(2)}, u32[]{:S(2)}) async-start(bf16[8,64,1024]{2,1,0:T(8,128)(2,1)} %tile.2), calls=%async_computation.1 | async-start | bytes 2097152 | tf_op jit(solution)/shard_map/all_to_all | solution.py:274
  99.2 17.3 %collective-permute-start.9 = (bf16[64,1024]{1,0:T(8,128)(2,1)S(1)}, bf16[64,1024]{1,0:T(8,128)(2,1)S(1)}, u32[]{:S(2)}, u32[]{:S(2)}) collective-permute-start(bf16[64,1024]{1,0:T(8,128)(2,1)S(1)} %pad_maximum_fusion.4), channel_id=1, source_target_pairs={{0,2},{1,3},{2,0},{3,1},{4,6},{5,7},{6,4},{7,5},{8,10},{9,11},{10,... | collective-permute-start | bytes 393224 | tf_op jit(solution)/shard_map/ppermute | solution.py:276
  117.2 10.9 %collective-permute-start.10 = (bf16[128,1024]{1,0:T(8,128)(2,1)}, bf16[128,1024]{1,0:T(8,128)(2,1)S(1)}, u32[]{:S(2)}, u32[]{:S(2)}) collective-permute-start(bf16[128,1024]{1,0:T(8,128)(2,1)} %pad_maximum_fusion.3), channel_id=1, source_target_pairs={{0,6},{1,7},{2,4},{3,5},{4,2},{5,3},{6,0},{7,1},{8,14},{9,15},{10,... | collective-permute-start | bytes 786440 | tf_op jit(solution)/shard_map/ppermute | solution.py:276
  127.7 34.8 %collective-permute-start.22 = (bf16[128,4096]{1,0:T(8,128)(2,1)S(1)}, bf16[128,4096]{1,0:T(8,128)(2,1)S(1)}, u32[]{:S(2)}, u32[]{:S(2)}) collective-permute-start(bf16[128,4096]{1,0:T(8,128)(2,1)S(1)} %get-tuple-element.70), channel_id=1, source_target_pairs={{0,32},{8,40},{16,48},{24,56},{32,64},{40,72},{48,80},{56,88},{64,... | collective-permute-start | bytes 3145736 | tf_op jit(solution)/shard_map/ppermute | solution.py:222
  128.2 55.9 %collective-permute-start.23 = (bf16[128,4096]{1,0:T(8,128)(2,1)S(1)}, bf16[128,4096]{1,0:T(8,128)(2,1)S(1)}, u32[]{:S(2)}, u32[]{:S(2)}) collective-permute-start(bf16[128,4096]{1,0:T(8,128)(2,1)S(1)} %get-tuple-element.71), channel_id=1, source_target_pairs={{0,96},{8,104},{16,112},{24,120},{32,0},{40,8},{48,16},{56,24},{64... | collective-permute-start | bytes 3145736 | tf_op jit(solution)/shard_map/ppermute | solution.py:222
  131.2 52.9 %collective-permute-start.24 = (bf16[128,4096]{1,0:T(8,128)(2,1)S(1)}, bf16[128,4096]{1,0:T(8,128)(2,1)S(1)}, u32[]{:S(2)}, u32[]{:S(2)}) collective-permute-start(bf16[128,4096]{1,0:T(8,128)(2,1)S(1)} %get-tuple-element.72), channel_id=1, source_target_pairs={{0,64},{8,72},{16,80},{24,88},{32,96},{40,104},{48,112},{56,120},{... | collective-permute-start | bytes 3145736 | tf_op jit(solution)/shard_map/ppermute | solution.py:222
  149.0 39.8 %collective-permute-start.14 = (bf16[128,4096]{1,0:T(8,128)(2,1)}, bf16[128,4096]{1,0:T(8,128)(2,1)S(1)}, u32[]{:S(2)}, u32[]{:S(2)}) collective-permute-start(bf16[128,4096]{1,0:T(8,128)(2,1)} %get-tuple-element.58), channel_id=1, source_target_pairs={{0,8},{8,16},{16,24},{24,0},{32,40},{40,48},{48,56},{56,32},{64,72... | collective-permute-start | bytes 3145736 | tf_op jit(solution)/shard_map/ppermute | solution.py:222
  149.6 39.2 %collective-permute-start.15 = (bf16[128,4096]{1,0:T(8,128)(2,1)S(1)}, bf16[128,4096]{1,0:T(8,128)(2,1)S(1)}, u32[]{:S(2)}, u32[]{:S(2)}) collective-permute-start(bf16[128,4096]{1,0:T(8,128)(2,1)S(1)} %get-tuple-element.59), channel_id=1, source_target_pairs={{0,24},{8,0},{16,8},{24,16},{32,56},{40,32},{48,40},{56,48},{64,88... | collective-permute-start | bytes 3145736 | tf_op jit(solution)/shard_map/ppermute | solution.py:222
  162.5 40.1 %collective-permute-start.16 = (bf16[128,4096]{1,0:T(8,128)(2,1)S(1)}, bf16[128,4096]{1,0:T(8,128)(2,1)S(1)}, u32[]{:S(2)}, u32[]{:S(2)}) collective-permute-start(bf16[128,4096]{1,0:T(8,128)(2,1)S(1)} %get-tuple-element.60), channel_id=1, source_target_pairs={{0,16},{8,24},{16,0},{24,8},{32,48},{40,56},{48,32},{56,40},{64,80... | collective-permute-start | bytes 3145736 | tf_op jit(solution)/shard_map/ppermute | solution.py:222
  184.5 21.1 %collective-permute-start.27 = (bf16[32,4096]{1,0:T(8,128)(2,1)S(1)}, bf16[32,4096]{1,0:T(8,128)(2,1)S(1)}, u32[]{:S(2)}, u32[]{:S(2)}) collective-permute-start(bf16[32,4096]{1,0:T(8,128)(2,1)S(1)} %collect.7), channel_id=1, source_target_pairs={{0,16},{8,24},{16,0},{24,8},{32,48},{40,56},{48,32},{56,40},{64,80... | collective-permute-start | bytes 786440 | tf_op jit(solution)/shard_map/ppermute | solution.py:222
  185.2 23.6 %collective-permute-start.25 = (bf16[32,4096]{1,0:T(8,128)(2,1)S(1)}, bf16[32,4096]{1,0:T(8,128)(2,1)S(1)}, u32[]{:S(2)}, u32[]{:S(2)}) collective-permute-start(bf16[32,4096]{1,0:T(8,128)(2,1)S(1)} %get-tuple-element.73), channel_id=1, source_target_pairs={{0,8},{8,16},{16,24},{24,0},{32,40},{40,48},{48,56},{56,32},{64,72... | collective-permute-start | bytes 786440 | tf_op jit(solution)/shard_map/ppermute | solution.py:222
  188.8 20.0 %collective-permute-start.26 = (bf16[32,4096]{1,0:T(8,128)(2,1)S(1)}, bf16[32,4096]{1,0:T(8,128)(2,1)S(1)}, u32[]{:S(2)}, u32[]{:S(2)}) collective-permute-start(bf16[32,4096]{1,0:T(8,128)(2,1)S(1)} %get-tuple-element.74), channel_id=1, source_target_pairs={{0,24},{8,0},{16,8},{24,16},{32,56},{40,32},{48,40},{56,48},{64,88... | collective-permute-start | bytes 786440 | tf_op jit(solution)/shard_map/ppermute | solution.py:222
  (18 other events, 243.6 us)

commit v5 on v3

--- a/solution.py
+++ b/solution.py
@@ -275,14 +275,15 @@
         bases[1] = jnp.concatenate([bases[1], other], axis=0)
 
     x_received, y_received = (*x_near, x_far), (*y_near, y_far)
-    terms = [
-        product(axis, (0,) + DISTANCES, where, bases[axis], slab, received)
-        for axis, received in enumerate((x_received, y_received))
-    ]
+    x_own, *sends = product(0, (0,) + DISTANCES, where, bases[0], slab, x_received)
+    x_got = [shift(send, 1, distance) for send, distance in zip(sends, DISTANCES)]
+    sends = product(1, (1, 3), where, bases[1], slab, y_received)
+    y_got = [shift(send, 0, distance) for send, distance in zip(sends, DISTANCES)]
+    y_basis, x_got[0] = lax.optimization_barrier((bases[1], x_got[0]))
+    y_own, y_send = product(1, (0, 2), where, y_basis, slab, y_received)
+    y_got.append(shift(y_send, 0, 2))
     out = ()
-    for axis in range(2):
-        own, *sends = terms[axis]
-        got = [shift(send, 1 - axis, distance) for send, distance in zip(sends, DISTANCES)]
+    for axis, own, got in ((0, x_own, x_got), (1, y_own, y_got)):
         (far,) = collect(own, got, 2, 1)
         far = shift(far, axis, 2)
         near = collect(own, got, 0, 2)

time: 195 us -> 195 us (level)
  waiting for transfers between devices: 78.3 us -> 73 us
  Pallas kernels: 38.6 us -> 43.2 us
    ppermute x24, waiting for transfers between devices: 52.7 us -> 47.2 us  [shift(): lax.ppermute(value, 'rows', PERMS[axis](lambda q: (q + distance) % SIDE))]
    pallas_call x2 -> x3, Pallas kernels: 17.2 us -> 21.9 us  [product(): pl.pallas_call(functools.partial(product_kernel, axis, distances), grid_s...]
  transfers between devices with their start and end apart: 29 -> 29, of which waited for: 16 -> 13; matrix products, arithmetic and copies ran while one was open for 6% -> 6% of each run, Pallas kernels for 19% -> 21%
where the time goes in v5:
time: 195 us
  waiting for transfers between devices  73 us (37%)
  starting transfers between devices  62.6 us (32%)
  Pallas kernels  43.2 us (22%)
  local copies, waits for them, and re-layouts  15 us (8%)
    ppermute x24, starting transfers between devices, shift(): lax.ppermute(value, 'rows', PERMS[axis](lambda q: (q + distance) % SIDE))  47.4 us
    ppermute x24, waiting for transfers between devices, shift(): lax.ppermute(value, 'rows', PERMS[axis](lambda q: (q + distance) % SIDE))  47.2 us
    pallas_call x3, Pallas kernels, product(): pl.pallas_call(functools.partial(product_kernel, axis, distances), grid_s...  21.9 us
    pallas_call x1, Pallas kernels, local_sketch(): pl.pallas_call(sketch_kernel, grid_spec=pltpu.PrefetchScalarGridSpec(num_...  15.5 us
    ppermute x3, waiting for transfers between devices, per_device(): lax.ppermute(bases[1], 'cols', [(k, k ^ mask) for k in range(col_devices)])  15.4 us
    dynamic_slice x3, local copies, waits for them, and re-layouts, block(): return lax.dynamic_slice(source, (0, start), (rows, size))  13.6 us
    all_to_all x1, waiting for transfers between devices, per_device(): parts = lax.all_to_all(partial, 'cols', 0, 0, tiled=True)  10.3 us
    all_to_all x1, starting transfers between devices, per_device(): lax.all_to_all(jnp.tile(bases[0], (col_devices, 1)), 'cols', 0, 0, tiled=...  5.45 us
  transfers between devices with their start and end apart: 29, of which 13 were waited for; matrix products, arithmetic and copies ran while one was open for 6% of the time, Pallas kernels for 21%

profile of v5, /device:TPU:0, one launch (start us, length us, event | category | flops | bytes accessed | tf_op | source)
XLA Modules:
  0.0 194.8 jit_solution(16176739737134279632)
XLA Ops:
  0.0 3.2 %constant_dynamic-slice_fusion.5 = bf16[256,4096]{1,0:T(8,128)(2,1)} fusion(bf16[256,32768]{1,0:T(8,128)(2,1)} %p0.5, s32[]{:T(128)S(6)} %select_n.56), kind=kLoop, calls=%fused_computation.24 | loop fusion | bytes 4194308 | tf_op jit(solution)/shard_map/dynamic_slice | solution.py:240
  3.2 3.1 %collective-permute-start.3 = (bf16[256,4096]{1,0:T(8,128)(2,1)}, bf16[256,4096]{1,0:T(8,128)(2,1)}, u32[]{:S(2)}, u32[]{:S(2)}) collective-permute-start(bf16[256,4096]{1,0:T(8,128)(2,1)} %constant_dynamic-slice_fusion.5), channel_id=1, source_target_pairs={{0,16},{8,24},{16,0},{24,8},{32,48},{40,56},{48,32},{56,40},{64,80... | collective-permute-start | bytes 6291464 | tf_op jit(solution)/shard_map/ppermute | solution.py:222
  6.3 3.2 %constant_dynamic-slice_fusion.4 = bf16[256,4096]{1,0:T(8,128)(2,1)} fusion(bf16[256,32768]{1,0:T(8,128)(2,1)} %p0.5, s32[]{:T(128)S(6)} %select_n.58), kind=kLoop, calls=%fused_computation.23 | loop fusion | bytes 4194308 | tf_op jit(solution)/shard_map/dynamic_slice | solution.py:240
  9.6 3.2 %collective-permute-start.7 = (bf16[256,4096]{1,0:T(8,128)(2,1)}, bf16[256,4096]{1,0:T(8,128)(2,1)S(1)}, u32[]{:S(2)}, u32[]{:S(2)}) collective-permute-start(bf16[256,4096]{1,0:T(8,128)(2,1)} %constant_dynamic-slice_fusion.4), channel_id=1, source_target_pairs={{0,64},{8,72},{16,80},{24,88},{32,96},{40,104},{48,112},{56,120},{... | collective-permute-start | bytes 6291464 | tf_op jit(solution)/shard_map/ppermute | solution.py:222
  12.9 15.5 %sketch.1 = f32[512,256]{1,0:T(8,128)} custom-call(s32[1]{0:T(128)} %bitcast.3.first_ref, bf16[256,32768]{1,0:T(8,128)(2,1)} %p0.5, s32[1,32768]{1,0:T(1,128)S(1)} %bitcast.9, s32[512,1]{1,0:T(8,128)S(1)} %copy.5.sampled_ref), custom_call_target="tpu_custom_call" | custom-call | flops 1 | bytes 1 | tf_op jit(solution)/shard_map/sketch/pallas_call | solution.py:69
  28.4 5.3 %all-to-all-start = ((f32[8,64,256]{2,1,0:T(8,128)}), f32[8,64,256]{2,1,0:T(8,128)S(1)}, u32[]{:S(2)}, u32[]{:S(2)}) async-start(f32[8,64,256]{2,1,0:T(8,128)} %bitcast.6), calls=%async_computation | async-start | bytes 1048576 | tf_op jit(solution)/shard_map/all_to_all | solution.py:248
  33.7 10.3 %all-to-all-done = f32[8,64,256]{2,1,0:T(8,128)S(1)} async-done(((f32[8,64,256]{2,1,0:T(8,128)}), f32[8,64,256]{2,1,0:T(8,128)S(1)}, u32[]{:S(2)}, u32[]{:S(2)}) %all-to-all-start) | async-done | bytes 524320 | tf_op jit(solution)/shard_map/all_to_all | solution.py:248
  44.8 2.6 %collective-permute-start.1 = (f32[64,256]{1,0:T(8,128)S(1)}, f32[64,256]{1,0:T(8,128)S(1)}, u32[]{:S(2)}, u32[]{:S(2)}) collective-permute-start(f32[64,256]{1,0:T(8,128)S(1)} %reduce_sum.45), channel_id=1, source_target_pairs={{0,24},{8,0},{16,8},{24,16},{32,56},{40,32},{48,40},{56,48},{64,88... | collective-permute-start | bytes 196616 | tf_op jit(solution)/shard_map/ppermute | solution.py:222
  47.4 7.2 %constant_dynamic-slice_fusion = (bf16[256,4096]{1,0:T(8,128)(2,1)}, bf16[256,4096]{1,0:T(8,128)(2,1)}, bf16[256,4096]{1,0:T(8,128)(2,1)}, bf16[256,4096]{1,0:T(8,128)(2,1)}) fusion(bf16[256,32768]{1,0:T(8,128)(2,1)} %p0.5, s32[]{:T(128)S(6)} %select_n.66, s32[]{:T(128)S(6)} %select_n.64, s32[]{:T(128)S(6)} %select_n.62, s32[]{:T(128)S(6)} %select_n.60), kind=kLoop, calls=%fused_computation.19 | loop fusion | bytes 16777232 | tf_op jit(solution)/shard_map/dynamic_slice | solution.py:240
  65.7 2.4 %collective-permute-done.6 = f32[64,384]{1,0:T(8,128)S(1)} collective-permute-done((f32[64,384]{1,0:T(8,128)S(1)}, f32[64,384]{1,0:T(8,128)S(1)}, u32[]{:S(2)}, u32[]{:S(2)}) %collective-permute-start.6) | collective-permute-done | bytes 98336 | tf_op jit(solution)/shard_map/ppermute | solution.py:222
  68.6 2.7 %collective-permute-start.15 = (bf16[256,4096]{1,0:T(8,128)(2,1)}, bf16[256,4096]{1,0:T(8,128)(2,1)}, u32[]{:S(2)}, u32[]{:S(2)}) collective-permute-start(bf16[256,4096]{1,0:T(8,128)(2,1)} %get-tuple-element.55), channel_id=1, source_target_pairs={{0,96},{8,104},{16,112},{24,120},{32,0},{40,8},{48,16},{56,24},{64... | collective-permute-start | bytes 6291464 | tf_op jit(solution)/shard_map/ppermute | solution.py:222
  72.7 5.5 %all-to-all-start.1 = ((bf16[8,64,1024]{2,1,0:T(8,128)(2,1)}), bf16[8,64,1024]{2,1,0:T(8,128)(2,1)S(1)}, u32[]{:S(2)}, u32[]{:S(2)}) async-start(bf16[8,64,1024]{2,1,0:T(8,128)(2,1)} %tile.2), calls=%async_computation.1 | async-start | bytes 2097152 | tf_op jit(solution)/shard_map/all_to_all | solution.py:272
  80.3 15.2 %collective-permute-done.8 = bf16[64,1024]{1,0:T(8,128)(2,1)S(1)} collective-permute-done((bf16[64,1024]{1,0:T(8,128)(2,1)S(1)}, bf16[64,1024]{1,0:T(8,128)(2,1)S(1)}, u32[]{:S(2)}, u32[]{:S(2)}) %collective-permute-start.8) | collective-permute-done | bytes 131104 | tf_op jit(solution)/shard_map/ppermute | solution.py:274
  97.9 5.5 %collective-permute-done.11.p1 = bf16[256,4096]{1,0:T(8,128)(2,1)} collective-permute-done((bf16[256,4096]{1,0:T(8,128)(2,1)}, bf16[256,4096]{1,0:T(8,128)(2,1)}, u32[]{:S(2)}, u32[]{:S(2)}) %collective-permute-start.11) | collective-permute-done | bytes 2097184 | tf_op jit(solution)/shard_map/ppermute | solution.py:222
  103.6 8.6 %product.3 = (f32[128,4096]{1,0:T(8,128)}, bf16[128,4096]{1,0:T(8,128)(2,1)S(1)}, bf16[128,4096]{1,0:T(8,128)(2,1)}, bf16[128,4096]{1,0:T(8,128)(2,1)S(1)}) custom-call(s32[3]{0:T(128)S(1)} %pad_add_fusion.where_ref, bf16[512,1024]{1,0:T(8,128)(2,1)S(1)} %bitcast.8, bf16[256,32768]{1,0:T(8,128)(2,1)} %p0.5, bf16[256,4096]{1,0:T(8,128)(2,1)} %collective-permute-done.11.p1, ...), custom_call_target="tpu_custom_call" | custom-call | flops 1 | bytes 1 | tf_op jit(solution)/shard_map/product/pallas_call | solution.py:168
  115.8 2.9 %collective-permute-start.23 = (bf16[128,4096]{1,0:T(8,128)(2,1)S(1)}, bf16[128,4096]{1,0:T(8,128)(2,1)S(1)}, u32[]{:S(2)}, u32[]{:S(2)}) collective-permute-start(bf16[128,4096]{1,0:T(8,128)(2,1)S(1)} %get-tuple-element.66), channel_id=1, source_target_pairs={{0,64},{8,72},{16,80},{24,88},{32,96},{40,104},{48,112},{56,120},{... | collective-permute-start | bytes 3145736 | tf_op jit(solution)/shard_map/ppermute | solution.py:222
  118.8 7.1 %product.5 = (bf16[128,4096]{1,0:T(8,128)(2,1)}, bf16[128,4096]{1,0:T(8,128)(2,1)}) custom-call(s32[3]{0:T(128)S(1)} %pad_add_fusion.where_ref, bf16[512,1024]{1,0:T(8,128)(2,1)S(1)} %pad_maximum_fusion.basis_ref, bf16[256,32768]{1,0:T(8,128)(2,1)} %p0.5, bf16[256,4096]{1,0:T(8,128)(2,1)} %collective-permute-done.14.p1, ...), custom_call_target="tpu_custom_call" | custom-call | flops 1 | bytes 1 | tf_op jit(solution)/shard_map/product/pallas_call | solution.py:168
  129.2 10.6 %collective-permute-done.13.g1 = bf16[128,4096]{1,0:T(8,128)(2,1)S(1)} collective-permute-done((bf16[128,4096]{1,0:T(8,128)(2,1)S(1)}, bf16[128,4096]{1,0:T(8,128)(2,1)S(1)}, u32[]{:S(2)}, u32[]{:S(2)}) %collective-permute-start.13) | collective-permute-done | bytes 1048608 | tf_op jit(solution)/shard_map/ppermute | solution.py:222
  139.7 6.2 %product.4 = (f32[128,4096]{1,0:T(8,128)S(1)}, bf16[128,4096]{1,0:T(8,128)(2,1)S(1)}) custom-call(s32[3]{0:T(128)S(1)} %pad_add_fusion.where_ref, bf16[512,1024]{1,0:T(8,128)(2,1)S(1)} %pad_maximum_fusion.basis_ref, bf16[256,32768]{1,0:T(8,128)(2,1)} %p0.5, bf16[256,4096]{1,0:T(8,128)(2,1)} %collective-permute-done.14.p1, ...), custom_call_target="tpu_custom_call" | custom-call | flops 1 | bytes 1 | tf_op jit(solution)/shard_map/product/pallas_call | solution.py:168
  147.7 13.0 %collective-permute-done.23.g3 = bf16[128,4096]{1,0:T(8,128)(2,1)S(1)} collective-permute-done((bf16[128,4096]{1,0:T(8,128)(2,1)S(1)}, bf16[128,4096]{1,0:T(8,128)(2,1)S(1)}, u32[]{:S(2)}, u32[]{:S(2)}) %collective-permute-start.23) | collective-permute-done | bytes 1048608 | tf_op jit(solution)/shard_map/ppermute | solution.py:222
  161.0 2.4 %collective-permute-start.26 = (bf16[32,4096]{1,0:T(8,128)(2,1)S(1)}, bf16[32,4096]{1,0:T(8,128)(2,1)S(1)}, u32[]{:S(2)}, u32[]{:S(2)}) collective-permute-start(bf16[32,4096]{1,0:T(8,128)(2,1)S(1)} %collect.7), channel_id=1, source_target_pairs={{0,16},{8,24},{16,0},{24,8},{32,48},{40,56},{48,32},{56,40},{64,80... | collective-permute-start | bytes 786440 | tf_op jit(solution)/shard_map/ppermute | solution.py:222
  167.2 11.3 %collective-permute-done.17.g2 = bf16[128,4096]{1,0:T(8,128)(2,1)S(1)} collective-permute-done((bf16[128,4096]{1,0:T(8,128)(2,1)}, bf16[128,4096]{1,0:T(8,128)(2,1)S(1)}, u32[]{:S(2)}, u32[]{:S(2)}) %collective-permute-start.17) | collective-permute-done | bytes 1048608 | tf_op jit(solution)/shard_map/ppermute | solution.py:222
  178.9 5.6 %collective-permute-start.21 = (bf16[32,4096]{1,0:T(8,128)(2,1)S(1)}, bf16[32,4096]{1,0:T(8,128)(2,1)S(1)}, u32[]{:S(2)}, u32[]{:S(2)}) collective-permute-start(bf16[32,4096]{1,0:T(8,128)(2,1)S(1)} %collect.5), channel_id=1, source_target_pairs={{0,64},{8,72},{16,80},{24,88},{32,96},{40,104},{48,112},{56,120},{... | collective-permute-start | bytes 786440 | tf_op jit(solution)/shard_map/ppermute | solution.py:222
  185.1 3.2 %collective-permute-start.20 = (bf16[32,4096]{1,0:T(8,128)(2,1)S(1)}, bf16[32,4096]{1,0:T(8,128)(2,1)S(1)}, u32[]{:S(2)}, u32[]{:S(2)}) collective-permute-start(bf16[32,4096]{1,0:T(8,128)(2,1)S(1)} %get-tuple-element.62), channel_id=1, source_target_pairs={{0,96},{8,104},{16,112},{24,120},{32,0},{40,8},{48,16},{56,24},{64... | collective-permute-start | bytes 786440 | tf_op jit(solution)/shard_map/ppermute | solution.py:222
  (71 shorter events, 38.8 us)
Async XLA Ops:
  3.2 51.8 %collective-permute-start.3 = (bf16[256,4096]{1,0:T(8,128)(2,1)}, bf16[256,4096]{1,0:T(8,128)(2,1)}, u32[]{:S(2)}, u32[]{:S(2)}) collective-permute-start(bf16[256,4096]{1,0:T(8,128)(2,1)} %constant_dynamic-slice_fusion.5), channel_id=1, source_target_pairs={{0,16},{8,24},{16,0},{24,8},{32,48},{40,56},{48,32},{56,40},{64,80... | collective-permute-start | bytes 6291464 | tf_op jit(solution)/shard_map/ppermute | solution.py:222
  9.6 52.4 %collective-permute-start.7 = (bf16[256,4096]{1,0:T(8,128)(2,1)}, bf16[256,4096]{1,0:T(8,128)(2,1)S(1)}, u32[]{:S(2)}, u32[]{:S(2)}) collective-permute-start(bf16[256,4096]{1,0:T(8,128)(2,1)} %constant_dynamic-slice_fusion.4), channel_id=1, source_target_pairs={{0,64},{8,72},{16,80},{24,88},{32,96},{40,104},{48,112},{56,120},{... | collective-permute-start | bytes 6291464 | tf_op jit(solution)/shard_map/ppermute | solution.py:222
  28.4 15.7 %all-to-all-start = ((f32[8,64,256]{2,1,0:T(8,128)}), f32[8,64,256]{2,1,0:T(8,128)S(1)}, u32[]{:S(2)}, u32[]{:S(2)}) async-start(f32[8,64,256]{2,1,0:T(8,128)} %bitcast.6), calls=%async_computation | async-start | bytes 1048576 | tf_op jit(solution)/shard_map/all_to_all | solution.py:248
  44.1 10.5 %collective-permute-start = (f32[64,256]{1,0:T(8,128)S(1)}, f32[64,256]{1,0:T(8,128)S(1)}, u32[]{:S(2)}, u32[]{:S(2)}) collective-permute-start(f32[64,256]{1,0:T(8,128)S(1)} %reduce_sum.45), channel_id=1, source_target_pairs={{0,8},{8,16},{16,24},{24,0},{32,40},{40,48},{48,56},{56,32},{64,72... | collective-permute-start | bytes 196616 | tf_op jit(solution)/shard_map/ppermute | solution.py:222
  44.8 9.9 %collective-permute-start.1 = (f32[64,256]{1,0:T(8,128)S(1)}, f32[64,256]{1,0:T(8,128)S(1)}, u32[]{:S(2)}, u32[]{:S(2)}) collective-permute-start(f32[64,256]{1,0:T(8,128)S(1)} %reduce_sum.45), channel_id=1, source_target_pairs={{0,24},{8,0},{16,8},{24,16},{32,56},{40,32},{48,40},{56,48},{64,88... | collective-permute-start | bytes 196616 | tf_op jit(solution)/shard_map/ppermute | solution.py:222
  47.4 7.6 %collective-permute-start.2 = (f32[64,256]{1,0:T(8,128)S(1)}, f32[64,256]{1,0:T(8,128)S(1)}, u32[]{:S(2)}, u32[]{:S(2)}) collective-permute-start(f32[64,256]{1,0:T(8,128)S(1)} %reduce_sum.45), channel_id=1, source_target_pairs={{0,16},{8,24},{16,0},{24,8},{32,48},{40,56},{48,32},{56,40},{64,80... | collective-permute-start | bytes 196616 | tf_op jit(solution)/shard_map/ppermute | solution.py:222
  55.0 48.4 %collective-permute-start.11 = (bf16[256,4096]{1,0:T(8,128)(2,1)}, bf16[256,4096]{1,0:T(8,128)(2,1)}, u32[]{:S(2)}, u32[]{:S(2)}) collective-permute-start(bf16[256,4096]{1,0:T(8,128)(2,1)} %get-tuple-element.49), channel_id=1, source_target_pairs={{0,8},{8,16},{16,24},{24,0},{32,40},{40,48},{48,56},{56,32},{64,72... | collective-permute-start | bytes 6291464 | tf_op jit(solution)/shard_map/ppermute | solution.py:222
  56.7 46.8 %collective-permute-start.12 = (bf16[256,4096]{1,0:T(8,128)(2,1)}, bf16[256,4096]{1,0:T(8,128)(2,1)}, u32[]{:S(2)}, u32[]{:S(2)}) collective-permute-start(bf16[256,4096]{1,0:T(8,128)(2,1)} %get-tuple-element.50), channel_id=1, source_target_pairs={{0,24},{8,0},{16,8},{24,16},{32,56},{40,32},{48,40},{56,48},{64,88... | collective-permute-start | bytes 6291464 | tf_op jit(solution)/shard_map/ppermute | solution.py:222
  68.1 50.7 %collective-permute-start.14 = (bf16[256,4096]{1,0:T(8,128)(2,1)}, bf16[256,4096]{1,0:T(8,128)(2,1)}, u32[]{:S(2)}, u32[]{:S(2)}) collective-permute-start(bf16[256,4096]{1,0:T(8,128)(2,1)} %get-tuple-element.54), channel_id=1, source_target_pairs={{0,32},{8,40},{16,48},{24,56},{32,64},{40,72},{48,80},{56,88},{64,... | collective-permute-start | bytes 6291464 | tf_op jit(solution)/shard_map/ppermute | solution.py:222
  68.6 50.2 %collective-permute-start.15 = (bf16[256,4096]{1,0:T(8,128)(2,1)}, bf16[256,4096]{1,0:T(8,128)(2,1)}, u32[]{:S(2)}, u32[]{:S(2)}) collective-permute-start(bf16[256,4096]{1,0:T(8,128)(2,1)} %get-tuple-element.55), channel_id=1, source_target_pairs={{0,96},{8,104},{16,112},{24,120},{32,0},{40,8},{48,16},{56,24},{64... | collective-permute-start | bytes 6291464 | tf_op jit(solution)/shard_map/ppermute | solution.py:222
  72.7 25.2 %all-to-all-start.1 = ((bf16[8,64,1024]{2,1,0:T(8,128)(2,1)}), bf16[8,64,1024]{2,1,0:T(8,128)(2,1)S(1)}, u32[]{:S(2)}, u32[]{:S(2)}) async-start(bf16[8,64,1024]{2,1,0:T(8,128)(2,1)} %tile.2), calls=%async_computation.1 | async-start | bytes 2097152 | tf_op jit(solution)/shard_map/all_to_all | solution.py:272
  78.2 17.3 %collective-permute-start.8 = (bf16[64,1024]{1,0:T(8,128)(2,1)S(1)}, bf16[64,1024]{1,0:T(8,128)(2,1)S(1)}, u32[]{:S(2)}, u32[]{:S(2)}) collective-permute-start(bf16[64,1024]{1,0:T(8,128)(2,1)S(1)} %pad_maximum_fusion.3), channel_id=1, source_target_pairs={{0,2},{1,3},{2,0},{3,1},{4,6},{5,7},{6,4},{7,5},{8,10},{9,11},{10,... | collective-permute-start | bytes 393224 | tf_op jit(solution)/shard_map/ppermute | solution.py:274
  95.5 18.3 %collective-permute-start.9 = (bf16[128,1024]{1,0:T(8,128)(2,1)S(1)}, bf16[128,1024]{1,0:T(8,128)(2,1)S(1)}, u32[]{:S(2)}, u32[]{:S(2)}) collective-permute-start(bf16[128,1024]{1,0:T(8,128)(2,1)S(1)} %pad_maximum_fusion.2), channel_id=1, source_target_pairs={{0,6},{1,7},{2,4},{3,5},{4,2},{5,3},{6,0},{7,1},{8,14},{9,15},{10,... | collective-permute-start | bytes 786440 | tf_op jit(solution)/shard_map/ppermute | solution.py:274
  112.1 27.6 %collective-permute-start.13 = (bf16[128,4096]{1,0:T(8,128)(2,1)S(1)}, bf16[128,4096]{1,0:T(8,128)(2,1)S(1)}, u32[]{:S(2)}, u32[]{:S(2)}) collective-permute-start(bf16[128,4096]{1,0:T(8,128)(2,1)S(1)} %get-tuple-element.52), channel_id=1, source_target_pairs={{0,32},{8,40},{16,48},{24,56},{32,64},{40,72},{48,80},{56,88},{64,... | collective-permute-start | bytes 3145736 | tf_op jit(solution)/shard_map/ppermute | solution.py:222
  113.9 33.7 %collective-permute-start.22 = (bf16[128,4096]{1,0:T(8,128)(2,1)}, bf16[128,4096]{1,0:T(8,128)(2,1)S(1)}, u32[]{:S(2)}, u32[]{:S(2)}) collective-permute-start(bf16[128,4096]{1,0:T(8,128)(2,1)} %get-tuple-element.65), channel_id=1, source_target_pairs={{0,96},{8,104},{16,112},{24,120},{32,0},{40,8},{48,16},{56,24},{64... | collective-permute-start | bytes 3145736 | tf_op jit(solution)/shard_map/ppermute | solution.py:222
  115.8 44.8 %collective-permute-start.23 = (bf16[128,4096]{1,0:T(8,128)(2,1)S(1)}, bf16[128,4096]{1,0:T(8,128)(2,1)S(1)}, u32[]{:S(2)}, u32[]{:S(2)}) collective-permute-start(bf16[128,4096]{1,0:T(8,128)(2,1)S(1)} %get-tuple-element.66), channel_id=1, source_target_pairs={{0,64},{8,72},{16,80},{24,88},{32,96},{40,104},{48,112},{56,120},{... | collective-permute-start | bytes 3145736 | tf_op jit(solution)/shard_map/ppermute | solution.py:222
  125.9 39.3 %collective-permute-start.16 = (bf16[128,4096]{1,0:T(8,128)(2,1)}, bf16[128,4096]{1,0:T(8,128)(2,1)S(1)}, u32[]{:S(2)}, u32[]{:S(2)}) collective-permute-start(bf16[128,4096]{1,0:T(8,128)(2,1)} %get-tuple-element.58), channel_id=1, source_target_pairs={{0,8},{8,16},{16,24},{24,0},{32,40},{40,48},{48,56},{56,32},{64,72... | collective-permute-start | bytes 3145736 | tf_op jit(solution)/shard_map/ppermute | solution.py:222
  127.4 51.1 %collective-permute-start.17 = (bf16[128,4096]{1,0:T(8,128)(2,1)}, bf16[128,4096]{1,0:T(8,128)(2,1)S(1)}, u32[]{:S(2)}, u32[]{:S(2)}) collective-permute-start(bf16[128,4096]{1,0:T(8,128)(2,1)} %get-tuple-element.59), channel_id=1, source_target_pairs={{0,24},{8,0},{16,8},{24,16},{32,56},{40,32},{48,40},{56,48},{64,88... | collective-permute-start | bytes 3145736 | tf_op jit(solution)/shard_map/ppermute | solution.py:222
  145.9 32.6 %collective-permute-start.18 = (bf16[128,4096]{1,0:T(8,128)(2,1)S(1)}, bf16[128,4096]{1,0:T(8,128)(2,1)S(1)}, u32[]{:S(2)}, u32[]{:S(2)}) collective-permute-start(bf16[128,4096]{1,0:T(8,128)(2,1)S(1)} %get-tuple-element.60), channel_id=1, source_target_pairs={{0,16},{8,24},{16,0},{24,8},{32,48},{40,56},{48,32},{56,40},{64,80... | collective-permute-start | bytes 3145736 | tf_op jit(solution)/shard_map/ppermute | solution.py:222
  161.0 24.1 %collective-permute-start.26 = (bf16[32,4096]{1,0:T(8,128)(2,1)S(1)}, bf16[32,4096]{1,0:T(8,128)(2,1)S(1)}, u32[]{:S(2)}, u32[]{:S(2)}) collective-permute-start(bf16[32,4096]{1,0:T(8,128)(2,1)S(1)} %collect.7), channel_id=1, source_target_pairs={{0,16},{8,24},{16,0},{24,8},{32,48},{40,56},{48,32},{56,40},{64,80... | collective-permute-start | bytes 786440 | tf_op jit(solution)/shard_map/ppermute | solution.py:222
  163.9 24.4 %collective-permute-start.24 = (bf16[32,4096]{1,0:T(8,128)(2,1)S(1)}, bf16[32,4096]{1,0:T(8,128)(2,1)S(1)}, u32[]{:S(2)}, u32[]{:S(2)}) collective-permute-start(bf16[32,4096]{1,0:T(8,128)(2,1)S(1)} %get-tuple-element.67), channel_id=1, source_target_pairs={{0,8},{8,16},{16,24},{24,0},{32,40},{40,48},{48,56},{56,32},{64,72... | collective-permute-start | bytes 786440 | tf_op jit(solution)/shard_map/ppermute | solution.py:222
  165.2 23.1 %collective-permute-start.25 = (bf16[32,4096]{1,0:T(8,128)(2,1)S(1)}, bf16[32,4096]{1,0:T(8,128)(2,1)S(1)}, u32[]{:S(2)}, u32[]{:S(2)}) collective-permute-start(bf16[32,4096]{1,0:T(8,128)(2,1)S(1)} %get-tuple-element.68), channel_id=1, source_target_pairs={{0,24},{8,0},{16,8},{24,16},{32,56},{40,32},{48,40},{56,48},{64,88... | collective-permute-start | bytes 786440 | tf_op jit(solution)/shard_map/ppermute | solution.py:222
  178.9 11.6 %collective-permute-start.21 = (bf16[32,4096]{1,0:T(8,128)(2,1)S(1)}, bf16[32,4096]{1,0:T(8,128)(2,1)S(1)}, u32[]{:S(2)}, u32[]{:S(2)}) collective-permute-start(bf16[32,4096]{1,0:T(8,128)(2,1)S(1)} %collect.5), channel_id=1, source_target_pairs={{0,64},{8,72},{16,80},{24,88},{32,96},{40,104},{48,112},{56,120},{... | collective-permute-start | bytes 786440 | tf_op jit(solution)/shard_map/ppermute | solution.py:222
  185.0 7.7 %collective-permute-start.19 = (bf16[32,4096]{1,0:T(8,128)(2,1)S(1)}, bf16[32,4096]{1,0:T(8,128)(2,1)S(1)}, u32[]{:S(2)}, u32[]{:S(2)}) collective-permute-start(bf16[32,4096]{1,0:T(8,128)(2,1)S(1)} %get-tuple-element.61), channel_id=1, source_target_pairs={{0,32},{8,40},{16,48},{24,56},{32,64},{40,72},{48,80},{56,88},{64,... | collective-permute-start | bytes 786440 | tf_op jit(solution)/shard_map/ppermute | solution.py:222
  (9 other events, 83.8 us)
